TPU v7x, 256 devices: a whole 4x4x8 slice. The times are simulated.
256 devices in a mesh: seq: 16 (over z, y_hi), res: 16 (over y_lo, x, core).
Axes of the slice: x: 4, y: 4 (y_hi: 2, y_lo: 2; y = y_hi * 2 + y_lo), z: 8, core: 2. Of those that a mesh axis runs over, the one named last changes fastest.
Arguments:
- homolog_profile: bfloat16 [128, 2048, 256], P('seq', 'res'), may hold values from -6 to 6
- couplings_tensor: bfloat16 [2048, 2048, 128], P('res', 'seq'), may hold values from -6 to 6
- present_entries: int32 [128, 2048], P('seq', 'res'), may hold values 0 or 1
- resolved_positions: int32 [2048], P('res'), may hold values 0 or 1
- coupling_logit_matrix: bfloat16 [128, 8], replicated
- horizontal_asking_matrix: bfloat16 [256, 256], replicated
- horizontal_lookup_matrix: bfloat16 [256, 256], replicated, may hold values from -0.375 to 0.375
- horizontal_content_matrix: bfloat16 [256, 256], replicated, may hold values from -0.375 to 0.375
- horizontal_sigmoid_matrix: bfloat16 [256, 256], replicated, may hold values from -0.375 to 0.375
- horizontal_final_matrix: bfloat16 [256, 256], replicated, may hold values from -0.375 to 0.375
- vertical_asking_matrix: bfloat16 [256, 256], replicated
- vertical_lookup_matrix: bfloat16 [256, 256], replicated, may hold values from -0.375 to 0.375
- vertical_content_matrix: bfloat16 [256, 256], replicated, may hold values from -0.375 to 0.375
- vertical_sigmoid_matrix: bfloat16 [256, 256], replicated, may hold values from -0.375 to 0.375
- vertical_final_matrix: bfloat16 [256, 256], replicated, may hold values from -0.375 to 0.375
- widening_matrix: bfloat16 [256, 1024], replicated, may hold values from -0.375 to 0.375
- narrowing_matrix: bfloat16 [1024, 256], replicated, may hold values from -0.1875 to 0.1875
Outputs:
- msa_next: bfloat16 [128, 2048, 256], P('seq', 'res')
All inputs are finite; a program needn't handle non-finite values. No bound on the sum of `present_entries` or of `resolved_positions` on one device may be relied on, other than what follows from the above.
Results may differ from a plain program's by a relative error of at most 0.014.
The roundings to bfloat16 on the way count: a program that leaves them out, or rounds other values in their place, can miss the bound.
Values may be sent and summed in bfloat16 or wider, within the bound.
No kernel may reach another device: no remote copies, remote signals or barrier semaphores. Data moves between devices by JAX's collectives and lax.ppermute only.
A program may use at most 128 MiB of HBM per device.

v0:
```python
import math

import jax
import jax.numpy as jnp
from jax import lax
from jax.sharding import PartitionSpec as P

HEADS = 8
HEAD_DIM = 32


EPS = 1e-05
MASK_SCALE = 1000000000.0


def standardize_features_fn(values):
    values = values.astype(jnp.float32)
    center = values - jnp.mean(values, -1, keepdims=True)
    spread = jnp.mean(center * center, -1, keepdims=True)
    return center * lax.rsqrt(spread + EPS)


def on_device(
    homolog_profile,
    couplings_tensor,
    present_entries,
    resolved_positions,
    coupling_logit_matrix,
    horizontal_asking_matrix,
    horizontal_lookup_matrix,
    horizontal_content_matrix,
    horizontal_sigmoid_matrix,
    horizontal_final_matrix,
    vertical_asking_matrix,
    vertical_lookup_matrix,
    vertical_content_matrix,
    vertical_sigmoid_matrix,
    vertical_final_matrix,
    widening_matrix,
    narrowing_matrix,
):
    number_entries, homolog_groups, embedding_depth = homolog_profile.shape
    head_dim = embedding_depth // HEADS
    scale = HEAD_DIM ** (-0.5)
    bias = jnp.einsum(
        "ijc,ch->hij",
        standardize_features_fn(couplings_tensor),
        coupling_logit_matrix.astype(jnp.float32),
        precision=lax.Precision.HIGHEST,
    ).astype(jnp.bfloat16)
    bias_all = lax.all_gather(bias, "seq", axis=2, tiled=True)
    lone_source_tensor = standardize_features_fn(homolog_profile).astype(jnp.bfloat16)
    query = (
        jnp.dot(lone_source_tensor, horizontal_asking_matrix, preferred_element_type=jnp.float32)
        * scale
    ).astype(jnp.bfloat16)
    query = query.reshape(number_entries, homolog_groups, HEADS, head_dim)
    gate = jax.nn.sigmoid(
        jnp.dot(lone_source_tensor, horizontal_sigmoid_matrix, preferred_element_type=jnp.float32)
    )
    key_valid = (present_entries * resolved_positions[None, :]).astype(jnp.bfloat16)
    start_state = (
        jnp.full((number_entries, HEADS, homolog_groups), -1e30, jnp.float32),
        jnp.zeros((number_entries, HEADS, homolog_groups), jnp.float32),
        jnp.zeros((number_entries, HEADS, homolog_groups, head_dim), jnp.float32),
    )
    keys = jnp.dot(
        lone_source_tensor, horizontal_lookup_matrix, preferred_element_type=jnp.float32
    ).astype(jnp.bfloat16)
    values = jnp.dot(
        lone_source_tensor, horizontal_content_matrix, preferred_element_type=jnp.float32
    ).astype(jnp.bfloat16)
    pieces = (
        lax.all_gather(keys, "res", axis=1, tiled=True),
        lax.all_gather(values, "res", axis=1, tiled=True),
        lax.all_gather(key_valid, "res", axis=1, tiled=True),
    )
    keys = pieces[0]
    values = pieces[1]
    okay = pieces[2]
    stretch_extent = keys.shape[1]
    block = math.gcd(stretch_extent, 512)

    def update(index, state):
        top, total, accum = state
        first = index * block
        kk = lax.dynamic_slice_in_dim(keys, first, block, 1).reshape(
            number_entries, block, HEADS, head_dim
        )
        vv = lax.dynamic_slice_in_dim(values, first, block, 1).reshape(
            number_entries, block, HEADS, head_dim
        )
        ok = lax.dynamic_slice_in_dim(okay, first, block, 1)
        bb = lax.dynamic_slice_in_dim(bias_all, first, block, 2)
        score = jnp.einsum("sihd,sjhd->shij", query, kk, preferred_element_type=jnp.float32)
        score = (
            score
            + bb.astype(jnp.float32)[None]
            + ((ok.astype(jnp.float32) - 1.0) * MASK_SCALE)[:, None, None, :]
        )
        newtop = jnp.maximum(top, jnp.max(score, -1))
        probs = jnp.exp(score - newtop[..., None])
        factor = jnp.exp(top - newtop)
        total = total * factor + jnp.sum(probs, -1)
        accum = accum * factor[..., None] + jnp.einsum(
            "shij,sjhd->shid", probs.astype(jnp.bfloat16), vv, preferred_element_type=jnp.float32
        )
        return (newtop, total, accum)

    top, total, accum = lax.fori_loop(0, stretch_extent // block, update, start_state)
    row_mixed = jnp.transpose(accum / total[..., None], (0, 2, 1, 3)).reshape(
        number_entries, homolog_groups, embedding_depth
    )
    lone_head_mixing = (row_mixed * gate).astype(jnp.bfloat16)
    lone_homolog_group = homolog_profile.astype(jnp.float32) + jnp.dot(
        lone_head_mixing, horizontal_final_matrix, preferred_element_type=jnp.float32
    )
    second_activations = standardize_features_fn(lone_homolog_group).astype(jnp.bfloat16)
    column_valid = present_entries.astype(jnp.bfloat16)
    c_query = (
        jnp.dot(second_activations, vertical_asking_matrix, preferred_element_type=jnp.float32)
        * scale
    ).astype(jnp.bfloat16)
    c_query = c_query.reshape(number_entries, homolog_groups, HEADS, head_dim)
    c_keys = jnp.dot(
        second_activations, vertical_lookup_matrix, preferred_element_type=jnp.float32
    ).astype(jnp.bfloat16)
    c_values = jnp.dot(
        second_activations, vertical_content_matrix, preferred_element_type=jnp.float32
    ).astype(jnp.bfloat16)
    c_gate = jax.nn.sigmoid(
        jnp.dot(second_activations, vertical_sigmoid_matrix, preferred_element_type=jnp.float32)
    )
    pieces = (
        lax.all_gather(c_keys, "seq", axis=0, tiled=True),
        lax.all_gather(c_values, "seq", axis=0, tiled=True),
        lax.all_gather(column_valid, "seq", axis=0, tiled=True),
    )
    top_c = jnp.full((homolog_groups, HEADS, number_entries), -1e30, jnp.float32)
    many = pieces[0].shape[0]
    kk = pieces[0].reshape(many, homolog_groups, HEADS, head_dim)
    vv = pieces[1].reshape(many, homolog_groups, HEADS, head_dim)
    masking = ((pieces[2].astype(jnp.float32) - 1.0) * MASK_SCALE).T
    score = (
        jnp.einsum("sihd,tihd->ihst", c_query, kk, preferred_element_type=jnp.float32)
        + masking[:, None, None, :]
    )
    newtop = jnp.maximum(top_c, jnp.max(score, -1))
    probs = jnp.exp(score - newtop[..., None])
    factor = jnp.exp(top_c - newtop)
    total_c = jnp.sum(probs, -1)
    accum_c = jnp.einsum(
        "ihst,tihd->ihsd", probs.astype(jnp.bfloat16), vv, preferred_element_type=jnp.float32
    )
    top_c, total_c, accum_c = (newtop, total_c, accum_c)
    col_mixed = jnp.transpose(accum_c / total_c[..., None], (2, 0, 1, 3)).reshape(
        number_entries, homolog_groups, embedding_depth
    )
    second_mixing = (col_mixed * c_gate).astype(jnp.bfloat16)
    updated_profile = lone_homolog_group + jnp.dot(
        second_mixing, vertical_final_matrix, preferred_element_type=jnp.float32
    )
    x_three = standardize_features_fn(updated_profile).astype(jnp.bfloat16)
    hidden = jax.nn.relu(
        jnp.dot(x_three, widening_matrix, preferred_element_type=jnp.float32)
    ).astype(jnp.bfloat16)
    return (
        updated_profile + jnp.dot(hidden, narrowing_matrix, preferred_element_type=jnp.float32)
    ).astype(jnp.bfloat16)


def solution(mesh):
    placed = (
        P("seq", "res", None),
        P("res", "seq", None),
        P("seq", "res"),
        P("res"),
        P(),
        P(),
        P(),
        P(),
        P(),
        P(),
        P(),
        P(),
        P(),
        P(),
        P(),
        P(),
        P(),
    )
    return jax.shard_map(
        on_device, mesh=mesh, in_specs=placed, out_specs=P("seq", "res", None), check_vma=False
    )
```

profile of v0, /device:TPU:2, one launch (start us, length us, event | category | flops | bytes accessed | tf_op | source)
XLA Modules:
  0.0 722.0 jit_solution(4344095899514818209)
XLA Ops:
  6.5 3.5 convert_reduce_fusion
  10.1 4.8 fusion.12
  15.0 8.7 %fusion.42 = bf16[8,128,128]{2,0,1:T(8,128)(2,1)} fusion(bf16[128,128,128]{2,1,0:T(8,128)(2,1)S(1)} %copy-done.2, f32[128,128]{1,0:T(8,128)S(1)} %add_rsqrt_fusion, f32[128,128]{1,0:T(8,128)S(1)} %broadcast_multiply_fusion, bf16[128,8]{0,1:T(8,128)(2,1)S(1)} %copy-done.23), kind=kOutput, calls=%fused_computation.63 | convolution fusion | flops 207749120 | bytes 4589568 | tf_op jit(solution)/shard_map/ijc,ch->hij/dot_general | solution.py:45
  24.3 1.3 convolution_convert_fusion.2
  25.7 1.3 convolution_convert_fusion.3
  28.4 18.5 %all_gather.23 = bf16[8,2048]{1,0:T(8,128)(2,1)S(1)} all-gather(bf16[8,128]{1,0:T(8,128)(2,1)S(1)} %get-tuple-element.319), channel_id=1, replica_groups=mesh['seq'=16,'res'=16] {'res'}, dimensions={1}, use_global_device_ids=true | all-gather | bytes 34816 | tf_op jit(solution)/shard_map/all_gather | solution.py:76
  47.0 85.1 %all-gather.8.cloned.1.call-done = bf16[8,128,2048]{2,0,1:T(8,128)(2,1)} async-done(((bf16[8,128,128]{2,0,1:T(8,128)(2,1)}), bf16[8,128,2048]{2,0,1:T(8,128)(2,1)}) %all-gather.8.cloned.1.call-update) | async-done | bytes 4194320 | tf_op jit(solution)/shard_map/all_gather | solution.py:51
  132.1 52.9 %all-gather.10.cloned.1.call-done = bf16[8,2048,256]{2,1,0:T(8,128)(2,1)} async-done(((bf16[8,128,256]{2,1,0:T(8,128)(2,1)}), bf16[8,2048,256]{2,1,0:T(8,128)(2,1)}) %all-gather.10.cloned.1.call-update) | async-done | bytes 8388624 | tf_op jit(solution)/shard_map/all_gather | solution.py:75
  185.0 57.4 %all-gather.6.cloned.1.call-done = bf16[8,2048,256]{2,1,0:T(8,128)(2,1)} async-done(((bf16[8,128,256]{2,1,0:T(8,128)(2,1)}), bf16[8,2048,256]{2,1,0:T(8,128)(2,1)}) %all-gather.6.cloned.1.call-update) | async-done | bytes 8388624 | tf_op jit(solution)/shard_map/all_gather | solution.py:74
  242.4 164.2 %while.20 = (s32[]{:T(128)}, f32[8,8,128]{2,1,0:T(8,128)S(1)}, f32[8,8,128]{2,1,0:T(8,128)S(1)}, f32[8,8,128,32]{2,3,1,0:T(8,128)}, bf16[8,2048,256]{2,1,0:T(8,1...) while((s32[]{:T(128)}, f32[8,8,128]{2,1,0:T(8,128)S(1)}, ...), condition=%wide.region_7.0_spmd.clone, body=%wide.region_4.0_spmd.clone.sunk | while | flops 584372224 | bytes 96542936 | solution.py:110
  242.4 3.9 constant_dynamic-slice_fusion.6
  246.2 2.4 copy.83
  248.6 1.3 constant_dynamic-slice_fusion.5
  249.9 1.8 copy.82
  251.7 1.5 convert_element_type.211
  253.6 7.9 %fusion.104 = (f32[8,8,128]{2,1,0:T(8,128)S(1)}, f32[8,8,512,128]{3,2,1,0:T(8,128)}) fusion(f32[8,512]{1,0:T(8,128)S(1)} %add_multiply_fusion.2, f32[8,128,512]{1,2,0:T(8,128)S(1)} %convert_element_type.211, bf16[8,512,8,32]{1,3,2,0:T(8,128)(2,1)S(1)} %bitcast.104, bf16[8,128,8,32]{1,3,2,0:T(8,128)(2,1)S(1)} %get-tuple-element.424), kind=kOutput, calls=%fused_computation.5.clone.1 | convolution fusion | flops 281010176 | bytes 21544960 | tf_op jit(solution)/shard_map/while/body/eval_jaxpr/sihd,sjhd->shij/dot_general | solution.py:95
  261.5 8.1 %fusion.105 = f32[8,8,128]{2,1,0:T(8,128)S(1)} fusion(f32[8,8,512,128]{3,2,1,0:T(8,128)} %get-tuple-element.389, f32[8,8,128]{2,1,0:T(8,128)S(1)} %select_maximum_fusion.2, f32[8,512]{1,0:T(8,128)S(1)} %add_multiply_fusion.2, f32[8,128,512]{1,2,0:T(8,128)S(1)} %convert_element_type.211), kind=kLoop, calls=%fused_computation.4.clone.1 | loop fusion | flops 16769024 | bytes 18956288 | tf_op jit(solution)/shard_map/while/body/eval_jaxpr/reduce_sum | solution.py:104
  269.7 3.9 copy.84
  273.6 9.6 %fusion.107 = f32[8,8,128,32]{2,3,1,0:T(8,128)} fusion(bf16[8,512,8,32]{1,3,2,0:T(8,128)(2,1)} %bitcast.105, f32[8,8,512,128]{3,2,1,0:T(8,128)} %get-tuple-element.389, f32[8,8,128]{2,1,0:T(8,128)S(1)} %select_maximum_fusion.2, f32[8,512]{1,0:T(8,128)S(1)} %add_multiply_fusion.2, f32[8,128,512]{1,2,0:T(8,128)S(1)} %convert_element_type.211, ...), kind=kOutput, calls=%fused_computation.7.clone.1 | convolution fusion | flops 285999104 | bytes 23150592 | tf_op jit(solution)/shard_map/while/body/eval_jaxpr/shij,sjhd->shid/dot_general | solution.py:105
  283.2 3.9 constant_dynamic-slice_fusion.6
  287.1 2.4 copy.83
  289.5 1.3 constant_dynamic-slice_fusion.5
  290.8 1.8 copy.82
  292.5 1.5 convert_element_type.211
  294.4 7.9 %fusion.104 = (f32[8,8,128]{2,1,0:T(8,128)S(1)}, f32[8,8,512,128]{3,2,1,0:T(8,128)}) fusion(f32[8,512]{1,0:T(8,128)S(1)} %add_multiply_fusion.2, f32[8,128,512]{1,2,0:T(8,128)S(1)} %convert_element_type.211, bf16[8,512,8,32]{1,3,2,0:T(8,128)(2,1)S(1)} %bitcast.104, bf16[8,128,8,32]{1,3,2,0:T(8,128)(2,1)S(1)} %get-tuple-element.424), kind=kOutput, calls=%fused_computation.5.clone.1 | convolution fusion | flops 281010176 | bytes 21544960 | tf_op jit(solution)/shard_map/while/body/eval_jaxpr/sihd,sjhd->shij/dot_general | solution.py:95
  302.3 8.1 %fusion.105 = f32[8,8,128]{2,1,0:T(8,128)S(1)} fusion(f32[8,8,512,128]{3,2,1,0:T(8,128)} %get-tuple-element.389, f32[8,8,128]{2,1,0:T(8,128)S(1)} %select_maximum_fusion.2, f32[8,512]{1,0:T(8,128)S(1)} %add_multiply_fusion.2, f32[8,128,512]{1,2,0:T(8,128)S(1)} %convert_element_type.211), kind=kLoop, calls=%fused_computation.4.clone.1 | loop fusion | flops 16769024 | bytes 18956288 | tf_op jit(solution)/shard_map/while/body/eval_jaxpr/reduce_sum | solution.py:104
  310.5 3.9 copy.84
  314.5 9.9 %fusion.107 = f32[8,8,128,32]{2,3,1,0:T(8,128)} fusion(bf16[8,512,8,32]{1,3,2,0:T(8,128)(2,1)} %bitcast.105, f32[8,8,512,128]{3,2,1,0:T(8,128)} %get-tuple-element.389, f32[8,8,128]{2,1,0:T(8,128)S(1)} %select_maximum_fusion.2, f32[8,512]{1,0:T(8,128)S(1)} %add_multiply_fusion.2, f32[8,128,512]{1,2,0:T(8,128)S(1)} %convert_element_type.211, ...), kind=kOutput, calls=%fused_computation.7.clone.1 | convolution fusion | flops 285999104 | bytes 23150592 | tf_op jit(solution)/shard_map/while/body/eval_jaxpr/shij,sjhd->shid/dot_general | solution.py:105
  324.4 3.9 constant_dynamic-slice_fusion.6
  328.2 2.4 copy.83
  330.6 1.3 constant_dynamic-slice_fusion.5
  331.9 1.8 copy.82
  333.7 1.5 convert_element_type.211
  335.6 7.9 %fusion.104 = (f32[8,8,128]{2,1,0:T(8,128)S(1)}, f32[8,8,512,128]{3,2,1,0:T(8,128)}) fusion(f32[8,512]{1,0:T(8,128)S(1)} %add_multiply_fusion.2, f32[8,128,512]{1,2,0:T(8,128)S(1)} %convert_element_type.211, bf16[8,512,8,32]{1,3,2,0:T(8,128)(2,1)S(1)} %bitcast.104, bf16[8,128,8,32]{1,3,2,0:T(8,128)(2,1)S(1)} %get-tuple-element.424), kind=kOutput, calls=%fused_computation.5.clone.1 | convolution fusion | flops 281010176 | bytes 21544960 | tf_op jit(solution)/shard_map/while/body/eval_jaxpr/sihd,sjhd->shij/dot_general | solution.py:95
  343.5 8.1 %fusion.105 = f32[8,8,128]{2,1,0:T(8,128)S(1)} fusion(f32[8,8,512,128]{3,2,1,0:T(8,128)} %get-tuple-element.389, f32[8,8,128]{2,1,0:T(8,128)S(1)} %select_maximum_fusion.2, f32[8,512]{1,0:T(8,128)S(1)} %add_multiply_fusion.2, f32[8,128,512]{1,2,0:T(8,128)S(1)} %convert_element_type.211), kind=kLoop, calls=%fused_computation.4.clone.1 | loop fusion | flops 16769024 | bytes 18956288 | tf_op jit(solution)/shard_map/while/body/eval_jaxpr/reduce_sum | solution.py:104
  351.6 3.9 copy.84
  355.6 9.9 %fusion.107 = f32[8,8,128,32]{2,3,1,0:T(8,128)} fusion(bf16[8,512,8,32]{1,3,2,0:T(8,128)(2,1)} %bitcast.105, f32[8,8,512,128]{3,2,1,0:T(8,128)} %get-tuple-element.389, f32[8,8,128]{2,1,0:T(8,128)S(1)} %select_maximum_fusion.2, f32[8,512]{1,0:T(8,128)S(1)} %add_multiply_fusion.2, f32[8,128,512]{1,2,0:T(8,128)S(1)} %convert_element_type.211, ...), kind=kOutput, calls=%fused_computation.7.clone.1 | convolution fusion | flops 285999104 | bytes 23150592 | tf_op jit(solution)/shard_map/while/body/eval_jaxpr/shij,sjhd->shid/dot_general | solution.py:105
  365.5 3.9 constant_dynamic-slice_fusion.6
  369.4 2.4 copy.83
  371.7 1.3 constant_dynamic-slice_fusion.5
  373.0 1.8 copy.82
  374.8 1.5 convert_element_type.211
  376.7 7.9 %fusion.104 = (f32[8,8,128]{2,1,0:T(8,128)S(1)}, f32[8,8,512,128]{3,2,1,0:T(8,128)}) fusion(f32[8,512]{1,0:T(8,128)S(1)} %add_multiply_fusion.2, f32[8,128,512]{1,2,0:T(8,128)S(1)} %convert_element_type.211, bf16[8,512,8,32]{1,3,2,0:T(8,128)(2,1)S(1)} %bitcast.104, bf16[8,128,8,32]{1,3,2,0:T(8,128)(2,1)S(1)} %get-tuple-element.424), kind=kOutput, calls=%fused_computation.5.clone.1 | convolution fusion | flops 281010176 | bytes 21544960 | tf_op jit(solution)/shard_map/while/body/eval_jaxpr/sihd,sjhd->shij/dot_general | solution.py:95
  384.6 8.1 %fusion.105 = f32[8,8,128]{2,1,0:T(8,128)S(1)} fusion(f32[8,8,512,128]{3,2,1,0:T(8,128)} %get-tuple-element.389, f32[8,8,128]{2,1,0:T(8,128)S(1)} %select_maximum_fusion.2, f32[8,512]{1,0:T(8,128)S(1)} %add_multiply_fusion.2, f32[8,128,512]{1,2,0:T(8,128)S(1)} %convert_element_type.211), kind=kLoop, calls=%fused_computation.4.clone.1 | loop fusion | flops 16769024 | bytes 18956288 | tf_op jit(solution)/shard_map/while/body/eval_jaxpr/reduce_sum | solution.py:104
  392.8 3.9 copy.84
  396.7 9.9 %fusion.107 = f32[8,8,128,32]{2,3,1,0:T(8,128)} fusion(bf16[8,512,8,32]{1,3,2,0:T(8,128)(2,1)} %bitcast.105, f32[8,8,512,128]{3,2,1,0:T(8,128)} %get-tuple-element.389, f32[8,8,128]{2,1,0:T(8,128)S(1)} %select_maximum_fusion.2, f32[8,512]{1,0:T(8,128)S(1)} %add_multiply_fusion.2, f32[8,128,512]{1,2,0:T(8,128)S(1)} %convert_element_type.211, ...), kind=kOutput, calls=%fused_computation.7.clone.1 | convolution fusion | flops 285999104 | bytes 23150592 | tf_op jit(solution)/shard_map/while/body/eval_jaxpr/shij,sjhd->shid/dot_general | solution.py:105
  406.7 1.4 broadcast_divide_fusion
  408.5 1.6 fusion.78
  410.6 1.3 convolution_convert_fusion.1
  411.9 1.3 convolution_convert_fusion
  413.2 41.6 %all_gather.26 = bf16[128,128]{1,0:T(8,128)(2,1)S(1)} all-gather(bf16[8,128]{1,0:T(8,128)(2,1)S(1)} %copy-done.11), channel_id=1, replica_groups=mesh['seq'=16,'res'=16] {'seq'}, dimensions={0}, use_global_device_ids=true | all-gather | bytes 34816 | tf_op jit(solution)/shard_map/all_gather | solution.py:137
  455.7 3.9 copy.66
  459.6 89.2 %all-gather.12.cloned.1.call-done = bf16[128,128,256]{2,1,0:T(8,128)(2,1)} async-done(((bf16[8,128,256]{2,1,0:T(8,128)(2,1)}), bf16[128,128,256]{2,1,0:T(8,128)(2,1)}) %all-gather.12.cloned.1.call-update) | async-done | bytes 8388624 | tf_op jit(solution)/shard_map/all_gather | solution.py:135
  548.8 13.1 %copy.74 = bf16[128,128,256]{0,2,1:T(8,128)(2,1)} copy(bf16[128,128,256]{2,1,0:T(8,128)(2,1)} %all-gather.12.cloned.1.call-done) | data formatting | bytes 16777216 | tf_op jit(solution)/shard_map/reshape | solution.py:141
  561.9 6.4 add_reduce_fusion
  568.4 1.9 copy-done.3
  570.2 2.8 fusion.17
  573.0 110.9 %all-gather.14.cloned.1.call-done = bf16[128,128,256]{2,1,0:T(8,128)(2,1)} async-done(((bf16[8,128,256]{2,1,0:T(8,128)(2,1)}), bf16[128,128,256]{2,1,0:T(8,128)(2,1)}) %all-gather.14.cloned.1.call-update) | async-done | bytes 8388624 | tf_op jit(solution)/shard_map/all_gather | solution.py:136
  683.9 13.0 %copy.75 = bf16[128,128,256]{0,2,1:T(8,128)(2,1)} copy(bf16[128,128,256]{2,1,0:T(8,128)(2,1)} %all-gather.14.cloned.1.call-done) | data formatting | bytes 16777216 | tf_op jit(solution)/shard_map/reshape | solution.py:142
  696.9 8.8 %bitcast_divide_fusion = f32[8,128,8,32]{3,0,2,1:T(8,128)} fusion(bf16[128,128,8,32]{0,3,2,1:T(8,128)(2,1)} %bitcast.108, f32[128,8,8,128]{3,2,1,0:T(8,128)} %copy-done.3, f32[8,128,8]{0,2,1:T(8,128)S(1)} %bitcast.112, f32[128,8,8]{2,1,0:T(8,128)S(1)} %broadcast_maximum_fusion, f32[128,128]{1,0:T(8,128)S(1)} %copy.68), kind=kOutput, calls=%fused_computation.23 | convolution fusion | flops 70516736 | bytes 13762560 | tf_op jit(solution)/shard_map/ihst,tihd->ihsd/dot_general | solution.py:152
  705.8 3.8 copy.71
  709.5 1.3 copy.72
  710.9 2.0 fusion.83
  713.3 2.2 fusion.34
  (103 shorter events, 5.9 us)
Async XLA Ops:
  6.5 706.7 %copy-start = (bf16[1024,256]{1,0:T(8,128)(2,1)S(1)}, bf16[1024,256]{1,0:T(8,128)(2,1)}, u32[]{:S(2)}) copy-start(bf16[1024,256]{1,0:T(8,128)(2,1)} %param.35) | copy-start | bytes 1572868
  6.5 8.4 %copy-start.23 = (bf16[128,8]{0,1:T(8,128)(2,1)S(1)}, bf16[128,8]{0,1:T(8,128)(2,1)}, u32[]{:S(2)}) copy-start(bf16[128,8]{0,1:T(8,128)(2,1)} %param.23) | copy-start | bytes 6148
  6.5 125.5 %all-gather.8.cloned.1.call-start = ((), (), s32[]{:S(2)}) async-start(), calls=%async_computation.1 | async-start | bytes 4456448 | tf_op jit(solution)/shard_map/all_gather | solution.py:51
  6.5 3.5 copy-start.2
  14.9 8.8 %copy-start.4 = (bf16[8,128,256]{2,1,0:T(8,128)(2,1)S(1)}, bf16[8,128,256]{2,1,0:T(8,128)(2,1)}, u32[]{:S(2)}) copy-start(bf16[8,128,256]{2,1,0:T(8,128)(2,1)} %param.19) | copy-start | bytes 1572868
  14.9 9.4 %copy-start.17 = (bf16[256,256]{1,0:T(8,128)(2,1)S(1)}, bf16[256,256]{1,0:T(8,128)(2,1)}, u32[]{:S(2)}) copy-start(bf16[256,256]{1,0:T(8,128)(2,1)} %param.26) | copy-start | bytes 393220
  14.9 10.8 %copy-start.18 = (bf16[256,256]{1,0:T(8,128)(2,1)S(1)}, bf16[256,256]{1,0:T(8,128)(2,1)}, u32[]{:S(2)}) copy-start(bf16[256,256]{1,0:T(8,128)(2,1)} %param.25) | copy-start | bytes 393220
  14.9 12.1 %copy-start.19 = (bf16[256,256]{1,0:T(8,128)(2,1)S(1)}, bf16[256,256]{1,0:T(8,128)(2,1)}, u32[]{:S(2)}) copy-start(bf16[256,256]{1,0:T(8,128)(2,1)} %param.24) | copy-start | bytes 393220
  23.6 4.2 copy-start.12
  23.6 4.2 copy-start.15
  23.6 161.3 %all-gather.10.cloned.1.call-start = ((), (), s32[]{:S(2)}) async-start(), calls=%async_computation.2 | async-start | bytes 8912896 | tf_op jit(solution)/shard_map/all_gather | solution.py:75
  23.9 218.5 %copy-start.9 = (f32[8,128]{1,0:T(8,128)}, f32[8,128]{1,0:T(8,128)S(1)}, u32[]{:S(2)}) copy-start(f32[8,128]{1,0:T(8,128)S(1)} %broadcast_multiply_fusion.3) | copy-start | bytes 12292
  24.3 3.5 copy-start.13
  25.6 216.7 %all-gather.6.cloned.1.call-start = ((), (), s32[]{:S(2)}) async-start(), calls=%async_computation | async-start | bytes 8912896 | tf_op jit(solution)/shard_map/all_gather | solution.py:74
  27.0 521.8 %all-gather.12.cloned.1.call-start = ((), (), s32[]{:S(2)}) async-start(), calls=%async_computation.3 | async-start | bytes 8912896 | tf_op jit(solution)/shard_map/all_gather | solution.py:135
  251.7 1.9 copy-start.1
  292.5 1.9 copy-start.1
  333.7 1.9 copy-start.1
  374.8 1.9 copy-start.1
  406.6 1.8 copy-start.5
  406.6 1.8 copy-start.10
  406.6 1.8 copy-start.14
  406.7 1.8 copy-start.20
  408.5 2.1 copy-start.6
  408.5 3.4 copy-start.7
  410.2 3.1 copy-start.11
  410.2 44.7 %copy-start.8 = (bf16[256,256]{1,0:T(8,128)(2,1)S(1)}, bf16[256,256]{1,0:T(8,128)(2,1)}, u32[]{:S(2)}) copy-start(bf16[256,256]{1,0:T(8,128)(2,1)} %param.29) | copy-start | bytes 393220
  411.9 272.0 %all-gather.14.cloned.1.call-start = ((), (), s32[]{:S(2)}) async-start(), calls=%async_computation.4 | async-start | bytes 8912896 | tf_op jit(solution)/shard_map/all_gather | solution.py:136
  568.3 2.0 copy-start.3
  705.8 5.1 copy-start.21
  705.8 5.1 copy-start.22
  710.9 2.4 copy-start.16
Sparse Core Ops, SparseCore 0:
  23.8 108.2 all-gather.7
  133.9 51.0 all-gather.9
  186.8 55.5 all-gather.5
  412.0 136.7 all-gather.11
  551.3 132.5 all-gather.13
where the time goes:
time: 724 us; the launch traced here: 722 us
  waiting for transfers between devices  396 us (55%)
  matrix products  107 us (15%)
  local copies, waits for them, and re-layouts  92.6 us (13%)
  blocking collectives  60.1 us (8%)
  other arithmetic  53.3 us (7%)
  between operations  13.6 us (2%)
    all_gather x1, waiting for transfers between devices, on_device(): lax.all_gather(c_values, 'seq', axis=0, tiled=True)  111 us
    all_gather x1, waiting for transfers between devices, on_device(): lax.all_gather(c_keys, 'seq', axis=0, tiled=True)  89.2 us
    all_gather x1, waiting for transfers between devices, on_device(): bias_all = lax.all_gather(bias, 'seq', axis=2, tiled=True)  85.1 us
    all_gather x1, waiting for transfers between devices, on_device(): lax.all_gather(keys, 'res', axis=1, tiled=True)  57.4 us
    all_gather x1, waiting for transfers between devices, on_device(): lax.all_gather(values, 'res', axis=1, tiled=True)  52.9 us
    all_gather x1, blocking collectives, on_device(): lax.all_gather(column_valid, 'seq', axis=0, tiled=True)  41.6 us
    dot_general x4, matrix products, update(): jnp.einsum('shij,sjhd->shid', probs.astype(jnp.bfloat16), vv, preferred_e...  39.3 us
    reduce_sum x4, other arithmetic, update(): total = total * factor + jnp.sum(probs, -1)  32.5 us
  transfers between devices with their start and end apart: 5, of which 5 were waited for; matrix products, arithmetic and copies ran while one was open for 5% of the time, Pallas kernels for 0%

commit v1 on v0

v1 whole, which is shorter than its diff:
```python
import functools

import jax
import jax.numpy as jnp
import numpy as np
from jax import lax
from jax.experimental import pallas as pl
from jax.experimental.pallas import tpu as pltpu
from jax.sharding import PartitionSpec as P

HEADS = 8
HEAD_DIM = 32
EPS = 1e-05
MASK_SCALE = 1000000000.0
VMEM_LIMIT = 48 * 1024 * 1024

F32 = jnp.float32
BF16 = jnp.bfloat16


def mask_parts():
    parts = []
    rest = np.float64(-MASK_SCALE)
    for _ in range(3):
        part = np.float64(np.asarray(rest, jnp.bfloat16))
        parts.append(float(part))
        rest = rest - part
    assert rest == 0.0
    return parts


def standardize(values):
    center = values - jnp.mean(values, -1, keepdims=True)
    spread = jnp.mean(center * center, -1, keepdims=True)
    return center * lax.rsqrt(spread + EPS)


def dot_tt(a, b):
    return lax.dot_general(a, b, (((0,), (1,)), ((), ())), preferred_element_type=F32)


def dot_tn(a, b):
    return lax.dot_general(a, b, (((0,), (0,)), ((), ())), preferred_element_type=F32)


def dot_nt(a, b):
    return lax.dot_general(a, b, (((1,), (1,)), ((), ())), preferred_element_type=F32)


def dot_nn(a, b):
    return lax.dot_general(a, b, (((1,), (0,)), ((), ())), preferred_element_type=F32)


def whole(*_):
    return pl.BlockSpec(memory_space=pltpu.VMEM)


def params(**kw):
    return pltpu.CompilerParams(vmem_limit_bytes=VMEM_LIMIT, **kw)


def cost(us):
    return pl.CostEstimate(flops=int(us * 1e-6 * 9e14), bytes_accessed=1024, transcendentals=0)


def tokens_kernel(hp_ref, ok_ref, wq_ref, wk_ref, wv_ref, wg_ref, send_ref, gate_ref):
    x = standardize(hp_ref[...].reshape(1024, 256).astype(F32)).astype(BF16)
    scale = HEAD_DIM ** (-0.5)
    for n, w_ref in enumerate((wq_ref, wk_ref, wv_ref)):
        t = dot_tt(w_ref[...], x)
        if n == 0:
            t = t * scale
        t = t.astype(BF16)
        for h in range(HEADS):
            for s in range(8):
                send_ref[h, n * 256 + s * 32 : n * 256 + (s + 1) * 32, :] = t[
                    h * 32 : (h + 1) * 32, s * 128 : (s + 1) * 128
                ]
    ok = jnp.concatenate([ok_ref[...], jnp.zeros((8, 128), F32)], 0).astype(BF16)
    for h in range(HEADS):
        send_ref[h, 768:784, :] = ok
    gate_ref[...] = jax.nn.sigmoid(dot_tt(wg_ref[...], x))


def tokens_call(hp, ok, wq, wk, wv, wg):
    return pl.pallas_call(
        tokens_kernel,
        out_shape=(
            jax.ShapeDtypeStruct((8, 784, 128), BF16),
            jax.ShapeDtypeStruct((256, 1024), F32),
        ),
        in_specs=[whole()] * 6,
        out_specs=(whole(), whole()),
        compiler_params=params(),
        cost_estimate=cost(5),
        name="tokens",
    )(hp, ok, wq, wk, wv, wg)


BIAS_ROWS = 16


def bias_kernel(z_ref, wt_ref, out_ref, rows):
    step = pl.program_id(0)
    wt = wt_ref[...]
    ones_row = jnp.ones((16, 128), BF16)
    wsum = jnp.sum(wt.astype(F32), -1, keepdims=True)
    for n in range(BIAS_ROWS):
        z = z_ref[n]
        zf = z.astype(F32)
        center = zf - jnp.mean(zf, -1, keepdims=True)
        square = center * center
        high = square.astype(BF16)
        low = (square - high.astype(F32)).astype(BF16)
        dots = dot_nt(wt, z)
        mean = dot_nt(ones_row, z)[0:8] * (1.0 / 128)
        spread = (dot_nt(ones_row, high) + dot_nt(ones_row, low))[0:8] * (1.0 / 128)
        res = (dots[0:8] - mean * wsum[0:8]) * lax.rsqrt(spread + EPS)
        rows[pl.ds(step * BIAS_ROWS + n, 8, stride=128), :] = res

    @pl.when(step == pl.num_programs(0) - 1)
    def _():
        for h in range(HEADS):
            out_ref[h] = rows[h * 128 : (h + 1) * 128, :].T.astype(BF16)


def bias_call(z, wt):
    return pl.pallas_call(
        bias_kernel,
        out_shape=jax.ShapeDtypeStruct((8, 128, 128), BF16),
        grid=(128 // BIAS_ROWS,),
        in_specs=[
            pl.BlockSpec((BIAS_ROWS, 128, 128), lambda n: (n, 0, 0)),
            pl.BlockSpec((16, 128), lambda n: (0, 0)),
        ],
        out_specs=pl.BlockSpec((8, 128, 128), lambda n: (0, 0, 0)),
        scratch_shapes=[pltpu.VMEM((1024, 128), F32)],
        compiler_params=params(),
        cost_estimate=cost(8),
        name="pair_bias",
    )(z, wt)


def attend_kernel(n_bias, chunks, first, last, *refs):
    place_ref, own_ref, other_ref = refs[:3]
    bias_refs = refs[3 : 3 + n_bias]
    refs = refs[3 + n_bias :]
    if not first:
        m_in, l_in, acc_in = refs[:3]
        refs = refs[3:]
    if last:
        o_ref = refs[0]
        refs = refs[1:]
    else:
        m_ref, l_ref, acc_ref = refs[:3]
        refs = refs[3:]
    keys, vals = refs
    z = place_ref[0]
    slot_own = place_ref[1]
    parts = mask_parts()
    rowid = lax.broadcasted_iota(jnp.int32, (16, 128), 0)
    coeff = jnp.where(rowid == 0, parts[0], jnp.where(rowid == 1, parts[1], jnp.where(rowid == 2, parts[2], 0.0)))
    rowid = lax.broadcasted_iota(jnp.int32, (16, 256), 0)
    ones = jnp.where(rowid < 3, 1.0, 0.0).astype(BF16)
    n_chunks = len(chunks)

    for c, (shift, _) in enumerate(chunks):
        zz = lax.rem(z + shift + 8, 8)
        for src, slot in ((own_ref, slot_own), (other_ref, 1 - slot_own)):
            okay = src[zz, 768:784, :].astype(F32)
            for s in range(8):
                mask = ((1.0 - okay[s : s + 1, :]) * coeff).astype(BF16)
                kt = jnp.concatenate([src[zz, 256 + s * 32 : 256 + (s + 1) * 32, :], mask], 0)
                keys[c, slot, s] = kt.T
                vals[c, slot, s] = src[zz, 512 + s * 32 : 512 + (s + 1) * 32, :]

    def one_sequence(s, carry):
        kx = jnp.concatenate([keys[c, t, s] for c in range(n_chunks) for t in range(2)], 0)
        vt = jnp.concatenate([vals[c, t, s] for c in range(n_chunks) for t in range(2)], 1)
        for tile in range(4):
            lanes = slice(tile * 256, (tile + 1) * 256)
            q = jnp.concatenate(
                [own_ref[tile * 2 + u, pl.ds(pl.multiple_of(s * 32, 32), 32), :] for u in range(2)], 1
            )
            qx = jnp.concatenate([q, ones], 0)
            bias = jnp.concatenate(
                [
                    jnp.concatenate([bias_refs[b][t, tile * 2 + u] for u in range(2)], 1)
                    for _, slots in chunks
                    for b, t in slots
                ],
                0,
            )
            score = dot_nn(kx, qx) + bias.astype(F32)
            top = jnp.max(score, 0, keepdims=True)
            if not first:
                before = m_in[s, :, lanes]
                top = jnp.maximum(top, before)
            probs = jnp.exp(score - top)
            total = jnp.sum(probs, 0, keepdims=True)
            accum = dot_nn(vt, probs.astype(BF16))
            if not first:
                factor = jnp.exp(before - top)
                total = total + l_in[s, :, lanes] * factor
                accum = accum + acc_in[s, :, lanes] * factor
            if last:
                out = (accum / total).astype(BF16)
                for u in range(2):
                    o_ref[tile * 2 + u, pl.ds(pl.multiple_of(s * 32, 32), 32), :] = out[:, u * 128 : (u + 1) * 128]
            else:
                m_ref[s, :, lanes] = top
                l_ref[s, :, lanes] = total
                acc_ref[s, :, lanes] = accum
        return carry

    lax.fori_loop(0, 8, one_sequence, 0)


def attend_call(place, own, other, biases, chunks, state, last, us):
    first = state is None
    if last:
        out_shape = jax.ShapeDtypeStruct((8, 256, 128), BF16)
        out_specs = whole()
    else:
        out_shape = (
            jax.ShapeDtypeStruct((8, 1, 1024), F32),
            jax.ShapeDtypeStruct((8, 1, 1024), F32),
            jax.ShapeDtypeStruct((8, 32, 1024), F32),
        )
        out_specs = (whole(),) * 3
    args = [place, own, other, *biases] + ([] if first else list(state))
    return pl.pallas_call(
        functools.partial(attend_kernel, len(biases), chunks, first, last),
        out_shape=out_shape,
        in_specs=[pl.BlockSpec(memory_space=pltpu.SMEM)] + [whole()] * (len(args) - 1),
        out_specs=out_specs,
        scratch_shapes=[
            pltpu.VMEM((len(chunks), 2, 8, 128, 48), BF16),
            pltpu.VMEM((len(chunks), 2, 8, 32, 128), BF16),
        ],
        compiler_params=params(),
        cost_estimate=cost(us),
        name="attend",
    )(*args)


def mix_kernel(o_ref, gate_ref, hp_ref, present_ref, wf_ref, m1_ref, x2_ref):
    pieces = []
    wf = wf_ref[...]
    for s in range(8):
        ot = jnp.concatenate([o_ref[h, s * 32 : (s + 1) * 32, :] for h in range(HEADS)], 0)
        at = (ot.astype(F32) * gate_ref[:, s * 128 : (s + 1) * 128]).astype(BF16)
        m1 = hp_ref[s].astype(F32) + dot_tn(at, wf)
        m1_ref[s] = m1
        pieces.append(standardize(m1).reshape(16, 8, 256))
    present = present_ref[...]
    wide = jnp.concatenate([present, jnp.zeros_like(present)], 1)
    pieces.append(jnp.stack([pltpu.roll(wide, (256 - 8 * a) % 256, 1) for a in range(16)], 0))
    x2_ref[...] = jnp.concatenate(pieces, 1).astype(BF16)


def mix_call(o, gate, hp, present, wf):
    return pl.pallas_call(
        mix_kernel,
        out_shape=(
            jax.ShapeDtypeStruct((8, 128, 256), F32),
            jax.ShapeDtypeStruct((16, 72, 256), BF16),
        ),
        in_specs=[whole()] * 5,
        out_specs=(whole(), whole()),
        compiler_params=params(),
        cost_estimate=cost(5),
        name="row_mix",
    )(o, gate, hp, present, wf)


def column_kernel(x_ref, wq_ref, wk_ref, wv_ref, wg_ref, out_ref, rows0, rows1):
    x = x_ref[...].astype(F32)
    rows = (rows0, rows1)
    xs = x[:, :64, :].reshape(1024, 256)
    rows0[...] = xs[:, :128]
    rows1[...] = xs[:, 128:]
    masks = x[:, 64:72, :128].reshape(128, 128).T
    cols = jnp.concatenate(
        [jnp.concatenate([r[pl.ds(i, 128, stride=8), :] for r in rows], 1) for i in range(8)], 0
    ).astype(BF16)
    scale = HEAD_DIM ** (-0.5)
    qt = (dot_tt(wq_ref[...], cols) * scale).astype(BF16)
    kt = dot_tt(wk_ref[...], cols).astype(BF16)
    vt = dot_tt(wv_ref[...], cols).astype(BF16)
    gt = jax.nn.sigmoid(dot_tt(wg_ref[...], cols))
    parts = mask_parts()
    rowid = lax.broadcasted_iota(jnp.int32, (16, 128), 0)
    coeff = jnp.where(rowid == 0, parts[0], jnp.where(rowid == 1, parts[1], jnp.where(rowid == 2, parts[2], 0.0)))
    ones = jnp.where(rowid < 3, 1.0, 0.0).astype(BF16)
    for i in range(8):
        lanes = slice(i * 128, (i + 1) * 128)
        mask = ((1.0 - masks[i : i + 1, :]) * coeff).astype(BF16)
        heads = []
        for h in range(HEADS):
            ch = slice(h * 32, (h + 1) * 32)
            kx = jnp.concatenate([kt[ch, lanes], mask], 0)
            qx = jnp.concatenate([qt[ch, lanes], ones], 0)
            score = dot_tn(kx, qx)
            probs = jnp.exp(score - jnp.max(score, 0, keepdims=True))
            total = jnp.sum(probs, 0, keepdims=True)
            heads.append(dot_nn(vt[ch, lanes], probs.astype(BF16)) / total)
        at = jnp.concatenate(heads, 0) * gt[:, lanes]
        an = at.T
        for k, r in enumerate(rows):
            r[pl.ds(i, 128, stride=8), :] = an[:, k * 128 : (k + 1) * 128]
    out_ref[...] = jnp.concatenate([r[...] for r in rows], 1).astype(BF16).reshape(16, 64, 256)


def column_call(x, wq, wk, wv, wg):
    return pl.pallas_call(
        column_kernel,
        out_shape=jax.ShapeDtypeStruct((16, 64, 256), BF16),
        in_specs=[whole()] * 5,
        out_specs=whole(),
        scratch_shapes=[pltpu.VMEM((1024, 128), F32)] * 2,
        compiler_params=params(),
        cost_estimate=cost(10),
        name="column",
    )(x, wq, wk, wv, wg)


def final_kernel(a_ref, m1_ref, wf_ref, ww_ref, wn_ref, out_ref):
    a = a_ref[...].astype(F32)
    wf = wf_ref[...]
    ww = ww_ref[...]
    wn = wn_ref[...]
    for s in range(8):
        a2 = a[:, s * 8 : (s + 1) * 8, :].reshape(128, 256).astype(BF16)
        m2 = m1_ref[s] + dot_nn(a2, wf)
        x3 = standardize(m2).astype(BF16)
        hid = jnp.maximum(dot_nn(x3, ww), 0.0).astype(BF16)
        out_ref[s] = (m2 + dot_nn(hid, wn)).astype(BF16)


def final_call(a, m1, wf, ww, wn):
    return pl.pallas_call(
        final_kernel,
        out_shape=jax.ShapeDtypeStruct((8, 128, 256), BF16),
        in_specs=[whole()] * 5,
        out_specs=whole(),
        compiler_params=params(),
        cost_estimate=cost(6),
        name="transition",
    )(a, m1, wf, ww, wn)


def on_device(
    homolog_profile,
    couplings_tensor,
    present_entries,
    resolved_positions,
    coupling_logit_matrix,
    horizontal_asking_matrix,
    horizontal_lookup_matrix,
    horizontal_content_matrix,
    horizontal_sigmoid_matrix,
    horizontal_final_matrix,
    vertical_asking_matrix,
    vertical_lookup_matrix,
    vertical_content_matrix,
    vertical_sigmoid_matrix,
    vertical_final_matrix,
    widening_matrix,
    narrowing_matrix,
):
    seq = lax.axis_index("seq")
    res = lax.axis_index("res")
    same_core = [[r for r in range(16) if r % 2 == c] for c in range(2)]
    to_right = [(a, (a + 2) % 16) for a in range(16)]
    to_left = [(a, (a - 2) % 16) for a in range(16)]
    swap = [(a, a ^ 1) for a in range(16)]

    def to_heads(x):
        return lax.all_to_all(x, "res", 0, 0, axis_index_groups=same_core, tiled=True)

    present = present_entries.astype(F32)
    okay = (present_entries * resolved_positions[None, :]).astype(F32)
    wt = jnp.zeros((16, 128), BF16).at[:8].set(coupling_logit_matrix.T)
    place = jnp.stack([seq // 2, jnp.where(res % 2 == seq % 2, 0, 1)]).astype(jnp.int32)

    send, gate = tokens_call(
        homolog_profile,
        okay,
        horizontal_asking_matrix,
        horizontal_lookup_matrix,
        horizontal_content_matrix,
        horizontal_sigmoid_matrix,
    )
    own = to_heads(send)
    other = lax.ppermute(own, "res", swap)

    bias = to_heads(bias_call(couplings_tensor, wt))
    pair = jnp.stack([bias, lax.ppermute(bias, "seq", swap)])

    state = attend_call(place, own, other, [pair], [(0, [(0, 0), (0, 1)])], None, False, 6)
    right, left = pair, pair
    for k in range(1, 4):
        right = lax.ppermute(right, "seq", to_right)
        left = lax.ppermute(left, "seq", to_left)
        chunks = [(-k, [(0, 0), (0, 1)]), (k, [(1, 0), (1, 1)])]
        state = attend_call(place, own, other, [right, left], chunks, state, False, 12)
    right = lax.ppermute(right[:1], "seq", to_right)
    left = lax.ppermute(left[1:], "seq", to_left)
    o = attend_call(place, own, other, [right, left], [(4, [(0, 0), (1, 0)])], state, True, 6)

    o = to_heads(o)
    m1, x2 = mix_call(o, gate, homolog_profile, present, horizontal_final_matrix)
    x2 = lax.all_to_all(x2, "seq", 0, 0, tiled=True)
    a2 = column_call(
        x2, vertical_asking_matrix, vertical_lookup_matrix, vertical_content_matrix, vertical_sigmoid_matrix
    )
    a2 = lax.all_to_all(a2, "seq", 0, 0, tiled=True)
    return final_call(a2, m1, vertical_final_matrix, widening_matrix, narrowing_matrix)


def solution(mesh):
    placed = (
        P("seq", "res", None),
        P("res", "seq", None),
        P("seq", "res"),
        P("res"),
    ) + (P(),) * 13
    return jax.shard_map(
        on_device, mesh=mesh, in_specs=placed, out_specs=P("seq", "res", None), check_vma=False
    )
```

time: 724 us -> 244 us (0.34)
  waiting for transfers between devices: 396 us -> 50.4 us
  matrix products: 107 us -> 0 us
  Pallas kernels: 0 us -> 98 us
  local copies, waits for them, and re-layouts: 92.6 us -> 5.56 us
  other arithmetic: 53.3 us -> 0.13 us
  starting transfers between devices: 0.17 us -> 30.1 us
  between operations: 13.6 us -> 0.29 us
    all_gather x5 -> x0, waiting for transfers between devices: 396 us -> none  [the longest x1 111 us: on_device(): lax.all_gather(c_values, 'seq', axis=0, tiled=True)]
    dot_general x20 -> x0, matrix products: 107 us -> none  [the longest x4 39.3 us: update(): jnp.einsum('shij,sjhd->shid', probs.astype(jnp.bfloat16), vv, preferred_e...]
    pallas_call x0 -> x10, Pallas kernels: none -> 98 us  [the longest x5 67.6 us: attend_call(): pl.pallas_call(functools.partial(attend_kernel, len(biases), chunks, firs...]
    all_gather x2 -> x0, blocking collectives: 60.1 us -> none  [the longest x1 41.6 us: on_device(): lax.all_gather(column_valid, 'seq', axis=0, tiled=True)]
    all_to_all x0 -> x3, blocking collectives: none -> 58.9 us  [the longest x1 22.6 us: on_device(): x2 = lax.all_to_all(x2, 'seq', 0, 0, tiled=True)]
    dynamic_slice x20 -> x0, local copies, waits for them, and re-layouts: 53 us -> none  [the longest x8 31.2 us: update(): lax.dynamic_slice_in_dim(values, first, block, 1)]
    reduce_sum x11 -> x0, other arithmetic: 44.9 us -> none  [the longest x4 32.5 us: update(): total = total * factor + jnp.sum(probs, -1)]
    reshape x5 -> x0, local copies, waits for them, and re-layouts: 31.7 us -> none  [the longest x1 13.1 us: on_device(): kk = pieces[0].reshape(many, homolog_groups, HEADS, head_dim)]
  transfers between devices with their start and end apart: 5 -> 12, of which waited for: 5 -> 7; matrix products, arithmetic and copies ran while one was open for 5% -> 0% of each run, Pallas kernels for 0% -> 24%
where the time goes in v1:
time: 244 us; the launch traced here: 243 us
  Pallas kernels  98 us (40%)
  blocking collectives  58.9 us (24%)
  waiting for transfers between devices  50.4 us (21%)
  starting transfers between devices  30.1 us (12%)
  local copies, waits for them, and re-layouts  5.56 us (2%)
    pallas_call x5, Pallas kernels, attend_call(): pl.pallas_call(functools.partial(attend_kernel, len(biases), chunks, firs...  67.6 us
    ppermute x3, waiting for transfers between devices, on_device(): right = lax.ppermute(right, 'seq', to_right)  25.3 us
    all_to_all x1, blocking collectives, on_device(): x2 = lax.all_to_all(x2, 'seq', 0, 0, tiled=True)  22.6 us
    all_to_all x2, waiting for transfers between devices, to_heads(): lax.all_to_all(x, 'res', 0, 0, axis_index_groups=same_core, tiled=True)  20.4 us
    all_to_all x1, blocking collectives, to_heads(): lax.all_to_all(x, 'res', 0, 0, axis_index_groups=same_core, tiled=True)  18.7 us
    all_to_all x1, blocking collectives, on_device(): a2 = lax.all_to_all(a2, 'seq', 0, 0, tiled=True)  17.5 us
    pallas_call x1, Pallas kernels, column_call(): pl.pallas_call(column_kernel, out_shape=jax.ShapeDtypeStruct((16, 64, 256...  11.9 us
    pallas_call x1, Pallas kernels, bias_call(): pl.pallas_call(bias_kernel, out_shape=jax.ShapeDtypeStruct((8, 128, 128),...  11.3 us
  transfers between devices with their start and end apart: 12, of which 7 were waited for; matrix products, arithmetic and copies ran while one was open for 0% of the time, Pallas kernels for 24%

profile of v1, /device:TPU:2, one launch (start us, length us, event | category | flops | bytes accessed | tf_op | source)
XLA Modules:
  0.0 243.3 jit_solution(10072299100034988987)
XLA Ops:
  0.0 0.7 scatter.4.wt_ref
  0.7 2.2 copy-done
  2.9 0.0 copy-start.10
  2.9 0.0 copy-start.11
  2.9 0.0 copy-start.12
  2.9 11.3 %pair_bias.1 = bf16[8,128,128]{2,1,0:T(8,128)(2,1)} custom-call(bf16[128,128,128]{2,1,0:T(8,128)(2,1)S(1)} %copy-done, bf16[16,128]{1,0:T(8,128)(2,1)S(1)} %scatter.4.wt_ref), custom_call_target="tpu_custom_call" | custom-call | flops 7200000000 | bytes 1024 | tf_op jit(solution)/shard_map/pair_bias/pallas_call | solution.py:128
  14.2 5.8 %all-to-all-start.1 = ((bf16[8,128,128]{2,1,0:T(8,128)(2,1)}), bf16[8,128,128]{2,1,0:T(8,128)(2,1)S(1)}, u32[]{:S(2)}, u32[]{:S(2)}) async-start(bf16[8,128,128]{2,1,0:T(8,128)(2,1)} %pair_bias.1), calls=%async_computation.1 | async-start | bytes 524288 | tf_op jit(solution)/shard_map/all_to_all | solution.py:380
  20.0 0.0 copy-done.21
  20.0 0.0 copy-done.22
  20.1 2.3 tokens.1
  22.4 1.0 copy-done.19
  23.3 2.8 %all-to-all-done.1 = bf16[8,128,128]{2,1,0:T(8,128)(2,1)S(1)} async-done(((bf16[8,128,128]{2,1,0:T(8,128)(2,1)}), bf16[8,128,128]{2,1,0:T(8,128)(2,1)S(1)}, u32[]{:S(2)}, u32[]{:S(2)}) %all-to-all-start.1) | async-done | bytes 262176 | tf_op jit(solution)/shard_map/all_to_all | solution.py:380
  26.1 4.7 %all-to-all-start = ((bf16[8,784,128]{2,1,0:T(8,128)(2,1)}), bf16[8,784,128]{2,1,0:T(8,128)(2,1)S(1)}, u32[]{:S(2)}, u32[]{:S(2)}) async-start(bf16[8,784,128]{2,1,0:T(8,128)(2,1)} %get-tuple-element.33), calls=%async_computation | async-start | bytes 3211264 | tf_op jit(solution)/shard_map/all_to_all | solution.py:380
  30.8 2.9 %collective-permute-start.1 = (bf16[8,128,128]{2,1,0:T(8,128)(2,1)S(1)}, bf16[8,128,128]{2,1,0:T(8,128)(2,1)S(1)}, u32[]{:S(2)}, u32[]{:S(2)}) collective-permute-start(bf16[8,128,128]{2,1,0:T(8,128)(2,1)S(1)} %all-to-all-done.1), channel_id=1, source_target_pairs={{0,16},{16,0},{32,48},{48,32},{64,80},{80,64},{96,112},{112,96},{1... | collective-permute-start | bytes 786440 | tf_op jit(solution)/shard_map/ppermute | solution.py:399
  33.7 17.6 %all-to-all-done.refs_1_ = bf16[8,784,128]{2,1,0:T(8,128)(2,1)S(1)} async-done(((bf16[8,784,128]{2,1,0:T(8,128)(2,1)}), bf16[8,784,128]{2,1,0:T(8,128)(2,1)S(1)}, u32[]{:S(2)}, u32[]{:S(2)}) %all-to-all-start) | async-done | bytes 1605664 | tf_op jit(solution)/shard_map/all_to_all | solution.py:380
  51.3 0.0 collective-permute-start
  51.3 4.6 %collective-permute-done.1 = bf16[8,128,128]{2,1,0:T(8,128)(2,1)S(1)} collective-permute-done((bf16[8,128,128]{2,1,0:T(8,128)(2,1)S(1)}, bf16[8,128,128]{2,1,0:T(8,128)(2,1)S(1)}, u32[]{:S(2)}, u32[]{:S(2)}) %collective-permute-start.1) | collective-permute-done | bytes 262176 | tf_op jit(solution)/shard_map/ppermute | solution.py:399
  55.9 0.1 pad_maximum_fusion.refs_3_
  55.9 2.0 collective-permute-start.2
  57.9 4.0 %collective-permute-start.6 = (bf16[2,8,128,128]{3,2,1,0:T(8,128)(2,1)S(1)}, bf16[2,8,128,128]{3,2,1,0:T(8,128)(2,1)S(1)}, u32[]{:S(2)}, u32[]{:S(2)}) collective-permute-start(bf16[2,8,128,128]{3,2,1,0:T(8,128)(2,1)S(1)} %pad_maximum_fusion.refs_3_), channel_id=1, source_target_pairs={{0,224},{16,240},{32,0},{48,16},{64,32},{80,48},{96,64},{112,80},{... | collective-permute-start | bytes 1572872 | tf_op jit(solution)/shard_map/ppermute | solution.py:405
  61.9 9.6 %collective-permute-done.2.refs_3_ = bf16[2,8,128,128]{3,2,1,0:T(8,128)(2,1)S(1)} collective-permute-done((bf16[2,8,128,128]{3,2,1,0:T(8,128)(2,1)S(1)}, bf16[2,8,128,128]{3,2,1,0:T(8,128)(2,1)S(1)}, u32[]{:S(2)}, u32[]{:S(2)}) %collective-permute-start.2) | collective-permute-done | bytes 524320 | tf_op jit(solution)/shard_map/ppermute | solution.py:404
  71.6 0.0 collective-permute-start.3
  71.6 0.8 copy-done.5
  72.4 0.0 collective-permute-done.6.refs_4_
  72.4 3.2 %collective-permute-start.7 = (bf16[2,8,128,128]{3,2,1,0:T(8,128)(2,1)S(1)}, bf16[2,8,128,128]{3,2,1,0:T(8,128)(2,1)}, u32[]{:S(2)}, u32[]{:S(2)}) collective-permute-start(bf16[2,8,128,128]{3,2,1,0:T(8,128)(2,1)S(1)} %collective-permute-done.6.refs_4_), channel_id=1, source_target_pairs={{0,224},{16,240},{32,0},{48,16},{64,32},{80,48},{96,64},{112,80},{... | collective-permute-start | bytes 1572872 | tf_op jit(solution)/shard_map/ppermute | solution.py:405
  75.6 0.8 copy-done.7
  76.4 7.3 %collective-permute-done.3.refs_3_ = bf16[2,8,128,128]{3,2,1,0:T(8,128)(2,1)} collective-permute-done((bf16[2,8,128,128]{3,2,1,0:T(8,128)(2,1)S(1)}, bf16[2,8,128,128]{3,2,1,0:T(8,128)(2,1)}, u32[]{:S(2)}, u32[]{:S(2)}) %collective-permute-start.3) | collective-permute-done | bytes 524320 | tf_op jit(solution)/shard_map/ppermute | solution.py:404
  83.7 0.0 collective-permute-start.4
  83.7 0.1 collective-permute-done.7.refs_4_
  83.8 3.6 %collective-permute-start.8 = (bf16[2,8,128,128]{3,2,1,0:T(8,128)(2,1)}, bf16[2,8,128,128]{3,2,1,0:T(8,128)(2,1)S(1)}, u32[]{:S(2)}, u32[]{:S(2)}) collective-permute-start(bf16[2,8,128,128]{3,2,1,0:T(8,128)(2,1)} %collective-permute-done.7.refs_4_), channel_id=1, source_target_pairs={{0,224},{16,240},{32,0},{48,16},{64,32},{80,48},{96,64},{112,80},{... | collective-permute-start | bytes 1572872 | tf_op jit(solution)/shard_map/ppermute | solution.py:405
  87.5 0.1 pad_add_fusion.refs_0_
  87.6 8.4 %collective-permute-done.4.refs_3_ = bf16[2,8,128,128]{3,2,1,0:T(8,128)(2,1)S(1)} collective-permute-done((bf16[2,8,128,128]{3,2,1,0:T(8,128)(2,1)}, bf16[2,8,128,128]{3,2,1,0:T(8,128)(2,1)S(1)}, u32[]{:S(2)}, u32[]{:S(2)}) %collective-permute-start.4) | collective-permute-done | bytes 524320 | tf_op jit(solution)/shard_map/ppermute | solution.py:404
  95.9 0.1 collective-permute-start.5
  96.0 0.0 collective-permute-done.8.refs_4_
  96.1 0.0 copy-start.6
  96.1 3.7 %collective-permute-start.9 = (bf16[1,8,128,128]{3,2,1,0:T(8,128)(2,1)S(1)}, bf16[1,8,128,128]{3,2,1,0:T(8,128)(2,1)S(1)}, u32[]{:S(2)}, u32[]{:S(2)}) collective-permute-start(bf16[1,8,128,128]{3,2,1,0:T(8,128)(2,1)S(1)} %slice.25), channel_id=1, source_target_pairs={{0,224},{16,240},{32,0},{48,16},{64,32},{80,48},{96,64},{112,80},{... | collective-permute-start | bytes 786440 | tf_op jit(solution)/shard_map/ppermute | solution.py:409
  99.8 0.0 collective-permute-done.refs_2_
  99.8 11.0 %attend.5 = (f32[8,1,1024]{2,1,0:T(1,128)S(1)}, f32[8,1,1024]{2,1,0:T(1,128)S(1)}, f32[8,32,1024]{2,1,0:T(8,128)S(1)}) custom-call(s32[2]{0:T(128)S(1)} %pad_add_fusion.refs_0_, bf16[8,784,128]{2,1,0:T(8,128)(2,1)S(1)} %all-to-all-done.refs_1_, bf16[8,784,128]{2,1,0:T(8,128)(2,1)} %collective-permute-done.refs_2_, ...), custom_call_target="tpu_custom_call" | custom-call | flops 5400000000 | bytes 1024 | tf_op jit(solution)/shard_map/attend/pallas_call | solution.py:232
  110.8 0.0 copy-done.8
  110.8 15.1 %attend.6 = (f32[8,1,1024]{2,1,0:T(1,128)S(1)}, f32[8,1,1024]{2,1,0:T(1,128)S(1)}, f32[8,32,1024]{2,1,0:T(8,128)S(1)}) custom-call(s32[2]{0:T(128)S(1)} %pad_add_fusion.refs_0_, bf16[8,784,128]{2,1,0:T(8,128)(2,1)S(1)} %all-to-all-done.refs_1_, bf16[8,784,128]{2,1,0:T(8,128)(2,1)} %collective-permute-done.refs_2_, bf16[2,8,128,128]{3,2,1,0:T(8,128)(2,1)S(1)} %copy-done.6, ...), custom_call_target="tpu_custom_call" | custom-call | flops 10800000000 | bytes 1024 | tf_op jit(solution)/shard_map/attend/pallas_call | solution.py:232
  125.9 15.3 %attend.7 = (f32[8,1,1024]{2,1,0:T(1,128)S(1)}, f32[8,1,1024]{2,1,0:T(1,128)S(1)}, f32[8,32,1024]{2,1,0:T(8,128)S(1)}) custom-call(s32[2]{0:T(128)S(1)} %pad_add_fusion.refs_0_, bf16[8,784,128]{2,1,0:T(8,128)(2,1)S(1)} %all-to-all-done.refs_1_, bf16[8,784,128]{2,1,0:T(8,128)(2,1)} %collective-permute-done.refs_2_, ...), custom_call_target="tpu_custom_call" | custom-call | flops 10800000000 | bytes 1024 | tf_op jit(solution)/shard_map/attend/pallas_call | solution.py:232
  141.2 15.0 %attend.8 = (f32[8,1,1024]{2,1,0:T(1,128)S(1)}, f32[8,1,1024]{2,1,0:T(1,128)S(1)}, f32[8,32,1024]{2,1,0:T(8,128)S(1)}) custom-call(s32[2]{0:T(128)S(1)} %pad_add_fusion.refs_0_, bf16[8,784,128]{2,1,0:T(8,128)(2,1)S(1)} %all-to-all-done.refs_1_, bf16[8,784,128]{2,1,0:T(8,128)(2,1)} %collective-permute-done.refs_2_, ...), custom_call_target="tpu_custom_call" | custom-call | flops 10800000000 | bytes 1024 | tf_op jit(solution)/shard_map/attend/pallas_call | solution.py:232
  156.3 0.0 collective-permute-done.5.refs_3_
  156.3 0.0 collective-permute-done.9.refs_4_
  156.3 0.0 copy-start.2
  156.3 0.0 copy-start.13
  156.3 11.1 %attend.9 = bf16[8,256,128]{2,1,0:T(8,128)(2,1)S(1)} custom-call(s32[2]{0:T(128)S(1)} %pad_add_fusion.refs_0_, bf16[8,784,128]{2,1,0:T(8,128)(2,1)S(1)} %all-to-all-done.refs_1_, bf16[8,784,128]{2,1,0:T(8,128)(2,1)} %collective-permute-done.refs_2_, bf16[1,8,128,128]{3,2,1,0:T(8,128)(2,1)S(1)} %collective-permute-done.5.refs_3_, ...), custom_call_target="tpu_custom_call" | custom-call | flops 5400000000 | bytes 1024 | tf_op jit(solution)/shard_map/attend/pallas_call | solution.py:232
  167.4 18.7 %all_to_all.25.o_ref = bf16[8,256,128]{2,1,0:T(8,128)(2,1)S(1)} all-to-all(bf16[8,256,128]{2,1,0:T(8,128)(2,1)S(1)} %attend.9), channel_id=1, replica_groups={{0,2,4,6,8,10,12,14},{1,3,5,7,9,11,13,15},{16,18,20,22,24,26,28,30},{17..., dimensions={0} | all-to-all | bytes 1048576 | tf_op jit(solution)/shard_map/all_to_all | solution.py:380
  186.2 0.0 copy-done.2
  186.2 0.0 copy-done.20
  186.2 0.0 copy-start.14
  186.2 0.0 copy-start.15
  186.2 0.0 copy-start.16
  186.2 0.0 copy-start.17
  186.2 1.1 row_mix.1
  187.3 22.6 %all_to_all.26.x_ref = bf16[16,72,256]{2,1,0:T(8,128)(2,1)S(1)} all-to-all(bf16[16,72,256]{2,1,0:T(8,128)(2,1)S(1)} %get-tuple-element.47), channel_id=1, replica_groups=mesh['seq'=16,'res'=16] {'seq'}, dimensions={0} | all-to-all | bytes 1179648 | tf_op jit(solution)/shard_map/all_to_all | solution.py:414
  210.0 0.0 copy-done.14
  210.0 0.0 copy-start.3
  210.0 0.0 copy-start.4
  210.0 0.0 copy-start.18
  210.0 11.9 %column.1 = bf16[16,64,256]{2,1,0:T(8,128)(2,1)S(1)} custom-call(bf16[16,72,256]{2,1,0:T(8,128)(2,1)S(1)} %all_to_all.26.x_ref, bf16[256,256]{1,0:T(8,128)(2,1)S(1)} %copy-done.14, bf16[256,256]{1,0:T(8,128)(2,1)S(1)} %copy-done.15, bf16[256,256]{1,0:T(8,128)(2,1)S(1)} %copy-done.16, bf16[256,256]{1,0:T(8,128)(2,1)S(1)} %copy-done.17), custom_call_target="tpu_custom_call" | custom-call | flops 8999999488 | bytes 1024 | tf_op jit(solution)/shard_map/column/pallas_call | solution.py:316
  221.9 17.5 %all_to_all.27.a_ref = bf16[16,64,256]{2,1,0:T(8,128)(2,1)S(1)} all-to-all(bf16[16,64,256]{2,1,0:T(8,128)(2,1)S(1)} %column.1), channel_id=1, replica_groups=mesh['seq'=16,'res'=16] {'seq'}, dimensions={0} | all-to-all | bytes 1048576 | tf_op jit(solution)/shard_map/all_to_all | solution.py:418
  239.4 0.0 copy-done.3
  239.4 3.9 %transition.1 = bf16[8,128,256]{2,1,0:T(8,128)(2,1)} custom-call(bf16[16,64,256]{2,1,0:T(8,128)(2,1)S(1)} %all_to_all.27.a_ref, f32[8,128,256]{2,1,0:T(8,128)S(1)} %get-tuple-element.48.m1_ref, bf16[256,256]{1,0:T(8,128)(2,1)S(1)} %copy-done.18, bf16[256,1024]{1,0:T(8,128)(2,1)S(1)} %copy-done.3, bf16[1024,256]{1,0:T(8,128)(2,1)S(1)} %copy-done.4), custom_call_target="tpu_custom_call" | custom-call | flops 5400000000 | bytes 1024 | tf_op jit(solution)/shard_map/transition/pallas_call | solution.py:342
  (25 shorter events, 0.1 us)
Async XLA Ops:
  0.7 2.2 copy-start
  2.9 17.2 %copy-start.21 = (s32[8,128]{1,0:T(8,128)S(1)}, s32[8,128]{1,0:T(8,128)}, u32[]{:S(2)}) copy-start(s32[8,128]{1,0:T(8,128)} %param.21) | copy-start | bytes 12292
  2.9 17.2 %copy-start.22 = (s32[128]{0:T(128)S(1)}, s32[128]{0:T(128)}, u32[]{:S(2)}) copy-start(s32[128]{0:T(128)} %param.22) | copy-start | bytes 1540
  2.9 17.2 %copy-start.1 = (bf16[8,128,256]{2,1,0:T(8,128)(2,1)S(1)}, bf16[8,128,256]{2,1,0:T(8,128)(2,1)}, u32[]{:S(2)}) copy-start(bf16[8,128,256]{2,1,0:T(8,128)(2,1)} %hp_ref.3) | copy-start | bytes 1572868
  2.9 17.2 %copy-start.9 = (bf16[256,256]{1,0:T(8,128)(2,1)S(1)}, bf16[256,256]{1,0:T(8,128)(2,1)}, u32[]{:S(2)}) copy-start(bf16[256,256]{1,0:T(8,128)(2,1)} %wq_ref.2) | copy-start | bytes 393220
  2.9 17.2 %copy-start.10 = (bf16[256,256]{1,0:T(8,128)(2,1)S(1)}, bf16[256,256]{1,0:T(8,128)(2,1)}, u32[]{:S(2)}) copy-start(bf16[256,256]{1,0:T(8,128)(2,1)} %wk_ref.2) | copy-start | bytes 393220
  2.9 17.2 %copy-start.11 = (bf16[256,256]{1,0:T(8,128)(2,1)S(1)}, bf16[256,256]{1,0:T(8,128)(2,1)}, u32[]{:S(2)}) copy-start(bf16[256,256]{1,0:T(8,128)(2,1)} %wv_ref.2) | copy-start | bytes 393220
  2.9 17.2 %copy-start.12 = (bf16[256,256]{1,0:T(8,128)(2,1)S(1)}, bf16[256,256]{1,0:T(8,128)(2,1)}, u32[]{:S(2)}) copy-start(bf16[256,256]{1,0:T(8,128)(2,1)} %wg_ref.2) | copy-start | bytes 393220
  14.2 12.0 %all-to-all-start.1 = ((bf16[8,128,128]{2,1,0:T(8,128)(2,1)}), bf16[8,128,128]{2,1,0:T(8,128)(2,1)S(1)}, u32[]{:S(2)}, u32[]{:S(2)}) async-start(bf16[8,128,128]{2,1,0:T(8,128)(2,1)} %pair_bias.1), calls=%async_computation.1 | async-start | bytes 524288 | tf_op jit(solution)/shard_map/all_to_all | solution.py:380
  22.4 1.0 copy-start.19
  26.1 25.2 %all-to-all-start = ((bf16[8,784,128]{2,1,0:T(8,128)(2,1)}), bf16[8,784,128]{2,1,0:T(8,128)(2,1)S(1)}, u32[]{:S(2)}, u32[]{:S(2)}) async-start(bf16[8,784,128]{2,1,0:T(8,128)(2,1)} %get-tuple-element.33), calls=%async_computation | async-start | bytes 3211264 | tf_op jit(solution)/shard_map/all_to_all | solution.py:380
  30.8 25.1 %collective-permute-start.1 = (bf16[8,128,128]{2,1,0:T(8,128)(2,1)S(1)}, bf16[8,128,128]{2,1,0:T(8,128)(2,1)S(1)}, u32[]{:S(2)}, u32[]{:S(2)}) collective-permute-start(bf16[8,128,128]{2,1,0:T(8,128)(2,1)S(1)} %all-to-all-done.1), channel_id=1, source_target_pairs={{0,16},{16,0},{32,48},{48,32},{64,80},{80,64},{96,112},{112,96},{1... | collective-permute-start | bytes 786440 | tf_op jit(solution)/shard_map/ppermute | solution.py:399
  51.3 48.5 %collective-permute-start = (bf16[8,784,128]{2,1,0:T(8,128)(2,1)S(1)}, bf16[8,784,128]{2,1,0:T(8,128)(2,1)}, u32[]{:S(2)}, u32[]{:S(2)}) collective-permute-start(bf16[8,784,128]{2,1,0:T(8,128)(2,1)S(1)} %all-to-all-done.refs_1_), channel_id=1, source_target_pairs={{0,1},{1,0},{2,3},{3,2},{4,5},{5,4},{6,7},{7,6},{8,9},{9,8},{10,11... | collective-permute-start | bytes 4816904 | tf_op jit(solution)/shard_map/ppermute | solution.py:396
  55.9 15.7 %collective-permute-start.2 = (bf16[2,8,128,128]{3,2,1,0:T(8,128)(2,1)S(1)}, bf16[2,8,128,128]{3,2,1,0:T(8,128)(2,1)S(1)}, u32[]{:S(2)}, u32[]{:S(2)}) collective-permute-start(bf16[2,8,128,128]{3,2,1,0:T(8,128)(2,1)S(1)} %pad_maximum_fusion.refs_3_), channel_id=1, source_target_pairs={{0,32},{16,48},{32,64},{48,80},{64,96},{80,112},{96,128},{112,144}... | collective-permute-start | bytes 1572872 | tf_op jit(solution)/shard_map/ppermute | solution.py:404
  57.9 14.5 %collective-permute-start.6 = (bf16[2,8,128,128]{3,2,1,0:T(8,128)(2,1)S(1)}, bf16[2,8,128,128]{3,2,1,0:T(8,128)(2,1)S(1)}, u32[]{:S(2)}, u32[]{:S(2)}) collective-permute-start(bf16[2,8,128,128]{3,2,1,0:T(8,128)(2,1)S(1)} %pad_maximum_fusion.refs_3_), channel_id=1, source_target_pairs={{0,224},{16,240},{32,0},{48,16},{64,32},{80,48},{96,64},{112,80},{... | collective-permute-start | bytes 1572872 | tf_op jit(solution)/shard_map/ppermute | solution.py:405
  71.6 12.1 %collective-permute-start.3 = (bf16[2,8,128,128]{3,2,1,0:T(8,128)(2,1)S(1)}, bf16[2,8,128,128]{3,2,1,0:T(8,128)(2,1)}, u32[]{:S(2)}, u32[]{:S(2)}) collective-permute-start(bf16[2,8,128,128]{3,2,1,0:T(8,128)(2,1)S(1)} %collective-permute-done.2.refs_3_), channel_id=1, source_target_pairs={{0,32},{16,48},{32,64},{48,80},{64,96},{80,112},{96,128},{112,144}... | collective-permute-start | bytes 1572872 | tf_op jit(solution)/shard_map/ppermute | solution.py:404
  71.6 0.8 copy-start.5
  72.4 11.5 %collective-permute-start.7 = (bf16[2,8,128,128]{3,2,1,0:T(8,128)(2,1)S(1)}, bf16[2,8,128,128]{3,2,1,0:T(8,128)(2,1)}, u32[]{:S(2)}, u32[]{:S(2)}) collective-permute-start(bf16[2,8,128,128]{3,2,1,0:T(8,128)(2,1)S(1)} %collective-permute-done.6.refs_4_), channel_id=1, source_target_pairs={{0,224},{16,240},{32,0},{48,16},{64,32},{80,48},{96,64},{112,80},{... | collective-permute-start | bytes 1572872 | tf_op jit(solution)/shard_map/ppermute | solution.py:405
  75.6 0.8 copy-start.7
  83.7 12.2 %collective-permute-start.4 = (bf16[2,8,128,128]{3,2,1,0:T(8,128)(2,1)}, bf16[2,8,128,128]{3,2,1,0:T(8,128)(2,1)S(1)}, u32[]{:S(2)}, u32[]{:S(2)}) collective-permute-start(bf16[2,8,128,128]{3,2,1,0:T(8,128)(2,1)} %collective-permute-done.3.refs_3_), channel_id=1, source_target_pairs={{0,32},{16,48},{32,64},{48,80},{64,96},{80,112},{96,128},{112,144}... | collective-permute-start | bytes 1572872 | tf_op jit(solution)/shard_map/ppermute | solution.py:404
  83.8 12.2 %collective-permute-start.8 = (bf16[2,8,128,128]{3,2,1,0:T(8,128)(2,1)}, bf16[2,8,128,128]{3,2,1,0:T(8,128)(2,1)S(1)}, u32[]{:S(2)}, u32[]{:S(2)}) collective-permute-start(bf16[2,8,128,128]{3,2,1,0:T(8,128)(2,1)} %collective-permute-done.7.refs_4_), channel_id=1, source_target_pairs={{0,224},{16,240},{32,0},{48,16},{64,32},{80,48},{96,64},{112,80},{... | collective-permute-start | bytes 1572872 | tf_op jit(solution)/shard_map/ppermute | solution.py:405
  95.9 60.3 %collective-permute-start.5 = (bf16[1,8,128,128]{3,2,1,0:T(8,128)(2,1)S(1)}, bf16[1,8,128,128]{3,2,1,0:T(8,128)(2,1)S(1)}, u32[]{:S(2)}, u32[]{:S(2)}) collective-permute-start(bf16[1,8,128,128]{3,2,1,0:T(8,128)(2,1)S(1)} %slice.24), channel_id=1, source_target_pairs={{0,32},{16,48},{32,64},{48,80},{64,96},{80,112},{96,128},{112,144}... | collective-permute-start | bytes 786440 | tf_op jit(solution)/shard_map/ppermute | solution.py:408
  96.1 14.7 %copy-start.6 = (bf16[2,8,128,128]{3,2,1,0:T(8,128)(2,1)S(1)}, bf16[2,8,128,128]{3,2,1,0:T(8,128)(2,1)}, u32[]{:S(2)}) copy-start(bf16[2,8,128,128]{3,2,1,0:T(8,128)(2,1)} %copy-done.5) | copy-start | bytes 1572868
  96.1 14.7 %copy-start.8 = (bf16[2,8,128,128]{3,2,1,0:T(8,128)(2,1)S(1)}, bf16[2,8,128,128]{3,2,1,0:T(8,128)(2,1)}, u32[]{:S(2)}) copy-start(bf16[2,8,128,128]{3,2,1,0:T(8,128)(2,1)} %copy-done.7) | copy-start | bytes 1572868
  96.1 60.2 %collective-permute-start.9 = (bf16[1,8,128,128]{3,2,1,0:T(8,128)(2,1)S(1)}, bf16[1,8,128,128]{3,2,1,0:T(8,128)(2,1)S(1)}, u32[]{:S(2)}, u32[]{:S(2)}) collective-permute-start(bf16[1,8,128,128]{3,2,1,0:T(8,128)(2,1)S(1)} %slice.25), channel_id=1, source_target_pairs={{0,224},{16,240},{32,0},{48,16},{64,32},{80,48},{96,64},{112,80},{... | collective-permute-start | bytes 786440 | tf_op jit(solution)/shard_map/ppermute | solution.py:409
  156.3 29.9 %copy-start.2 = (bf16[8,128,256]{2,1,0:T(8,128)(2,1)S(1)}, bf16[8,128,256]{2,1,0:T(8,128)(2,1)}, u32[]{:S(2)}) copy-start(bf16[8,128,256]{2,1,0:T(8,128)(2,1)} %hp_ref.3) | copy-start | bytes 1572868
  156.3 29.9 %copy-start.13 = (bf16[256,256]{1,0:T(8,128)(2,1)S(1)}, bf16[256,256]{1,0:T(8,128)(2,1)}, u32[]{:S(2)}) copy-start(bf16[256,256]{1,0:T(8,128)(2,1)} %wf_ref.2) | copy-start | bytes 393220
  156.3 29.9 %copy-start.20 = (f32[256,1024]{1,0:T(8,128)S(1)}, f32[256,1024]{1,0:T(8,128)}, u32[]{:S(2)}) copy-start(f32[256,1024]{1,0:T(8,128)} %copy-done.19) | copy-start | bytes 3145732
  186.2 23.8 %copy-start.14 = (bf16[256,256]{1,0:T(8,128)(2,1)S(1)}, bf16[256,256]{1,0:T(8,128)(2,1)}, u32[]{:S(2)}) copy-start(bf16[256,256]{1,0:T(8,128)(2,1)} %wq_ref.3) | copy-start | bytes 393220
  186.2 23.8 %copy-start.15 = (bf16[256,256]{1,0:T(8,128)(2,1)S(1)}, bf16[256,256]{1,0:T(8,128)(2,1)}, u32[]{:S(2)}) copy-start(bf16[256,256]{1,0:T(8,128)(2,1)} %wk_ref.3) | copy-start | bytes 393220
  186.2 23.8 %copy-start.16 = (bf16[256,256]{1,0:T(8,128)(2,1)S(1)}, bf16[256,256]{1,0:T(8,128)(2,1)}, u32[]{:S(2)}) copy-start(bf16[256,256]{1,0:T(8,128)(2,1)} %wv_ref.3) | copy-start | bytes 393220
  186.2 23.8 %copy-start.17 = (bf16[256,256]{1,0:T(8,128)(2,1)S(1)}, bf16[256,256]{1,0:T(8,128)(2,1)}, u32[]{:S(2)}) copy-start(bf16[256,256]{1,0:T(8,128)(2,1)} %wg_ref.3) | copy-start | bytes 393220
  210.0 29.4 %copy-start.3 = (bf16[256,1024]{1,0:T(8,128)(2,1)S(1)}, bf16[256,1024]{1,0:T(8,128)(2,1)}, u32[]{:S(2)}) copy-start(bf16[256,1024]{1,0:T(8,128)(2,1)} %ww_ref.1) | copy-start | bytes 1572868
  210.0 29.4 %copy-start.4 = (bf16[1024,256]{1,0:T(8,128)(2,1)S(1)}, bf16[1024,256]{1,0:T(8,128)(2,1)}, u32[]{:S(2)}) copy-start(bf16[1024,256]{1,0:T(8,128)(2,1)} %wn_ref.1) | copy-start | bytes 1572868
  210.0 29.4 %copy-start.18 = (bf16[256,256]{1,0:T(8,128)(2,1)S(1)}, bf16[256,256]{1,0:T(8,128)(2,1)}, u32[]{:S(2)}) copy-start(bf16[256,256]{1,0:T(8,128)(2,1)} %wf_ref.3) | copy-start | bytes 393220

commit v2 on v1

v2 whole, which is shorter than its diff:
```python
import functools

import jax
import jax.numpy as jnp
import numpy as np
from jax import lax
from jax.experimental import pallas as pl
from jax.experimental.pallas import tpu as pltpu
from jax.sharding import PartitionSpec as P

HEADS = 8
HEAD_DIM = 32
EPS = 1e-05
MASK_SCALE = 1000000000.0

F32 = jnp.float32
BF16 = jnp.bfloat16


def mask_parts():
    parts = []
    rest = np.float64(-MASK_SCALE)
    for _ in range(3):
        part = np.float64(np.asarray(rest, jnp.bfloat16))
        parts.append(float(part))
        rest = rest - part
    assert rest == 0.0
    return parts


def standardize(values):
    center = values - jnp.mean(values, -1, keepdims=True)
    spread = jnp.mean(center * center, -1, keepdims=True)
    return center * lax.rsqrt(spread + EPS)


def dot_tt(a, b):
    return lax.dot_general(a, b, (((0,), (1,)), ((), ())), preferred_element_type=F32)


def dot_tn(a, b):
    return lax.dot_general(a, b, (((0,), (0,)), ((), ())), preferred_element_type=F32)


def dot_nt(a, b):
    return lax.dot_general(a, b, (((1,), (1,)), ((), ())), preferred_element_type=F32)


def dot_nn(a, b):
    return lax.dot_general(a, b, (((1,), (0,)), ((), ())), preferred_element_type=F32)


def whole(*_):
    return pl.BlockSpec(memory_space=pltpu.VMEM)


def params(mib=24):
    return pltpu.CompilerParams(vmem_limit_bytes=mib * 1024 * 1024)


def cost(us):
    return pl.CostEstimate(flops=int(us * 1e-6 * 9e14), bytes_accessed=1024, transcendentals=0)


def tokens_kernel(hp_ref, ok_ref, wq_ref, wk_ref, wv_ref, wg_ref, send_ref, gate_ref):
    x = standardize(hp_ref[...].reshape(1024, 256).astype(F32)).astype(BF16)
    scale = HEAD_DIM ** (-0.5)
    for n, w_ref in enumerate((wq_ref, wk_ref, wv_ref)):
        t = dot_tt(w_ref[...], x)
        if n == 0:
            t = t * scale
        t = t.astype(BF16)
        for h in range(HEADS):
            for s in range(8):
                send_ref[h, n * 256 + s * 32 : n * 256 + (s + 1) * 32, :] = t[
                    h * 32 : (h + 1) * 32, s * 128 : (s + 1) * 128
                ]
    ok = jnp.concatenate([ok_ref[...], jnp.zeros((8, 128), F32)], 0).astype(BF16)
    for h in range(HEADS):
        send_ref[h, 768:784, :] = ok
    gate_ref[...] = jax.nn.sigmoid(dot_tt(wg_ref[...], x))


def tokens_call(hp, ok, wq, wk, wv, wg):
    return pl.pallas_call(
        tokens_kernel,
        out_shape=(
            jax.ShapeDtypeStruct((8, 784, 128), BF16),
            jax.ShapeDtypeStruct((256, 1024), F32),
        ),
        in_specs=[whole()] * 6,
        out_specs=(whole(), whole()),
        compiler_params=params(),
        cost_estimate=cost(5),
        name="tokens",
    )(hp, ok, wq, wk, wv, wg)


BIAS_ROWS = 64


def bias_kernel(z_ref, w_ref, out_ref, rows):
    step = pl.program_id(0)
    w = w_ref[...].astype(F32)
    wsum = jnp.sum(w, -1, keepdims=True)
    wt = jnp.concatenate([w, jnp.zeros((8, 128), F32)], 0).astype(BF16)
    for n in range(BIAS_ROWS):
        zt = z_ref[n].T
        zf = zt.astype(F32)
        mean = jnp.sum(zf, 0, keepdims=True) * (1.0 / 128)
        center = zf - mean
        spread = jnp.sum(center * center, 0, keepdims=True) * (1.0 / 128)
        res = (dot_nn(wt, zt)[0:8] - mean * wsum) * lax.rsqrt(spread + EPS)
        rows[pl.ds(step * BIAS_ROWS + n, 8, stride=128), :] = res

    @pl.when(step == pl.num_programs(0) - 1)
    def _():
        for h in range(HEADS):
            block = rows[h * 128 : (h + 1) * 128, :].T.astype(BF16)
            out_ref[h] = block
            out_ref[HEADS + h] = block


def bias_call(z, w):
    return pl.pallas_call(
        bias_kernel,
        out_shape=jax.ShapeDtypeStruct((16, 128, 128), BF16),
        grid=(128 // BIAS_ROWS,),
        in_specs=[
            pl.BlockSpec((BIAS_ROWS, 128, 128), lambda n: (n, 0, 0)),
            pl.BlockSpec((8, 128), lambda n: (0, 0)),
        ],
        out_specs=pl.BlockSpec((16, 128, 128), lambda n: (0, 0, 0)),
        scratch_shapes=[pltpu.VMEM((1024, 128), F32)],
        compiler_params=params(60),
        cost_estimate=cost(6),
        name="pair_bias",
    )(z, w)


def attend_kernel(width, unroll, n_bias, blocks, has_other, first, last, *refs):
    place_ref, own_ref = refs[:2]
    refs = refs[2:]
    sources = [own_ref]
    if has_other:
        sources.append(refs[0])
        refs = refs[1:]
    bias_refs = refs[:n_bias]
    refs = refs[n_bias:]
    if not first:
        m_in, l_in, acc_in = refs[:3]
        refs = refs[3:]
    if last:
        o_ref, keys = refs
    else:
        m_ref, l_ref, acc_ref, keys = refs
    z = place_ref[0]
    core = place_ref[1]
    parts = mask_parts()
    rowid = lax.broadcasted_iota(jnp.int32, (16, 128), 0)
    coeff = jnp.where(rowid == 0, parts[0], jnp.where(rowid == 1, parts[1], jnp.where(rowid == 2, parts[2], 0.0)))
    rowid = lax.broadcasted_iota(jnp.int32, (16, width), 0)
    ones = jnp.where(rowid < 3, 1.0, 0.0).astype(BF16)
    places = [(sources[far], lax.rem(z + shift + 8, 8)) for shift, far, _ in blocks]

    for n, (src, zz) in enumerate(places):
        okay = src[zz, 768:784, :].astype(F32)
        for s in range(8):
            mask = ((1.0 - okay[s : s + 1, :]) * coeff).astype(BF16)
            keys[n, s] = jnp.concatenate([src[zz, 256 + s * 32 : 256 + (s + 1) * 32, :], mask], 0).T

    span = width // 128

    def bias_block(n, tile):
        _, far, operands = blocks[n]
        slot = 1 - core if far else core
        ref = bias_refs[operands[tile * width // 512]]
        base = tile * span if ref.shape[1] == 8 else tile * span % 4
        return jnp.concatenate([ref[slot, base + u] for u in range(span)], 1)

    def scores(s, tile):
        kx = jnp.concatenate([keys[n, s] for n in range(len(blocks))], 0)
        q = jnp.concatenate(
            [own_ref[tile * span + u, pl.ds(pl.multiple_of(s * 32, 32), 32), :] for u in range(span)], 1
        )
        qx = jnp.concatenate([q, ones], 0)
        bias = jnp.concatenate([bias_block(n, tile) for n in range(len(blocks))], 0)
        return dot_nn(kx, qx) + bias.astype(F32)

    def finish(s, tile, score):
        lanes = slice(tile * width, (tile + 1) * width)
        top = jnp.max(score, 0, keepdims=True)
        if not first:
            before = m_in[s, :, lanes]
            top = jnp.maximum(top, before)
        probs = jnp.exp(score - top)
        total = jnp.sum(probs, 0, keepdims=True)
        vt = jnp.concatenate(
            [src[zz, pl.ds(pl.multiple_of(512 + s * 32, 32), 32), :] for src, zz in places], 1
        )
        accum = dot_nn(vt, probs.astype(BF16))
        if not first:
            factor = jnp.exp(before - top)
            total = total + l_in[s, :, lanes] * factor
            accum = accum + acc_in[s, :, lanes] * factor
        if last:
            out = (accum / total).astype(o_ref.dtype)
            for u in range(span):
                o_ref[tile * span + u, pl.ds(pl.multiple_of(s * 32, 32), 32), :] = out[
                    :, u * 128 : (u + 1) * 128
                ]
        else:
            m_ref[s, :, lanes] = top
            l_ref[s, :, lanes] = total
            acc_ref[s, :, lanes] = accum

    def some_sequences(k, carry):
        items = [(k * unroll + d, tile) for d in range(unroll) for tile in range(1024 // width)]
        score = scores(*items[0])
        for n, item in enumerate(items):
            upcoming = scores(*items[n + 1]) if n + 1 < len(items) else None
            finish(*item, score)
            score = upcoming
        return carry

    lax.fori_loop(0, 8 // unroll, some_sequences, 0)


def attend_call(place, own, other, biases, blocks, state, last, us):
    first = state is None
    if last:
        out_shape = jax.ShapeDtypeStruct((8, 256, 128), F32)
        out_specs = whole()
    else:
        out_shape = (
            jax.ShapeDtypeStruct((8, 1, 1024), F32),
            jax.ShapeDtypeStruct((8, 1, 1024), F32),
            jax.ShapeDtypeStruct((8, 32, 1024), F32),
        )
        out_specs = (whole(),) * 3
    args = [place, own] + ([] if other is None else [other]) + list(biases) + ([] if first else list(state))
    unroll = 4 if len(blocks) <= 4 else 2
    return pl.pallas_call(
        functools.partial(attend_kernel, 512, unroll, len(biases), blocks, other is not None, first, last),
        out_shape=out_shape,
        in_specs=[pl.BlockSpec(memory_space=pltpu.SMEM)] + [whole()] * (len(args) - 1),
        out_specs=out_specs,
        scratch_shapes=[pltpu.VMEM((len(blocks), 8, 128, 48), BF16)],
        compiler_params=params(),
        cost_estimate=cost(us),
        name="attend",
    )(*args)


def mix_kernel(o_ref, gate_ref, hp_ref, present_ref, wf_ref, m1_ref, x2_ref):
    pieces = []
    wf = wf_ref[...]
    for s in range(8):
        ot = jnp.concatenate([o_ref[h, s * 32 : (s + 1) * 32, :] for h in range(HEADS)], 0)
        at = (ot.astype(F32) * gate_ref[:, s * 128 : (s + 1) * 128]).astype(BF16)
        m1 = hp_ref[s].astype(F32) + dot_tn(at, wf)
        m1_ref[s] = m1
        pieces.append(standardize(m1).reshape(16, 8, 256))
    present = present_ref[...]
    wide = jnp.concatenate([present, jnp.zeros_like(present)], 1)
    pieces.append(jnp.stack([pltpu.roll(wide, (256 - 8 * a) % 256, 1) for a in range(16)], 0))
    x2_ref[...] = jnp.concatenate(pieces, 1).astype(BF16)


def mix_call(o, gate, hp, present, wf):
    return pl.pallas_call(
        mix_kernel,
        out_shape=(
            jax.ShapeDtypeStruct((8, 128, 256), F32),
            jax.ShapeDtypeStruct((16, 72, 256), BF16),
        ),
        in_specs=[whole()] * 5,
        out_specs=(whole(), whole()),
        compiler_params=params(),
        cost_estimate=cost(5),
        name="row_mix",
    )(o, gate, hp, present, wf)


def column_kernel(x_ref, wq_ref, wk_ref, wv_ref, wg_ref, out_ref, rows0, rows1):
    x = x_ref[...].astype(F32)
    rows = (rows0, rows1)
    xs = x[:, :64, :].reshape(1024, 256)
    rows0[...] = xs[:, :128]
    rows1[...] = xs[:, 128:]
    masks = (x[:, 64:72, :128].reshape(128, 128) - 1.0) * MASK_SCALE
    cols = jnp.concatenate(
        [jnp.concatenate([r[pl.ds(i, 128, stride=8), :] for r in rows], 1) for i in range(8)], 0
    ).astype(BF16)
    scale = HEAD_DIM ** (-0.5)
    qt = (dot_tt(wq_ref[...], cols) * scale).astype(BF16)
    kn = dot_nn(cols, wk_ref[...]).astype(BF16)
    vt = dot_tt(wv_ref[...], cols).astype(BF16)
    gt = jax.nn.sigmoid(dot_tt(wg_ref[...], cols))

    def scores(i, pair):
        lanes = slice(i * 128, (i + 1) * 128)
        sides = []
        for h in (pair * 2, pair * 2 + 1):
            parts = [qt[h * 32 : (h + 1) * 32, lanes]]
            if h > 0:
                parts.insert(0, jnp.zeros((h * 32, 128), BF16))
            if h < HEADS - 1:
                parts.append(jnp.zeros(((HEADS - 1 - h) * 32, 128), BF16))
            sides.append(jnp.concatenate(parts, 0))
        q = jnp.concatenate(sides, 1)
        return dot_nn(kn[i * 128 : (i + 1) * 128, :], q) + masks[:, i : i + 1]

    def finish(i, pair, score):
        lanes = slice(i * 128, (i + 1) * 128)
        probs = jnp.exp(score - jnp.max(score, 0, keepdims=True))
        total = jnp.sum(probs, 0, keepdims=True)
        accum = dot_nn(vt[pair * 64 : (pair + 1) * 64, lanes], probs.astype(BF16)) / total
        return [accum[:32, :128], accum[32:, 128:]]

    items = [(i, pair) for i in range(8) for pair in range(HEADS // 2)]
    score = scores(*items[0])
    heads = []
    for n, (i, pair) in enumerate(items):
        upcoming = scores(*items[n + 1]) if n + 1 < len(items) else None
        heads += finish(i, pair, score)
        score = upcoming
        if pair == HEADS // 2 - 1:
            an = (jnp.concatenate(heads, 0) * gt[:, i * 128 : (i + 1) * 128]).T
            heads = []
            for k, r in enumerate(rows):
                r[pl.ds(i, 128, stride=8), :] = an[:, k * 128 : (k + 1) * 128]
    out_ref[...] = jnp.concatenate([r[...] for r in rows], 1).astype(BF16).reshape(16, 64, 256)


def column_call(x, wq, wk, wv, wg):
    return pl.pallas_call(
        column_kernel,
        out_shape=jax.ShapeDtypeStruct((16, 64, 256), BF16),
        in_specs=[whole()] * 5,
        out_specs=whole(),
        scratch_shapes=[pltpu.VMEM((1024, 128), F32)] * 2,
        compiler_params=params(),
        cost_estimate=cost(10),
        name="column",
    )(x, wq, wk, wv, wg)


def final_kernel(a_ref, m1_ref, wf_ref, ww_ref, wn_ref, out_ref):
    a = a_ref[...].astype(F32)
    wf = wf_ref[...]
    ww = ww_ref[...]
    wn = wn_ref[...]
    for p in range(2):
        a2 = jnp.concatenate(
            [a[:, s * 8 : (s + 1) * 8, :].reshape(128, 256) for s in range(p * 4, p * 4 + 4)], 0
        ).astype(BF16)
        m2 = m1_ref[p * 4 : p * 4 + 4].reshape(512, 256) + dot_nn(a2, wf)
        x3 = standardize(m2).astype(BF16)
        hid = jnp.maximum(dot_nn(x3, ww), 0.0).astype(BF16)
        out_ref[p * 4 : p * 4 + 4] = (m2 + dot_nn(hid, wn)).astype(BF16).reshape(4, 128, 256)


def final_call(a, m1, wf, ww, wn):
    return pl.pallas_call(
        final_kernel,
        out_shape=jax.ShapeDtypeStruct((8, 128, 256), BF16),
        in_specs=[whole()] * 5,
        out_specs=whole(),
        compiler_params=params(),
        cost_estimate=cost(6),
        name="transition",
    )(a, m1, wf, ww, wn)


def on_device(
    homolog_profile,
    couplings_tensor,
    present_entries,
    resolved_positions,
    coupling_logit_matrix,
    horizontal_asking_matrix,
    horizontal_lookup_matrix,
    horizontal_content_matrix,
    horizontal_sigmoid_matrix,
    horizontal_final_matrix,
    vertical_asking_matrix,
    vertical_lookup_matrix,
    vertical_content_matrix,
    vertical_sigmoid_matrix,
    vertical_final_matrix,
    widening_matrix,
    narrowing_matrix,
):
    seq = lax.axis_index("seq")
    res = lax.axis_index("res")
    same_core = [[r for r in range(16) if r % 2 == c] for c in range(2)]
    to_right = [(a, (a + 2) % 16) for a in range(16)]
    to_left = [(a, (a - 2) % 16) for a in range(16)]
    swap = [(a, a ^ 1) for a in range(16)]

    wide_groups = [
        [(z * 2 + y) * 16 + g * 2 + c for y in range(2) for g in range(8)] for z in range(8) for c in range(2)
    ]

    def to_heads(x):
        return lax.all_to_all(x, "res", 0, 0, axis_index_groups=same_core, tiled=True)

    present = present_entries.astype(F32)
    okay = (present_entries * resolved_positions[None, :]).astype(F32)
    place = jnp.stack([seq // 2, res % 2]).astype(jnp.int32)

    barrier = lax.optimization_barrier
    bias = bias_call(couplings_tensor, coupling_logit_matrix.T)
    pair = lax.all_to_all(bias, ("seq", "res"), 0, 0, axis_index_groups=wide_groups, tiled=True)
    pair = pair.reshape(2, 8, 128, 128)
    send, gate = tokens_call(
        homolog_profile,
        okay,
        horizontal_asking_matrix,
        horizontal_lookup_matrix,
        horizontal_content_matrix,
        horizontal_sigmoid_matrix,
    )

    pair, send = barrier((pair, send))

    def ring(right, left):
        return lax.ppermute(right, "seq", to_right), lax.ppermute(left, "seq", to_left)

    def steps(far, *counts):
        blocks = []
        for n, k in counts:
            blocks += [(k, far, (n, n))] if k == 0 else [(-k, far, (n, n)), (k, far, (n + 1, n + 1))]
        return blocks

    one = ring(pair, pair)
    own = to_heads(send)
    two = ring(*one)
    own, one = barrier((own, one))
    other = lax.ppermute(own, "res", swap)
    near = [pair, *one]
    state = attend_call(place, own, None, near, steps(0, (0, 0), (1, 1)), None, False, 6)
    other, state = barrier((other, state))
    state = attend_call(place, own, other, near, steps(1, (0, 0), (1, 1)), state, False, 6)
    two, state = barrier((two, state))
    three = ring(*two)
    state = attend_call(place, own, other, two, steps(0, (0, 2)) + steps(1, (0, 2)), state, False, 7)
    three, state = barrier((three, state))
    four = ring(three[0][:, :4], three[1][:, 4:])
    state = attend_call(place, own, other, three, steps(0, (0, 3)) + steps(1, (0, 3)), state, False, 7)
    o = attend_call(place, own, other, four, [(4, 0, (0, 1)), (4, 1, (0, 1))], state, True, 4)

    o = to_heads(o)
    m1, x2 = mix_call(o, gate, homolog_profile, present, horizontal_final_matrix)
    x2 = lax.all_to_all(x2, "seq", 0, 0, tiled=True)
    a2 = column_call(
        x2, vertical_asking_matrix, vertical_lookup_matrix, vertical_content_matrix, vertical_sigmoid_matrix
    )
    a2 = lax.all_to_all(a2, "seq", 0, 0, tiled=True)
    return final_call(a2, m1, vertical_final_matrix, widening_matrix, narrowing_matrix)


def solution(mesh):
    placed = (
        P("seq", "res", None),
        P("res", "seq", None),
        P("seq", "res"),
        P("res"),
    ) + (P(),) * 13
    return jax.shard_map(
        on_device, mesh=mesh, in_specs=placed, out_specs=P("seq", "res", None), check_vma=False
    )
```

time: 244 us -> 168 us (0.69)
  Pallas kernels: 98 us -> 50 us
  waiting for transfers between devices: 50.4 us -> 24.4 us
  local copies, waits for them, and re-layouts: 5.56 us -> 1.12 us
    pallas_call x6, Pallas kernels: 78.8 us -> 39.8 us  [the longest x5 34.8 us: attend_call(): pl.pallas_call(functools.partial(attend_kernel, 512, unroll, len(biases),...]
    all_to_all x2 -> x1, waiting for transfers between devices: 20.4 us -> 3.32 us  [to_heads(): lax.all_to_all(x, 'res', 0, 0, axis_index_groups=same_core, tiled=True)]
    ppermute x9 -> x8, waiting for transfers between devices: 30 us -> 14.2 us  [the longest x4 14.2 us: ring(): lax.ppermute(right, 'seq', to_right)]
    pallas_call x1, Pallas kernels: 11.9 us -> 3.97 us  [column_call(): pl.pallas_call(column_kernel, out_shape=jax.ShapeDtypeStruct((16, 64, 256...]
    all_to_all x0 -> x1, starting transfers between devices: none -> 7.48 us  [on_device(): lax.all_to_all(bias, ('seq', 'res'), 0, 0, axis_index_groups=wide_groups,...]
    all_to_all x0 -> x1, waiting for transfers between devices: none -> 6.8 us  [on_device(): lax.all_to_all(bias, ('seq', 'res'), 0, 0, axis_index_groups=wide_groups,...]
    all_to_all x2 -> x1, starting transfers between devices: 10.5 us -> 4.94 us  [to_heads(): lax.all_to_all(x, 'res', 0, 0, axis_index_groups=same_core, tiled=True)]
    unnamed x46 -> x34, local copies, waits for them, and re-layouts: 4.84 us -> 1.08 us
  transfers between devices with their start and end apart: 12 -> 11, of which waited for: 7 -> 4; matrix products, arithmetic and copies ran while one was open for 0% -> 0% of each run, Pallas kernels for 24% -> 19%
where the time goes in v2:
time: 168 us
  blocking collectives  60.9 us (36%)
  Pallas kernels  50 us (30%)
  starting transfers between devices  31.1 us (19%)
  waiting for transfers between devices  24.4 us (15%)
    pallas_call x5, Pallas kernels, attend_call(): pl.pallas_call(functools.partial(attend_kernel, 512, unroll, len(biases),...  34.8 us
    all_to_all x1, blocking collectives, on_device(): x2 = lax.all_to_all(x2, 'seq', 0, 0, tiled=True)  24.4 us
    all_to_all x1, blocking collectives, on_device(): a2 = lax.all_to_all(a2, 'seq', 0, 0, tiled=True)  19 us
    all_to_all x1, blocking collectives, to_heads(): lax.all_to_all(x, 'res', 0, 0, axis_index_groups=same_core, tiled=True)  17.5 us
    ppermute x4, waiting for transfers between devices, ring(): lax.ppermute(right, 'seq', to_right)  14.2 us
    ppermute x4, starting transfers between devices, ring(): lax.ppermute(left, 'seq', to_left)  13.7 us
    all_to_all x1, starting transfers between devices, on_device(): lax.all_to_all(bias, ('seq', 'res'), 0, 0, axis_index_groups=wide_groups,...  7.48 us
    all_to_all x1, waiting for transfers between devices, on_device(): lax.all_to_all(bias, ('seq', 'res'), 0, 0, axis_index_groups=wide_groups,...  6.8 us
  transfers between devices with their start and end apart: 11, of which 4 were waited for; matrix products, arithmetic and copies ran while one was open for 0% of the time, Pallas kernels for 19%

profile of v2, /device:TPU:2, one launch (start us, length us, event | category | flops | bytes accessed | tf_op | source)
XLA Modules:
  0.0 167.9 jit_solution(3455824147137209383)
XLA Ops:
  0.0 0.0 copy-start.3
  0.0 0.0 copy-start.4
  0.0 0.0 copy-start.5
  0.0 0.0 copy-start.6
  0.0 5.1 %pair_bias.1 = bf16[16,128,128]{2,1,0:T(8,128)(2,1)} custom-call(bf16[128,128,128]{2,1,0:T(8,128)(2,1)} %z_ref.1, bf16[8,128]{1,0:T(8,128)(2,1)} %bitcast.8), custom_call_target="tpu_custom_call" | custom-call | flops 5400000000 | bytes 1024 | tf_op jit(solution)/shard_map/pair_bias/pallas_call | solution.py:125
  5.1 7.5 %all-to-all-start = ((bf16[16,128,128]{2,1,0:T(8,128)(2,1)}), bf16[16,128,128]{2,1,0:T(8,128)(2,1)S(1)}, u32[]{:S(2)}, u32[]{:S(2)}) async-start(bf16[16,128,128]{2,1,0:T(8,128)(2,1)} %pair_bias.1), calls=%async_computation | async-start | bytes 1048576 | tf_op jit(solution)/shard_map/all_to_all | solution.py:415
  12.6 0.0 copy-done.15
  12.6 0.0 copy-done.16
  12.6 0.0 copy-done
  12.6 0.0 copy-done.3
  12.6 0.0 copy-done.4
  12.6 0.0 copy-done.5
  12.7 0.0 copy-done.6
  12.7 2.3 %tokens.1 = (bf16[8,784,128]{2,1,0:T(8,128)(2,1)}, f32[256,1024]{1,0:T(8,128)S(1)}) custom-call(bf16[8,128,256]{2,1,0:T(8,128)(2,1)S(1)} %copy-done, f32[8,128]{1,0:T(8,128)S(1)} %get-tuple-element.76.ok_ref, bf16[256,256]{1,0:T(8,128)(2,1)S(1)} %copy-done.3, bf16[256,256]{1,0:T(8,128)(2,1)S(1)} %copy-done.4, bf16[256,256]{1,0:T(8,128)(2,1)S(1)} %copy-done.5, ...), custom_call_target="tpu_custom_call" | custom-call | flops 4499999744 | bytes 1024 | tf_op jit(solution)/shard_map/tokens/pallas_call | solution.py:85
  15.0 1.0 copy-done.13
  16.0 6.8 %all-to-all-done = bf16[16,128,128]{2,1,0:T(8,128)(2,1)S(1)} async-done(((bf16[16,128,128]{2,1,0:T(8,128)(2,1)}), bf16[16,128,128]{2,1,0:T(8,128)(2,1)S(1)}, u32[]{:S(2)}, u32[]{:S(2)}) %all-to-all-start) | async-done | bytes 524320 | tf_op jit(solution)/shard_map/all_to_all | solution.py:415
  22.8 4.9 %all-to-all-start.1 = ((bf16[8,784,128]{2,1,0:T(8,128)(2,1)}), bf16[8,784,128]{2,1,0:T(8,128)(2,1)S(1)}, u32[]{:S(2)}, u32[]{:S(2)}) async-start(bf16[8,784,128]{2,1,0:T(8,128)(2,1)} %get-tuple-element.41), calls=%async_computation.1 | async-start | bytes 3211264 | tf_op jit(solution)/shard_map/all_to_all | solution.py:407
  27.7 1.9 %collective-permute-start = (bf16[2,8,128,128]{3,2,1,0:T(8,128)(2,1)S(1)}, bf16[2,8,128,128]{3,2,1,0:T(8,128)(2,1)S(1)}, u32[]{:S(2)}, u32[]{:S(2)}) collective-permute-start(bf16[2,8,128,128]{3,2,1,0:T(8,128)(2,1)S(1)} %bitcast.4), channel_id=1, source_target_pairs={{0,32},{16,48},{32,64},{48,80},{64,96},{80,112},{96,128},{112,144}... | collective-permute-start | bytes 1572872 | tf_op jit(solution)/shard_map/ppermute | solution.py:429
  29.6 3.9 %collective-permute-start.1 = (bf16[2,8,128,128]{3,2,1,0:T(8,128)(2,1)S(1)}, bf16[2,8,128,128]{3,2,1,0:T(8,128)(2,1)}, u32[]{:S(2)}, u32[]{:S(2)}) collective-permute-start(bf16[2,8,128,128]{3,2,1,0:T(8,128)(2,1)S(1)} %bitcast.5), channel_id=1, source_target_pairs={{0,224},{16,240},{32,0},{48,16},{64,32},{80,48},{96,64},{112,80},{... | collective-permute-start | bytes 1572872 | tf_op jit(solution)/shard_map/ppermute | solution.py:429
  33.6 10.3 %collective-permute-done.refs_3_.refs_4_ = bf16[2,8,128,128]{3,2,1,0:T(8,128)(2,1)S(1)} collective-permute-done((bf16[2,8,128,128]{3,2,1,0:T(8,128)(2,1)S(1)}, bf16[2,8,128,128]{3,2,1,0:T(8,128)(2,1)S(1)}, u32[]{:S(2)}, u32[]{:S(2)}) %collective-permute-start) | collective-permute-done | bytes 524320 | tf_op jit(solution)/shard_map/ppermute | solution.py:429
  43.9 0.0 collective-permute-done.1.refs_4_.refs_5_
  43.9 3.3 %all-to-all-done.1.refs_1_ = bf16[8,784,128]{2,1,0:T(8,128)(2,1)S(1)} async-done(((bf16[8,784,128]{2,1,0:T(8,128)(2,1)}), bf16[8,784,128]{2,1,0:T(8,128)(2,1)S(1)}, u32[]{:S(2)}, u32[]{:S(2)}) %all-to-all-start.1) | async-done | bytes 1605664 | tf_op jit(solution)/shard_map/all_to_all | solution.py:407
  47.2 0.0 collective-permute-start.2
  47.2 0.1 pad_add_fusion.refs_0_
  47.3 1.9 %collective-permute-start.3 = (bf16[2,8,128,128]{3,2,1,0:T(8,128)(2,1)S(1)}, bf16[2,8,128,128]{3,2,1,0:T(8,128)(2,1)S(1)}, u32[]{:S(2)}, u32[]{:S(2)}) collective-permute-start(bf16[2,8,128,128]{3,2,1,0:T(8,128)(2,1)S(1)} %collective-permute-done.refs_3_.refs_4_), channel_id=1, source_target_pairs={{0,32},{16,48},{32,64},{48,80},{64,96},{80,112},{96,128},{112,144}... | collective-permute-start | bytes 1572872 | tf_op jit(solution)/shard_map/ppermute | solution.py:429
  49.2 4.0 %collective-permute-start.4 = (bf16[2,8,128,128]{3,2,1,0:T(8,128)(2,1)}, bf16[2,8,128,128]{3,2,1,0:T(8,128)(2,1)S(1)}, u32[]{:S(2)}, u32[]{:S(2)}) collective-permute-start(bf16[2,8,128,128]{3,2,1,0:T(8,128)(2,1)} %collective-permute-done.1.refs_4_.refs_5_), channel_id=1, source_target_pairs={{0,224},{16,240},{32,0},{48,16},{64,32},{80,48},{96,64},{112,80},{... | collective-permute-start | bytes 1572872 | tf_op jit(solution)/shard_map/ppermute | solution.py:429
  53.3 6.2 %attend.5 = (f32[8,1,1024]{2,1,0:T(1,128)S(1)}, f32[8,1,1024]{2,1,0:T(1,128)S(1)}, f32[8,32,1024]{2,1,0:T(8,128)S(1)}) custom-call(s32[2]{0:T(128)S(1)} %pad_add_fusion.refs_0_, bf16[8,784,128]{2,1,0:T(8,128)(2,1)S(1)} %all-to-all-done.1.refs_1_, bf16[2,8,128,128]{3,2,1,0:T(8,128)(2,1)S(1)} %bitcast.6, ...), custom_call_target="tpu_custom_call" | custom-call | flops 5400000000 | bytes 1024 | tf_op jit(solution)/shard_map/attend/pallas_call | solution.py:243
  59.5 0.0 collective-permute-done.2.refs_2_
  59.5 7.0 %attend.6 = (f32[8,1,1024]{2,1,0:T(1,128)S(1)}, f32[8,1,1024]{2,1,0:T(1,128)S(1)}, f32[8,32,1024]{2,1,0:T(8,128)S(1)}) custom-call(s32[2]{0:T(128)S(1)} %pad_add_fusion.refs_0_, bf16[8,784,128]{2,1,0:T(8,128)(2,1)S(1)} %all-to-all-done.1.refs_1_, bf16[8,784,128]{2,1,0:T(8,128)(2,1)} %collective-permute-done.2.refs_2_, bf16[2,8,128,128]{3,2,1,0:T(8,128)(2,1)S(1)} %bitcast.7, ...), custom_call_target="tpu_custom_call" | custom-call | flops 5400000000 | bytes 1024 | tf_op jit(solution)/shard_map/attend/pallas_call | solution.py:243
  66.5 0.0 collective-permute-done.3.refs_3_
  66.5 0.0 collective-permute-done.4.refs_4_
  66.5 0.3 collective-permute-start.5
  66.8 3.2 %collective-permute-start.6 = (bf16[2,8,128,128]{3,2,1,0:T(8,128)(2,1)S(1)}, bf16[2,8,128,128]{3,2,1,0:T(8,128)(2,1)S(1)}, u32[]{:S(2)}, u32[]{:S(2)}) collective-permute-start(bf16[2,8,128,128]{3,2,1,0:T(8,128)(2,1)S(1)} %collective-permute-done.4.refs_4_), channel_id=1, source_target_pairs={{0,224},{16,240},{32,0},{48,16},{64,32},{80,48},{96,64},{112,80},{... | collective-permute-start | bytes 1572872 | tf_op jit(solution)/shard_map/ppermute | solution.py:429
  70.0 8.1 %attend.7 = (f32[8,1,1024]{2,1,0:T(1,128)S(1)}, f32[8,1,1024]{2,1,0:T(1,128)S(1)}, f32[8,32,1024]{2,1,0:T(8,128)S(1)}) custom-call(s32[2]{0:T(128)S(1)} %pad_add_fusion.refs_0_, bf16[8,784,128]{2,1,0:T(8,128)(2,1)S(1)} %all-to-all-done.1.refs_1_, bf16[8,784,128]{2,1,0:T(8,128)(2,1)} %collective-permute-done.2.refs_2_, ...), custom_call_target="tpu_custom_call" | custom-call | flops 6300000256 | bytes 1024 | tf_op jit(solution)/shard_map/attend/pallas_call | solution.py:243
  78.2 3.9 %collective-permute-done.5.refs_3_ = bf16[2,8,128,128]{3,2,1,0:T(8,128)(2,1)S(1)} collective-permute-done((bf16[2,8,128,128]{3,2,1,0:T(8,128)(2,1)S(1)}, bf16[2,8,128,128]{3,2,1,0:T(8,128)(2,1)S(1)}, u32[]{:S(2)}, u32[]{:S(2)}) %collective-permute-start.5) | collective-permute-done | bytes 524320 | tf_op jit(solution)/shard_map/ppermute | solution.py:429
  82.1 0.0 collective-permute-done.6.refs_4_
  82.1 0.9 collective-permute-start.7
  83.0 2.5 %collective-permute-start.8 = (bf16[2,4,128,128]{3,2,1,0:T(8,128)(2,1)S(1)}, bf16[2,4,128,128]{3,2,1,0:T(8,128)(2,1)S(1)}, u32[]{:S(2)}, u32[]{:S(2)}) collective-permute-start(bf16[2,4,128,128]{3,2,1,0:T(8,128)(2,1)S(1)} %slice.7), channel_id=1, source_target_pairs={{0,224},{16,240},{32,0},{48,16},{64,32},{80,48},{96,64},{112,80},{... | collective-permute-start | bytes 786440 | tf_op jit(solution)/shard_map/ppermute | solution.py:429
  85.5 8.1 %attend.8 = (f32[8,1,1024]{2,1,0:T(1,128)S(1)}, f32[8,1,1024]{2,1,0:T(1,128)S(1)}, f32[8,32,1024]{2,1,0:T(8,128)S(1)}) custom-call(s32[2]{0:T(128)S(1)} %pad_add_fusion.refs_0_, bf16[8,784,128]{2,1,0:T(8,128)(2,1)S(1)} %all-to-all-done.1.refs_1_, bf16[8,784,128]{2,1,0:T(8,128)(2,1)} %collective-permute-done.2.refs_2_, ...), custom_call_target="tpu_custom_call" | custom-call | flops 6300000256 | bytes 1024 | tf_op jit(solution)/shard_map/attend/pallas_call | solution.py:243
  93.6 0.0 collective-permute-done.7.refs_3_
  93.6 0.0 collective-permute-done.8.refs_4_
  93.6 5.3 %attend.9 = f32[8,256,128]{2,1,0:T(8,128)S(1)} custom-call(s32[2]{0:T(128)S(1)} %pad_add_fusion.refs_0_, bf16[8,784,128]{2,1,0:T(8,128)(2,1)S(1)} %all-to-all-done.1.refs_1_, bf16[8,784,128]{2,1,0:T(8,128)(2,1)} %collective-permute-done.2.refs_2_, bf16[2,4,128,128]{3,2,1,0:T(8,128)(2,1)S(1)} %collective-permute-done.7.refs_3_, ...), custom_call_target="tpu_custom_call" | custom-call | flops 3600000000 | bytes 1024 | tf_op jit(solution)/shard_map/attend/pallas_call | solution.py:243
  98.9 0.0 copy-start.7
  98.9 0.0 copy-start.14
  98.9 17.5 %all_to_all.25.o_ref = f32[8,256,128]{2,1,0:T(8,128)S(1)} all-to-all(f32[8,256,128]{2,1,0:T(8,128)S(1)} %attend.9), channel_id=1, replica_groups={{0,2,4,6,8,10,12,14},{1,3,5,7,9,11,13,15},{16,18,20,22,24,26,28,30},{17..., dimensions={0} | all-to-all | bytes 2097152 | tf_op jit(solution)/shard_map/all_to_all | solution.py:407
  116.5 0.0 copy-done.7
  116.5 0.0 copy-done.14
  116.5 0.0 copy-start.10
  116.5 0.0 copy-start.11
  116.5 1.1 row_mix.1
  117.6 24.4 %all_to_all.26.x_ref = bf16[16,72,256]{2,1,0:T(8,128)(2,1)S(1)} all-to-all(bf16[16,72,256]{2,1,0:T(8,128)(2,1)S(1)} %get-tuple-element.73), channel_id=1, replica_groups=mesh['seq'=16,'res'=16] {'seq'}, dimensions={0} | all-to-all | bytes 1179648 | tf_op jit(solution)/shard_map/all_to_all | solution.py:456
  142.0 0.0 copy-done.8
  142.0 0.0 copy-done.9
  142.0 0.0 copy-done.10
  142.0 0.0 copy-done.11
  142.0 0.0 copy-start.1
  142.0 0.0 copy-start.2
  142.0 0.0 copy-start.12
  142.0 4.0 %column.1 = bf16[16,64,256]{2,1,0:T(8,128)(2,1)S(1)} custom-call(bf16[16,72,256]{2,1,0:T(8,128)(2,1)S(1)} %all_to_all.26.x_ref, bf16[256,256]{1,0:T(8,128)(2,1)S(1)} %copy-done.8, bf16[256,256]{1,0:T(8,128)(2,1)S(1)} %copy-done.9, bf16[256,256]{1,0:T(8,128)(2,1)S(1)} %copy-done.10, bf16[256,256]{1,0:T(8,128)(2,1)S(1)} %copy-done.11), custom_call_target="tpu_custom_call" | custom-call | flops 8999999488 | bytes 1024 | tf_op jit(solution)/shard_map/column/pallas_call | solution.py:337
  146.0 19.0 %all_to_all.27.a_ref = bf16[16,64,256]{2,1,0:T(8,128)(2,1)S(1)} all-to-all(bf16[16,64,256]{2,1,0:T(8,128)(2,1)S(1)} %column.1), channel_id=1, replica_groups=mesh['seq'=16,'res'=16] {'seq'}, dimensions={0} | all-to-all | bytes 1048576 | tf_op jit(solution)/shard_map/all_to_all | solution.py:460
  165.0 0.0 copy-done.1
  165.0 0.0 copy-done.2
  165.0 0.0 copy-done.12
  165.0 2.8 %transition.1 = bf16[8,128,256]{2,1,0:T(8,128)(2,1)} custom-call(bf16[16,64,256]{2,1,0:T(8,128)(2,1)S(1)} %all_to_all.27.a_ref, f32[8,128,256]{2,1,0:T(8,128)S(1)} %get-tuple-element.74.m1_ref, bf16[256,256]{1,0:T(8,128)(2,1)S(1)} %copy-done.12, bf16[256,1024]{1,0:T(8,128)(2,1)S(1)} %copy-done.1, bf16[1024,256]{1,0:T(8,128)(2,1)S(1)} %copy-done.2), custom_call_target="tpu_custom_call" | custom-call | flops 5400000000 | bytes 1024 | tf_op jit(solution)/shard_map/transition/pallas_call | solution.py:365
  (9 shorter events, 0.1 us)
Async XLA Ops:
  0.0 12.6 %copy-start.15 = (s32[8,128]{1,0:T(8,128)S(1)}, s32[8,128]{1,0:T(8,128)}, u32[]{:S(2)}) copy-start(s32[8,128]{1,0:T(8,128)} %param.19) | copy-start | bytes 12292
  0.0 12.6 %copy-start.16 = (s32[128]{0:T(128)S(1)}, s32[128]{0:T(128)}, u32[]{:S(2)}) copy-start(s32[128]{0:T(128)} %param.20) | copy-start | bytes 1540
  0.0 12.6 %copy-start = (bf16[8,128,256]{2,1,0:T(8,128)(2,1)S(1)}, bf16[8,128,256]{2,1,0:T(8,128)(2,1)}, u32[]{:S(2)}) copy-start(bf16[8,128,256]{2,1,0:T(8,128)(2,1)} %hp_ref.3) | copy-start | bytes 1572868
  0.0 12.6 %copy-start.3 = (bf16[256,256]{1,0:T(8,128)(2,1)S(1)}, bf16[256,256]{1,0:T(8,128)(2,1)}, u32[]{:S(2)}) copy-start(bf16[256,256]{1,0:T(8,128)(2,1)} %wq_ref.2) | copy-start | bytes 393220
  0.0 12.6 %copy-start.4 = (bf16[256,256]{1,0:T(8,128)(2,1)S(1)}, bf16[256,256]{1,0:T(8,128)(2,1)}, u32[]{:S(2)}) copy-start(bf16[256,256]{1,0:T(8,128)(2,1)} %wk_ref.2) | copy-start | bytes 393220
  0.0 12.6 %copy-start.5 = (bf16[256,256]{1,0:T(8,128)(2,1)S(1)}, bf16[256,256]{1,0:T(8,128)(2,1)}, u32[]{:S(2)}) copy-start(bf16[256,256]{1,0:T(8,128)(2,1)} %wv_ref.2) | copy-start | bytes 393220
  0.0 12.6 %copy-start.6 = (bf16[256,256]{1,0:T(8,128)(2,1)S(1)}, bf16[256,256]{1,0:T(8,128)(2,1)}, u32[]{:S(2)}) copy-start(bf16[256,256]{1,0:T(8,128)(2,1)} %wg_ref.2) | copy-start | bytes 393220
  5.1 17.6 %all-to-all-start = ((bf16[16,128,128]{2,1,0:T(8,128)(2,1)}), bf16[16,128,128]{2,1,0:T(8,128)(2,1)S(1)}, u32[]{:S(2)}, u32[]{:S(2)}) async-start(bf16[16,128,128]{2,1,0:T(8,128)(2,1)} %pair_bias.1), calls=%async_computation | async-start | bytes 1048576 | tf_op jit(solution)/shard_map/all_to_all | solution.py:415
  15.0 1.0 copy-start.13
  22.8 24.5 %all-to-all-start.1 = ((bf16[8,784,128]{2,1,0:T(8,128)(2,1)}), bf16[8,784,128]{2,1,0:T(8,128)(2,1)S(1)}, u32[]{:S(2)}, u32[]{:S(2)}) async-start(bf16[8,784,128]{2,1,0:T(8,128)(2,1)} %get-tuple-element.41), calls=%async_computation.1 | async-start | bytes 3211264 | tf_op jit(solution)/shard_map/all_to_all | solution.py:407
  27.7 16.2 %collective-permute-start = (bf16[2,8,128,128]{3,2,1,0:T(8,128)(2,1)S(1)}, bf16[2,8,128,128]{3,2,1,0:T(8,128)(2,1)S(1)}, u32[]{:S(2)}, u32[]{:S(2)}) collective-permute-start(bf16[2,8,128,128]{3,2,1,0:T(8,128)(2,1)S(1)} %bitcast.4), channel_id=1, source_target_pairs={{0,32},{16,48},{32,64},{48,80},{64,96},{80,112},{96,128},{112,144}... | collective-permute-start | bytes 1572872 | tf_op jit(solution)/shard_map/ppermute | solution.py:429
  29.6 14.3 %collective-permute-start.1 = (bf16[2,8,128,128]{3,2,1,0:T(8,128)(2,1)S(1)}, bf16[2,8,128,128]{3,2,1,0:T(8,128)(2,1)}, u32[]{:S(2)}, u32[]{:S(2)}) collective-permute-start(bf16[2,8,128,128]{3,2,1,0:T(8,128)(2,1)S(1)} %bitcast.5), channel_id=1, source_target_pairs={{0,224},{16,240},{32,0},{48,16},{64,32},{80,48},{96,64},{112,80},{... | collective-permute-start | bytes 1572872 | tf_op jit(solution)/shard_map/ppermute | solution.py:429
  47.2 12.3 %collective-permute-start.2 = (bf16[8,784,128]{2,1,0:T(8,128)(2,1)S(1)}, bf16[8,784,128]{2,1,0:T(8,128)(2,1)}, u32[]{:S(2)}, u32[]{:S(2)}) collective-permute-start(bf16[8,784,128]{2,1,0:T(8,128)(2,1)S(1)} %all-to-all-done.1.refs_1_), channel_id=1, source_target_pairs={{0,1},{1,0},{2,3},{3,2},{4,5},{5,4},{6,7},{7,6},{8,9},{9,8},{10,11... | collective-permute-start | bytes 4816904 | tf_op jit(solution)/shard_map/ppermute | solution.py:441
  47.3 19.2 %collective-permute-start.3 = (bf16[2,8,128,128]{3,2,1,0:T(8,128)(2,1)S(1)}, bf16[2,8,128,128]{3,2,1,0:T(8,128)(2,1)S(1)}, u32[]{:S(2)}, u32[]{:S(2)}) collective-permute-start(bf16[2,8,128,128]{3,2,1,0:T(8,128)(2,1)S(1)} %collective-permute-done.refs_3_.refs_4_), channel_id=1, source_target_pairs={{0,32},{16,48},{32,64},{48,80},{64,96},{80,112},{96,128},{112,144}... | collective-permute-start | bytes 1572872 | tf_op jit(solution)/shard_map/ppermute | solution.py:429
  49.2 17.3 %collective-permute-start.4 = (bf16[2,8,128,128]{3,2,1,0:T(8,128)(2,1)}, bf16[2,8,128,128]{3,2,1,0:T(8,128)(2,1)S(1)}, u32[]{:S(2)}, u32[]{:S(2)}) collective-permute-start(bf16[2,8,128,128]{3,2,1,0:T(8,128)(2,1)} %collective-permute-done.1.refs_4_.refs_5_), channel_id=1, source_target_pairs={{0,224},{16,240},{32,0},{48,16},{64,32},{80,48},{96,64},{112,80},{... | collective-permute-start | bytes 1572872 | tf_op jit(solution)/shard_map/ppermute | solution.py:429
  66.5 15.5 %collective-permute-start.5 = (bf16[2,8,128,128]{3,2,1,0:T(8,128)(2,1)S(1)}, bf16[2,8,128,128]{3,2,1,0:T(8,128)(2,1)S(1)}, u32[]{:S(2)}, u32[]{:S(2)}) collective-permute-start(bf16[2,8,128,128]{3,2,1,0:T(8,128)(2,1)S(1)} %collective-permute-done.3.refs_3_), channel_id=1, source_target_pairs={{0,32},{16,48},{32,64},{48,80},{64,96},{80,112},{96,128},{112,144}... | collective-permute-start | bytes 1572872 | tf_op jit(solution)/shard_map/ppermute | solution.py:429
  66.8 15.3 %collective-permute-start.6 = (bf16[2,8,128,128]{3,2,1,0:T(8,128)(2,1)S(1)}, bf16[2,8,128,128]{3,2,1,0:T(8,128)(2,1)S(1)}, u32[]{:S(2)}, u32[]{:S(2)}) collective-permute-start(bf16[2,8,128,128]{3,2,1,0:T(8,128)(2,1)S(1)} %collective-permute-done.4.refs_4_), channel_id=1, source_target_pairs={{0,224},{16,240},{32,0},{48,16},{64,32},{80,48},{96,64},{112,80},{... | collective-permute-start | bytes 1572872 | tf_op jit(solution)/shard_map/ppermute | solution.py:429
  82.1 11.5 %collective-permute-start.7 = (bf16[2,4,128,128]{3,2,1,0:T(8,128)(2,1)S(1)}, bf16[2,4,128,128]{3,2,1,0:T(8,128)(2,1)S(1)}, u32[]{:S(2)}, u32[]{:S(2)}) collective-permute-start(bf16[2,4,128,128]{3,2,1,0:T(8,128)(2,1)S(1)} %slice.6), channel_id=1, source_target_pairs={{0,32},{16,48},{32,64},{48,80},{64,96},{80,112},{96,128},{112,144}... | collective-permute-start | bytes 786440 | tf_op jit(solution)/shard_map/ppermute | solution.py:429
  83.0 10.6 %collective-permute-start.8 = (bf16[2,4,128,128]{3,2,1,0:T(8,128)(2,1)S(1)}, bf16[2,4,128,128]{3,2,1,0:T(8,128)(2,1)S(1)}, u32[]{:S(2)}, u32[]{:S(2)}) collective-permute-start(bf16[2,4,128,128]{3,2,1,0:T(8,128)(2,1)S(1)} %slice.7), channel_id=1, source_target_pairs={{0,224},{16,240},{32,0},{48,16},{64,32},{80,48},{96,64},{112,80},{... | collective-permute-start | bytes 786440 | tf_op jit(solution)/shard_map/ppermute | solution.py:429
  98.9 17.5 %copy-start.7 = (bf16[256,256]{1,0:T(8,128)(2,1)S(1)}, bf16[256,256]{1,0:T(8,128)(2,1)}, u32[]{:S(2)}) copy-start(bf16[256,256]{1,0:T(8,128)(2,1)} %wf_ref.2) | copy-start | bytes 393220
  98.9 17.5 %copy-start.14 = (f32[256,1024]{1,0:T(8,128)S(1)}, f32[256,1024]{1,0:T(8,128)}, u32[]{:S(2)}) copy-start(f32[256,1024]{1,0:T(8,128)} %copy-done.13) | copy-start | bytes 3145732
  116.5 25.5 %copy-start.8 = (bf16[256,256]{1,0:T(8,128)(2,1)S(1)}, bf16[256,256]{1,0:T(8,128)(2,1)}, u32[]{:S(2)}) copy-start(bf16[256,256]{1,0:T(8,128)(2,1)} %wq_ref.3) | copy-start | bytes 393220
  116.5 25.5 %copy-start.9 = (bf16[256,256]{1,0:T(8,128)(2,1)S(1)}, bf16[256,256]{1,0:T(8,128)(2,1)}, u32[]{:S(2)}) copy-start(bf16[256,256]{1,0:T(8,128)(2,1)} %wk_ref.3) | copy-start | bytes 393220
  116.5 25.5 %copy-start.10 = (bf16[256,256]{1,0:T(8,128)(2,1)S(1)}, bf16[256,256]{1,0:T(8,128)(2,1)}, u32[]{:S(2)}) copy-start(bf16[256,256]{1,0:T(8,128)(2,1)} %wv_ref.3) | copy-start | bytes 393220
  116.5 25.5 %copy-start.11 = (bf16[256,256]{1,0:T(8,128)(2,1)S(1)}, bf16[256,256]{1,0:T(8,128)(2,1)}, u32[]{:S(2)}) copy-start(bf16[256,256]{1,0:T(8,128)(2,1)} %wg_ref.3) | copy-start | bytes 393220
  142.0 23.0 %copy-start.1 = (bf16[256,1024]{1,0:T(8,128)(2,1)S(1)}, bf16[256,1024]{1,0:T(8,128)(2,1)}, u32[]{:S(2)}) copy-start(bf16[256,1024]{1,0:T(8,128)(2,1)} %ww_ref.1) | copy-start | bytes 1572868
  142.0 23.0 %copy-start.2 = (bf16[1024,256]{1,0:T(8,128)(2,1)S(1)}, bf16[1024,256]{1,0:T(8,128)(2,1)}, u32[]{:S(2)}) copy-start(bf16[1024,256]{1,0:T(8,128)(2,1)} %wn_ref.1) | copy-start | bytes 1572868
  142.0 23.0 %copy-start.12 = (bf16[256,256]{1,0:T(8,128)(2,1)S(1)}, bf16[256,256]{1,0:T(8,128)(2,1)}, u32[]{:S(2)}) copy-start(bf16[256,256]{1,0:T(8,128)(2,1)} %wf_ref.3) | copy-start | bytes 393220

commit v3 on v2

--- a/solution.py
+++ b/solution.py
@@ -138,18 +138,22 @@
     )(z, w)
 
 
-def attend_kernel(width, unroll, n_bias, blocks, has_other, first, last, *refs):
+def attend_kernel(width, unroll, n_bias, blocks, has_other, fetch, first, last, *refs):
     place_ref, own_ref = refs[:2]
     refs = refs[2:]
-    sources = [own_ref]
     if has_other:
-        sources.append(refs[0])
-        refs = refs[1:]
+        far_ref, refs = refs[0], refs[1:]
     bias_refs = refs[:n_bias]
     refs = refs[n_bias:]
     if not first:
         m_in, l_in, acc_in = refs[:3]
         refs = refs[3:]
+    copy = None
+    if fetch:
+        other_ref, far_ref, sem = far_ref, refs[3], refs[5]
+        refs = [*refs[:3], refs[4]]
+        copy = pltpu.make_async_copy(other_ref.at[:, pl.ds(256, 528)], far_ref, sem)
+        copy.start()
     if last:
         o_ref, keys = refs
     else:
@@ -161,13 +165,18 @@
     coeff = jnp.where(rowid == 0, parts[0], jnp.where(rowid == 1, parts[1], jnp.where(rowid == 2, parts[2], 0.0)))
     rowid = lax.broadcasted_iota(jnp.int32, (16, width), 0)
     ones = jnp.where(rowid < 3, 1.0, 0.0).astype(BF16)
-    places = [(sources[far], lax.rem(z + shift + 8, 8)) for shift, far, _ in blocks]
-
-    for n, (src, zz) in enumerate(places):
-        okay = src[zz, 768:784, :].astype(F32)
+    places = []
+    for shift, far, _ in blocks:
+        zz = lax.rem(z + shift + 8, 8)
+        places.append((far_ref, zz, 0) if far else (own_ref, zz, 256))
+
+    if copy is not None:
+        copy.wait()
+    for n, (src, at, base) in enumerate(places):
+        okay = src[at, base + 512 : base + 528, :].astype(F32)
         for s in range(8):
             mask = ((1.0 - okay[s : s + 1, :]) * coeff).astype(BF16)
-            keys[n, s] = jnp.concatenate([src[zz, 256 + s * 32 : 256 + (s + 1) * 32, :], mask], 0).T
+            keys[n, s] = jnp.concatenate([src[at, base + s * 32 : base + (s + 1) * 32, :], mask], 0).T
 
     span = width // 128
 
@@ -196,7 +205,7 @@
         probs = jnp.exp(score - top)
         total = jnp.sum(probs, 0, keepdims=True)
         vt = jnp.concatenate(
-            [src[zz, pl.ds(pl.multiple_of(512 + s * 32, 32), 32), :] for src, zz in places], 1
+            [src[at, pl.ds(pl.multiple_of(base + 256 + s * 32, 32), 32), :] for src, at, base in places], 1
         )
         accum = dot_nn(vt, probs.astype(BF16))
         if not first:
@@ -226,7 +235,7 @@
     lax.fori_loop(0, 8 // unroll, some_sequences, 0)
 
 
-def attend_call(place, own, other, biases, blocks, state, last, us):
+def attend_call(place, own, other, biases, blocks, state, last, us, fetch=False):
     first = state is None
     if last:
         out_shape = jax.ShapeDtypeStruct((8, 256, 128), F32)
@@ -239,13 +248,20 @@
         )
         out_specs = (whole(),) * 3
     args = [place, own] + ([] if other is None else [other]) + list(biases) + ([] if first else list(state))
+    in_specs = [pl.BlockSpec(memory_space=pltpu.SMEM)] + [whole()] * (len(args) - 1)
+    scratch = [pltpu.VMEM((len(blocks), 8, 128, 48), BF16)]
+    if fetch:
+        in_specs[2] = pl.BlockSpec(memory_space=pl.ANY)
+        out_shape += (jax.ShapeDtypeStruct((8, 528, 128), BF16),)
+        out_specs += (whole(),)
+        scratch.append(pltpu.SemaphoreType.DMA)
     unroll = 4 if len(blocks) <= 4 else 2
     return pl.pallas_call(
-        functools.partial(attend_kernel, 512, unroll, len(biases), blocks, other is not None, first, last),
+        functools.partial(attend_kernel, 512, unroll, len(biases), blocks, other is not None, fetch, first, last),
         out_shape=out_shape,
-        in_specs=[pl.BlockSpec(memory_space=pltpu.SMEM)] + [whole()] * (len(args) - 1),
+        in_specs=in_specs,
         out_specs=out_specs,
-        scratch_shapes=[pltpu.VMEM((len(blocks), 8, 128, 48), BF16)],
+        scratch_shapes=scratch,
         compiler_params=params(),
         cost_estimate=cost(us),
         name="attend",
@@ -442,7 +458,7 @@
     near = [pair, *one]
     state = attend_call(place, own, None, near, steps(0, (0, 0), (1, 1)), None, False, 6)
     other, state = barrier((other, state))
-    state = attend_call(place, own, other, near, steps(1, (0, 0), (1, 1)), state, False, 6)
+    *state, other = attend_call(place, own, other, near, steps(1, (0, 0), (1, 1)), state, False, 6, True)
     two, state = barrier((two, state))
     three = ring(*two)
     state = attend_call(place, own, other, two, steps(0, (0, 2)) + steps(1, (0, 2)), state, False, 7)

time: 168 us -> 167 us (level)
  Pallas kernels: 50 us -> 48 us
    pallas_call x5, Pallas kernels: 34.8 us -> 32.8 us  [attend_call(): pl.pallas_call(functools.partial(attend_kernel, 512, unroll, len(biases),...]
  transfers between devices with their start and end apart: 11 -> 11, of which waited for: 4 -> 4; matrix products, arithmetic and copies ran while one was open for 0% -> 0% of each run, Pallas kernels for 19% -> 18%
where the time goes in v3:
time: 167 us
  blocking collectives  60.9 us (36%)
  Pallas kernels  48 us (29%)
  starting transfers between devices  31.1 us (19%)
  waiting for transfers between devices  25.2 us (15%)
    pallas_call x5, Pallas kernels, attend_call(): pl.pallas_call(functools.partial(attend_kernel, 512, unroll, len(biases),...  32.8 us
    all_to_all x1, blocking collectives, on_device(): x2 = lax.all_to_all(x2, 'seq', 0, 0, tiled=True)  24.4 us
    all_to_all x1, blocking collectives, on_device(): a2 = lax.all_to_all(a2, 'seq', 0, 0, tiled=True)  19 us
    all_to_all x1, blocking collectives, to_heads(): lax.all_to_all(x, 'res', 0, 0, axis_index_groups=same_core, tiled=True)  17.5 us
    ppermute x4, waiting for transfers between devices, ring(): lax.ppermute(right, 'seq', to_right)  15.1 us
    ppermute x4, starting transfers between devices, ring(): lax.ppermute(left, 'seq', to_left)  14.4 us
    all_to_all x1, starting transfers between devices, on_device(): lax.all_to_all(bias, ('seq', 'res'), 0, 0, axis_index_groups=wide_groups,...  7.48 us
    all_to_all x1, waiting for transfers between devices, on_device(): lax.all_to_all(bias, ('seq', 'res'), 0, 0, axis_index_groups=wide_groups,...  6.8 us
  transfers between devices with their start and end apart: 11, of which 4 were waited for; matrix products, arithmetic and copies ran while one was open for 0% of the time, Pallas kernels for 18%

profile of v3, /device:TPU:2, one launch (start us, length us, event | category | flops | bytes accessed | tf_op | source)
XLA Modules:
  0.0 166.8 jit_solution(9495594877088889741)
XLA Ops:
  0.0 0.0 copy-start.3
  0.0 0.0 copy-start.4
  0.0 0.0 copy-start.5
  0.0 0.0 copy-start.6
  0.0 5.1 %pair_bias.1 = bf16[16,128,128]{2,1,0:T(8,128)(2,1)} custom-call(bf16[128,128,128]{2,1,0:T(8,128)(2,1)} %z_ref.1, bf16[8,128]{1,0:T(8,128)(2,1)} %bitcast.8), custom_call_target="tpu_custom_call" | custom-call | flops 5400000000 | bytes 1024 | tf_op jit(solution)/shard_map/pair_bias/pallas_call | solution.py:125
  5.1 7.5 %all-to-all-start = ((bf16[16,128,128]{2,1,0:T(8,128)(2,1)}), bf16[16,128,128]{2,1,0:T(8,128)(2,1)S(1)}, u32[]{:S(2)}, u32[]{:S(2)}) async-start(bf16[16,128,128]{2,1,0:T(8,128)(2,1)} %pair_bias.1), calls=%async_computation | async-start | bytes 1048576 | tf_op jit(solution)/shard_map/all_to_all | solution.py:431
  12.6 0.0 copy-done.15
  12.6 0.0 copy-done.16
  12.6 0.0 copy-done
  12.6 0.0 copy-done.3
  12.6 0.0 copy-done.4
  12.6 0.0 copy-done.5
  12.7 0.0 copy-done.6
  12.7 2.3 %tokens.1 = (bf16[8,784,128]{2,1,0:T(8,128)(2,1)}, f32[256,1024]{1,0:T(8,128)S(1)}) custom-call(bf16[8,128,256]{2,1,0:T(8,128)(2,1)S(1)} %copy-done, f32[8,128]{1,0:T(8,128)S(1)} %get-tuple-element.78.ok_ref, bf16[256,256]{1,0:T(8,128)(2,1)S(1)} %copy-done.3, bf16[256,256]{1,0:T(8,128)(2,1)S(1)} %copy-done.4, bf16[256,256]{1,0:T(8,128)(2,1)S(1)} %copy-done.5, ...), custom_call_target="tpu_custom_call" | custom-call | flops 4499999744 | bytes 1024 | tf_op jit(solution)/shard_map/tokens/pallas_call | solution.py:85
  15.0 1.0 copy-done.13
  16.0 6.8 %all-to-all-done = bf16[16,128,128]{2,1,0:T(8,128)(2,1)S(1)} async-done(((bf16[16,128,128]{2,1,0:T(8,128)(2,1)}), bf16[16,128,128]{2,1,0:T(8,128)(2,1)S(1)}, u32[]{:S(2)}, u32[]{:S(2)}) %all-to-all-start) | async-done | bytes 524320 | tf_op jit(solution)/shard_map/all_to_all | solution.py:431
  22.8 4.9 %all-to-all-start.1 = ((bf16[8,784,128]{2,1,0:T(8,128)(2,1)}), bf16[8,784,128]{2,1,0:T(8,128)(2,1)S(1)}, u32[]{:S(2)}, u32[]{:S(2)}) async-start(bf16[8,784,128]{2,1,0:T(8,128)(2,1)} %get-tuple-element.42), calls=%async_computation.1 | async-start | bytes 3211264 | tf_op jit(solution)/shard_map/all_to_all | solution.py:423
  27.7 1.9 %collective-permute-start = (bf16[2,8,128,128]{3,2,1,0:T(8,128)(2,1)S(1)}, bf16[2,8,128,128]{3,2,1,0:T(8,128)(2,1)S(1)}, u32[]{:S(2)}, u32[]{:S(2)}) collective-permute-start(bf16[2,8,128,128]{3,2,1,0:T(8,128)(2,1)S(1)} %bitcast.4), channel_id=1, source_target_pairs={{0,32},{16,48},{32,64},{48,80},{64,96},{80,112},{96,128},{112,144}... | collective-permute-start | bytes 1572872 | tf_op jit(solution)/shard_map/ppermute | solution.py:445
  29.6 3.9 %collective-permute-start.1 = (bf16[2,8,128,128]{3,2,1,0:T(8,128)(2,1)S(1)}, bf16[2,8,128,128]{3,2,1,0:T(8,128)(2,1)}, u32[]{:S(2)}, u32[]{:S(2)}) collective-permute-start(bf16[2,8,128,128]{3,2,1,0:T(8,128)(2,1)S(1)} %bitcast.5), channel_id=1, source_target_pairs={{0,224},{16,240},{32,0},{48,16},{64,32},{80,48},{96,64},{112,80},{... | collective-permute-start | bytes 1572872 | tf_op jit(solution)/shard_map/ppermute | solution.py:445
  33.6 10.3 %collective-permute-done.refs_3_.refs_4_ = bf16[2,8,128,128]{3,2,1,0:T(8,128)(2,1)S(1)} collective-permute-done((bf16[2,8,128,128]{3,2,1,0:T(8,128)(2,1)S(1)}, bf16[2,8,128,128]{3,2,1,0:T(8,128)(2,1)S(1)}, u32[]{:S(2)}, u32[]{:S(2)}) %collective-permute-start) | collective-permute-done | bytes 524320 | tf_op jit(solution)/shard_map/ppermute | solution.py:445
  43.9 0.0 collective-permute-done.1.refs_4_.refs_5_
  43.9 3.3 %all-to-all-done.1.refs_1_ = bf16[8,784,128]{2,1,0:T(8,128)(2,1)S(1)} async-done(((bf16[8,784,128]{2,1,0:T(8,128)(2,1)}), bf16[8,784,128]{2,1,0:T(8,128)(2,1)S(1)}, u32[]{:S(2)}, u32[]{:S(2)}) %all-to-all-start.1) | async-done | bytes 1605664 | tf_op jit(solution)/shard_map/all_to_all | solution.py:423
  47.2 0.0 collective-permute-start.2
  47.2 0.1 pad_add_fusion.refs_0_
  47.3 1.9 %collective-permute-start.3 = (bf16[2,8,128,128]{3,2,1,0:T(8,128)(2,1)S(1)}, bf16[2,8,128,128]{3,2,1,0:T(8,128)(2,1)S(1)}, u32[]{:S(2)}, u32[]{:S(2)}) collective-permute-start(bf16[2,8,128,128]{3,2,1,0:T(8,128)(2,1)S(1)} %collective-permute-done.refs_3_.refs_4_), channel_id=1, source_target_pairs={{0,32},{16,48},{32,64},{48,80},{64,96},{80,112},{96,128},{112,144}... | collective-permute-start | bytes 1572872 | tf_op jit(solution)/shard_map/ppermute | solution.py:445
  49.2 4.0 %collective-permute-start.4 = (bf16[2,8,128,128]{3,2,1,0:T(8,128)(2,1)}, bf16[2,8,128,128]{3,2,1,0:T(8,128)(2,1)S(1)}, u32[]{:S(2)}, u32[]{:S(2)}) collective-permute-start(bf16[2,8,128,128]{3,2,1,0:T(8,128)(2,1)} %collective-permute-done.1.refs_4_.refs_5_), channel_id=1, source_target_pairs={{0,224},{16,240},{32,0},{48,16},{64,32},{80,48},{96,64},{112,80},{... | collective-permute-start | bytes 1572872 | tf_op jit(solution)/shard_map/ppermute | solution.py:445
  53.3 6.2 %attend.5 = (f32[8,1,1024]{2,1,0:T(1,128)S(1)}, f32[8,1,1024]{2,1,0:T(1,128)S(1)}, f32[8,32,1024]{2,1,0:T(8,128)S(1)}) custom-call(s32[2]{0:T(128)S(1)} %pad_add_fusion.refs_0_, bf16[8,784,128]{2,1,0:T(8,128)(2,1)S(1)} %all-to-all-done.1.refs_1_, bf16[2,8,128,128]{3,2,1,0:T(8,128)(2,1)S(1)} %bitcast.6, ...), custom_call_target="tpu_custom_call" | custom-call | flops 5400000000 | bytes 1024 | tf_op jit(solution)/shard_map/attend/pallas_call | solution.py:259
  59.5 0.0 collective-permute-done.2.refs_2_
  59.5 7.7 %attend.6 = (f32[8,1,1024]{2,1,0:T(1,128)S(1)}, f32[8,1,1024]{2,1,0:T(1,128)S(1)}, f32[8,32,1024]{2,1,0:T(8,128)S(1)}, bf16[8,528,128]{2,1,0:T(8,128)(2,1)S(1)}) custom-call(s32[2]{0:T(128)S(1)} %pad_add_fusion.refs_0_, bf16[8,784,128]{2,1,0:T(8,128)(2,1)S(1)} %all-to-all-done.1.refs_1_, bf16[8,784,128]{2,1,0:T(8,128)(2,1)} %collective-permute-done.2.refs_2_, ...), custom_call_target="tpu_custom_call" | custom-call | flops 5400000000 | bytes 1024 | tf_op jit(solution)/shard_map/attend/pallas_call | solution.py:259
  67.2 0.0 collective-permute-done.3.refs_3_
  67.2 0.0 collective-permute-done.4.refs_4_
  67.2 0.3 collective-permute-start.5
  67.5 3.2 %collective-permute-start.6 = (bf16[2,8,128,128]{3,2,1,0:T(8,128)(2,1)S(1)}, bf16[2,8,128,128]{3,2,1,0:T(8,128)(2,1)S(1)}, u32[]{:S(2)}, u32[]{:S(2)}) collective-permute-start(bf16[2,8,128,128]{3,2,1,0:T(8,128)(2,1)S(1)} %collective-permute-done.4.refs_4_), channel_id=1, source_target_pairs={{0,224},{16,240},{32,0},{48,16},{64,32},{80,48},{96,64},{112,80},{... | collective-permute-start | bytes 1572872 | tf_op jit(solution)/shard_map/ppermute | solution.py:445
  70.7 7.2 %attend.7 = (f32[8,1,1024]{2,1,0:T(1,128)S(1)}, f32[8,1,1024]{2,1,0:T(1,128)S(1)}, f32[8,32,1024]{2,1,0:T(8,128)S(1)}) custom-call(s32[2]{0:T(128)S(1)} %pad_add_fusion.refs_0_, bf16[8,784,128]{2,1,0:T(8,128)(2,1)S(1)} %all-to-all-done.1.refs_1_, bf16[8,528,128]{2,1,0:T(8,128)(2,1)S(1)} %get-tuple-element.54.refs_2_, ...), custom_call_target="tpu_custom_call" | custom-call | flops 6300000256 | bytes 1024 | tf_op jit(solution)/shard_map/attend/pallas_call | solution.py:259
  78.0 4.8 %collective-permute-done.5.refs_3_ = bf16[2,8,128,128]{3,2,1,0:T(8,128)(2,1)S(1)} collective-permute-done((bf16[2,8,128,128]{3,2,1,0:T(8,128)(2,1)S(1)}, bf16[2,8,128,128]{3,2,1,0:T(8,128)(2,1)S(1)}, u32[]{:S(2)}, u32[]{:S(2)}) %collective-permute-start.5) | collective-permute-done | bytes 524320 | tf_op jit(solution)/shard_map/ppermute | solution.py:445
  82.8 0.0 collective-permute-done.6.refs_4_
  82.8 0.2 collective-permute-start.7
  83.0 3.2 %collective-permute-start.8 = (bf16[2,4,128,128]{3,2,1,0:T(8,128)(2,1)S(1)}, bf16[2,4,128,128]{3,2,1,0:T(8,128)(2,1)S(1)}, u32[]{:S(2)}, u32[]{:S(2)}) collective-permute-start(bf16[2,4,128,128]{3,2,1,0:T(8,128)(2,1)S(1)} %slice.7), channel_id=1, source_target_pairs={{0,224},{16,240},{32,0},{48,16},{64,32},{80,48},{96,64},{112,80},{... | collective-permute-start | bytes 786440 | tf_op jit(solution)/shard_map/ppermute | solution.py:445
  86.2 7.2 %attend.8 = (f32[8,1,1024]{2,1,0:T(1,128)S(1)}, f32[8,1,1024]{2,1,0:T(1,128)S(1)}, f32[8,32,1024]{2,1,0:T(8,128)S(1)}) custom-call(s32[2]{0:T(128)S(1)} %pad_add_fusion.refs_0_, bf16[8,784,128]{2,1,0:T(8,128)(2,1)S(1)} %all-to-all-done.1.refs_1_, bf16[8,528,128]{2,1,0:T(8,128)(2,1)S(1)} %get-tuple-element.54.refs_2_, ...), custom_call_target="tpu_custom_call" | custom-call | flops 6300000256 | bytes 1024 | tf_op jit(solution)/shard_map/attend/pallas_call | solution.py:259
  93.4 0.0 collective-permute-done.7.refs_3_
  93.4 0.0 collective-permute-done.8.refs_4_
  93.5 4.4 %attend.9 = f32[8,256,128]{2,1,0:T(8,128)S(1)} custom-call(s32[2]{0:T(128)S(1)} %pad_add_fusion.refs_0_, bf16[8,784,128]{2,1,0:T(8,128)(2,1)S(1)} %all-to-all-done.1.refs_1_, bf16[8,528,128]{2,1,0:T(8,128)(2,1)S(1)} %get-tuple-element.54.refs_2_, bf16[2,4,128,128]{3,2,1,0:T(8,128)(2,1)S(1)} %collective-permute-done.7.refs_3_, ...), custom_call_target="tpu_custom_call" | custom-call | flops 3600000000 | bytes 1024 | tf_op jit(solution)/shard_map/attend/pallas_call | solution.py:259
  97.9 0.0 copy-start.7
  97.9 0.0 copy-start.14
  97.9 17.5 %all_to_all.25.o_ref = f32[8,256,128]{2,1,0:T(8,128)S(1)} all-to-all(f32[8,256,128]{2,1,0:T(8,128)S(1)} %attend.9), channel_id=1, replica_groups={{0,2,4,6,8,10,12,14},{1,3,5,7,9,11,13,15},{16,18,20,22,24,26,28,30},{17..., dimensions={0} | all-to-all | bytes 2097152 | tf_op jit(solution)/shard_map/all_to_all | solution.py:423
  115.4 0.0 copy-done.7
  115.4 0.0 copy-done.14
  115.4 0.0 copy-start.10
  115.4 0.0 copy-start.11
  115.5 1.1 row_mix.1
  116.5 24.4 %all_to_all.26.x_ref = bf16[16,72,256]{2,1,0:T(8,128)(2,1)S(1)} all-to-all(bf16[16,72,256]{2,1,0:T(8,128)(2,1)S(1)} %get-tuple-element.75), channel_id=1, replica_groups=mesh['seq'=16,'res'=16] {'seq'}, dimensions={0} | all-to-all | bytes 1179648 | tf_op jit(solution)/shard_map/all_to_all | solution.py:472
  140.9 0.0 copy-done.8
  140.9 0.0 copy-done.9
  140.9 0.0 copy-done.10
  140.9 0.0 copy-done.11
  140.9 0.0 copy-start.1
  141.0 0.0 copy-start.2
  141.0 0.0 copy-start.12
  141.0 4.0 %column.1 = bf16[16,64,256]{2,1,0:T(8,128)(2,1)S(1)} custom-call(bf16[16,72,256]{2,1,0:T(8,128)(2,1)S(1)} %all_to_all.26.x_ref, bf16[256,256]{1,0:T(8,128)(2,1)S(1)} %copy-done.8, bf16[256,256]{1,0:T(8,128)(2,1)S(1)} %copy-done.9, bf16[256,256]{1,0:T(8,128)(2,1)S(1)} %copy-done.10, bf16[256,256]{1,0:T(8,128)(2,1)S(1)} %copy-done.11), custom_call_target="tpu_custom_call" | custom-call | flops 8999999488 | bytes 1024 | tf_op jit(solution)/shard_map/column/pallas_call | solution.py:353
  145.0 19.0 %all_to_all.27.a_ref = bf16[16,64,256]{2,1,0:T(8,128)(2,1)S(1)} all-to-all(bf16[16,64,256]{2,1,0:T(8,128)(2,1)S(1)} %column.1), channel_id=1, replica_groups=mesh['seq'=16,'res'=16] {'seq'}, dimensions={0} | all-to-all | bytes 1048576 | tf_op jit(solution)/shard_map/all_to_all | solution.py:476
  164.0 0.0 copy-done.1
  164.0 0.0 copy-done.2
  164.0 0.0 copy-done.12
  164.0 2.8 %transition.1 = bf16[8,128,256]{2,1,0:T(8,128)(2,1)} custom-call(bf16[16,64,256]{2,1,0:T(8,128)(2,1)S(1)} %all_to_all.27.a_ref, f32[8,128,256]{2,1,0:T(8,128)S(1)} %get-tuple-element.76.m1_ref, bf16[256,256]{1,0:T(8,128)(2,1)S(1)} %copy-done.12, bf16[256,1024]{1,0:T(8,128)(2,1)S(1)} %copy-done.1, bf16[1024,256]{1,0:T(8,128)(2,1)S(1)} %copy-done.2), custom_call_target="tpu_custom_call" | custom-call | flops 5400000000 | bytes 1024 | tf_op jit(solution)/shard_map/transition/pallas_call | solution.py:381
  (9 shorter events, 0.1 us)
Async XLA Ops:
  0.0 12.6 %copy-start.15 = (s32[8,128]{1,0:T(8,128)S(1)}, s32[8,128]{1,0:T(8,128)}, u32[]{:S(2)}) copy-start(s32[8,128]{1,0:T(8,128)} %param.19) | copy-start | bytes 12292
  0.0 12.6 %copy-start.16 = (s32[128]{0:T(128)S(1)}, s32[128]{0:T(128)}, u32[]{:S(2)}) copy-start(s32[128]{0:T(128)} %param.20) | copy-start | bytes 1540
  0.0 12.6 %copy-start = (bf16[8,128,256]{2,1,0:T(8,128)(2,1)S(1)}, bf16[8,128,256]{2,1,0:T(8,128)(2,1)}, u32[]{:S(2)}) copy-start(bf16[8,128,256]{2,1,0:T(8,128)(2,1)} %hp_ref.3) | copy-start | bytes 1572868
  0.0 12.6 %copy-start.3 = (bf16[256,256]{1,0:T(8,128)(2,1)S(1)}, bf16[256,256]{1,0:T(8,128)(2,1)}, u32[]{:S(2)}) copy-start(bf16[256,256]{1,0:T(8,128)(2,1)} %wq_ref.2) | copy-start | bytes 393220
  0.0 12.6 %copy-start.4 = (bf16[256,256]{1,0:T(8,128)(2,1)S(1)}, bf16[256,256]{1,0:T(8,128)(2,1)}, u32[]{:S(2)}) copy-start(bf16[256,256]{1,0:T(8,128)(2,1)} %wk_ref.2) | copy-start | bytes 393220
  0.0 12.6 %copy-start.5 = (bf16[256,256]{1,0:T(8,128)(2,1)S(1)}, bf16[256,256]{1,0:T(8,128)(2,1)}, u32[]{:S(2)}) copy-start(bf16[256,256]{1,0:T(8,128)(2,1)} %wv_ref.2) | copy-start | bytes 393220
  0.0 12.6 %copy-start.6 = (bf16[256,256]{1,0:T(8,128)(2,1)S(1)}, bf16[256,256]{1,0:T(8,128)(2,1)}, u32[]{:S(2)}) copy-start(bf16[256,256]{1,0:T(8,128)(2,1)} %wg_ref.2) | copy-start | bytes 393220
  5.1 17.6 %all-to-all-start = ((bf16[16,128,128]{2,1,0:T(8,128)(2,1)}), bf16[16,128,128]{2,1,0:T(8,128)(2,1)S(1)}, u32[]{:S(2)}, u32[]{:S(2)}) async-start(bf16[16,128,128]{2,1,0:T(8,128)(2,1)} %pair_bias.1), calls=%async_computation | async-start | bytes 1048576 | tf_op jit(solution)/shard_map/all_to_all | solution.py:431
  15.0 1.0 copy-start.13
  22.8 24.5 %all-to-all-start.1 = ((bf16[8,784,128]{2,1,0:T(8,128)(2,1)}), bf16[8,784,128]{2,1,0:T(8,128)(2,1)S(1)}, u32[]{:S(2)}, u32[]{:S(2)}) async-start(bf16[8,784,128]{2,1,0:T(8,128)(2,1)} %get-tuple-element.42), calls=%async_computation.1 | async-start | bytes 3211264 | tf_op jit(solution)/shard_map/all_to_all | solution.py:423
  27.7 16.2 %collective-permute-start = (bf16[2,8,128,128]{3,2,1,0:T(8,128)(2,1)S(1)}, bf16[2,8,128,128]{3,2,1,0:T(8,128)(2,1)S(1)}, u32[]{:S(2)}, u32[]{:S(2)}) collective-permute-start(bf16[2,8,128,128]{3,2,1,0:T(8,128)(2,1)S(1)} %bitcast.4), channel_id=1, source_target_pairs={{0,32},{16,48},{32,64},{48,80},{64,96},{80,112},{96,128},{112,144}... | collective-permute-start | bytes 1572872 | tf_op jit(solution)/shard_map/ppermute | solution.py:445
  29.6 14.3 %collective-permute-start.1 = (bf16[2,8,128,128]{3,2,1,0:T(8,128)(2,1)S(1)}, bf16[2,8,128,128]{3,2,1,0:T(8,128)(2,1)}, u32[]{:S(2)}, u32[]{:S(2)}) collective-permute-start(bf16[2,8,128,128]{3,2,1,0:T(8,128)(2,1)S(1)} %bitcast.5), channel_id=1, source_target_pairs={{0,224},{16,240},{32,0},{48,16},{64,32},{80,48},{96,64},{112,80},{... | collective-permute-start | bytes 1572872 | tf_op jit(solution)/shard_map/ppermute | solution.py:445
  47.2 12.3 %collective-permute-start.2 = (bf16[8,784,128]{2,1,0:T(8,128)(2,1)S(1)}, bf16[8,784,128]{2,1,0:T(8,128)(2,1)}, u32[]{:S(2)}, u32[]{:S(2)}) collective-permute-start(bf16[8,784,128]{2,1,0:T(8,128)(2,1)S(1)} %all-to-all-done.1.refs_1_), channel_id=1, source_target_pairs={{0,1},{1,0},{2,3},{3,2},{4,5},{5,4},{6,7},{7,6},{8,9},{9,8},{10,11... | collective-permute-start | bytes 4816904 | tf_op jit(solution)/shard_map/ppermute | solution.py:457
  47.3 19.9 %collective-permute-start.3 = (bf16[2,8,128,128]{3,2,1,0:T(8,128)(2,1)S(1)}, bf16[2,8,128,128]{3,2,1,0:T(8,128)(2,1)S(1)}, u32[]{:S(2)}, u32[]{:S(2)}) collective-permute-start(bf16[2,8,128,128]{3,2,1,0:T(8,128)(2,1)S(1)} %collective-permute-done.refs_3_.refs_4_), channel_id=1, source_target_pairs={{0,32},{16,48},{32,64},{48,80},{64,96},{80,112},{96,128},{112,144}... | collective-permute-start | bytes 1572872 | tf_op jit(solution)/shard_map/ppermute | solution.py:445
  49.2 18.0 %collective-permute-start.4 = (bf16[2,8,128,128]{3,2,1,0:T(8,128)(2,1)}, bf16[2,8,128,128]{3,2,1,0:T(8,128)(2,1)S(1)}, u32[]{:S(2)}, u32[]{:S(2)}) collective-permute-start(bf16[2,8,128,128]{3,2,1,0:T(8,128)(2,1)} %collective-permute-done.1.refs_4_.refs_5_), channel_id=1, source_target_pairs={{0,224},{16,240},{32,0},{48,16},{64,32},{80,48},{96,64},{112,80},{... | collective-permute-start | bytes 1572872 | tf_op jit(solution)/shard_map/ppermute | solution.py:445
  67.2 15.5 %collective-permute-start.5 = (bf16[2,8,128,128]{3,2,1,0:T(8,128)(2,1)S(1)}, bf16[2,8,128,128]{3,2,1,0:T(8,128)(2,1)S(1)}, u32[]{:S(2)}, u32[]{:S(2)}) collective-permute-start(bf16[2,8,128,128]{3,2,1,0:T(8,128)(2,1)S(1)} %collective-permute-done.3.refs_3_), channel_id=1, source_target_pairs={{0,32},{16,48},{32,64},{48,80},{64,96},{80,112},{96,128},{112,144}... | collective-permute-start | bytes 1572872 | tf_op jit(solution)/shard_map/ppermute | solution.py:445
  67.5 15.3 %collective-permute-start.6 = (bf16[2,8,128,128]{3,2,1,0:T(8,128)(2,1)S(1)}, bf16[2,8,128,128]{3,2,1,0:T(8,128)(2,1)S(1)}, u32[]{:S(2)}, u32[]{:S(2)}) collective-permute-start(bf16[2,8,128,128]{3,2,1,0:T(8,128)(2,1)S(1)} %collective-permute-done.4.refs_4_), channel_id=1, source_target_pairs={{0,224},{16,240},{32,0},{48,16},{64,32},{80,48},{96,64},{112,80},{... | collective-permute-start | bytes 1572872 | tf_op jit(solution)/shard_map/ppermute | solution.py:445
  82.8 10.6 %collective-permute-start.7 = (bf16[2,4,128,128]{3,2,1,0:T(8,128)(2,1)S(1)}, bf16[2,4,128,128]{3,2,1,0:T(8,128)(2,1)S(1)}, u32[]{:S(2)}, u32[]{:S(2)}) collective-permute-start(bf16[2,4,128,128]{3,2,1,0:T(8,128)(2,1)S(1)} %slice.6), channel_id=1, source_target_pairs={{0,32},{16,48},{32,64},{48,80},{64,96},{80,112},{96,128},{112,144}... | collective-permute-start | bytes 786440 | tf_op jit(solution)/shard_map/ppermute | solution.py:445
  83.0 10.5 %collective-permute-start.8 = (bf16[2,4,128,128]{3,2,1,0:T(8,128)(2,1)S(1)}, bf16[2,4,128,128]{3,2,1,0:T(8,128)(2,1)S(1)}, u32[]{:S(2)}, u32[]{:S(2)}) collective-permute-start(bf16[2,4,128,128]{3,2,1,0:T(8,128)(2,1)S(1)} %slice.7), channel_id=1, source_target_pairs={{0,224},{16,240},{32,0},{48,16},{64,32},{80,48},{96,64},{112,80},{... | collective-permute-start | bytes 786440 | tf_op jit(solution)/shard_map/ppermute | solution.py:445
  97.9 17.5 %copy-start.7 = (bf16[256,256]{1,0:T(8,128)(2,1)S(1)}, bf16[256,256]{1,0:T(8,128)(2,1)}, u32[]{:S(2)}) copy-start(bf16[256,256]{1,0:T(8,128)(2,1)} %wf_ref.2) | copy-start | bytes 393220
  97.9 17.5 %copy-start.14 = (f32[256,1024]{1,0:T(8,128)S(1)}, f32[256,1024]{1,0:T(8,128)}, u32[]{:S(2)}) copy-start(f32[256,1024]{1,0:T(8,128)} %copy-done.13) | copy-start | bytes 3145732
  115.4 25.5 %copy-start.8 = (bf16[256,256]{1,0:T(8,128)(2,1)S(1)}, bf16[256,256]{1,0:T(8,128)(2,1)}, u32[]{:S(2)}) copy-start(bf16[256,256]{1,0:T(8,128)(2,1)} %wq_ref.3) | copy-start | bytes 393220
  115.4 25.5 %copy-start.9 = (bf16[256,256]{1,0:T(8,128)(2,1)S(1)}, bf16[256,256]{1,0:T(8,128)(2,1)}, u32[]{:S(2)}) copy-start(bf16[256,256]{1,0:T(8,128)(2,1)} %wk_ref.3) | copy-start | bytes 393220
  115.4 25.5 %copy-start.10 = (bf16[256,256]{1,0:T(8,128)(2,1)S(1)}, bf16[256,256]{1,0:T(8,128)(2,1)}, u32[]{:S(2)}) copy-start(bf16[256,256]{1,0:T(8,128)(2,1)} %wv_ref.3) | copy-start | bytes 393220
  115.4 25.5 %copy-start.11 = (bf16[256,256]{1,0:T(8,128)(2,1)S(1)}, bf16[256,256]{1,0:T(8,128)(2,1)}, u32[]{:S(2)}) copy-start(bf16[256,256]{1,0:T(8,128)(2,1)} %wg_ref.3) | copy-start | bytes 393220
  140.9 23.0 %copy-start.1 = (bf16[256,1024]{1,0:T(8,128)(2,1)S(1)}, bf16[256,1024]{1,0:T(8,128)(2,1)}, u32[]{:S(2)}) copy-start(bf16[256,1024]{1,0:T(8,128)(2,1)} %ww_ref.1) | copy-start | bytes 1572868
  141.0 23.0 %copy-start.2 = (bf16[1024,256]{1,0:T(8,128)(2,1)S(1)}, bf16[1024,256]{1,0:T(8,128)(2,1)}, u32[]{:S(2)}) copy-start(bf16[1024,256]{1,0:T(8,128)(2,1)} %wn_ref.1) | copy-start | bytes 1572868
  141.0 23.0 %copy-start.12 = (bf16[256,256]{1,0:T(8,128)(2,1)S(1)}, bf16[256,256]{1,0:T(8,128)(2,1)}, u32[]{:S(2)}) copy-start(bf16[256,256]{1,0:T(8,128)(2,1)} %wf_ref.3) | copy-start | bytes 393220

commit v4 on v3

--- a/solution.py
+++ b/solution.py
@@ -362,19 +362,32 @@
     )(x, wq, wk, wv, wg)
 
 
-def final_kernel(a_ref, m1_ref, wf_ref, ww_ref, wn_ref, out_ref):
+def final_kernel(a_ref, m1_ref, wf_ref, ww_ref, wn_ref, out_ref, done, sems):
     a = a_ref[...].astype(F32)
     wf = wf_ref[...]
     ww = ww_ref[...]
     wn = wn_ref[...]
-    for p in range(2):
+
+    def front(p):
         a2 = jnp.concatenate(
-            [a[:, s * 8 : (s + 1) * 8, :].reshape(128, 256) for s in range(p * 4, p * 4 + 4)], 0
+            [a[:, s * 8 : (s + 1) * 8, :].reshape(128, 256) for s in (p * 2, p * 2 + 1)], 0
         ).astype(BF16)
-        m2 = m1_ref[p * 4 : p * 4 + 4].reshape(512, 256) + dot_nn(a2, wf)
-        x3 = standardize(m2).astype(BF16)
+        m2 = m1_ref[p * 2 : p * 2 + 2].reshape(256, 256) + dot_nn(a2, wf)
+        return m2, standardize(m2).astype(BF16)
+
+    copies = []
+    m2, x3 = front(0)
+    for p in range(4):
+        upcoming = front(p + 1) if p < 3 else (None, None)
         hid = jnp.maximum(dot_nn(x3, ww), 0.0).astype(BF16)
-        out_ref[p * 4 : p * 4 + 4] = (m2 + dot_nn(hid, wn)).astype(BF16).reshape(4, 128, 256)
+        done[p * 2 : p * 2 + 2] = (m2 + dot_nn(hid, wn)).astype(BF16).reshape(2, 128, 256)
+        copies.append(
+            pltpu.make_async_copy(done.at[pl.ds(p * 2, 2)], out_ref.at[pl.ds(p * 2, 2)], sems.at[p])
+        )
+        copies[-1].start()
+        m2, x3 = upcoming
+    for copy in copies:
+        copy.wait()
 
 
 def final_call(a, m1, wf, ww, wn):
@@ -382,9 +395,10 @@
         final_kernel,
         out_shape=jax.ShapeDtypeStruct((8, 128, 256), BF16),
         in_specs=[whole()] * 5,
-        out_specs=whole(),
+        out_specs=pl.BlockSpec(memory_space=pl.ANY),
+        scratch_shapes=[pltpu.VMEM((8, 128, 256), BF16), pltpu.SemaphoreType.DMA((4,))],
         compiler_params=params(),
-        cost_estimate=cost(6),
+        cost_estimate=cost(4),
         name="transition",
     )(a, m1, wf, ww, wn)
 

time: 167 us -> 167 us (level)
  no operation moved by 1% of the time
where the time goes in v4:
time: 167 us
  blocking collectives  60.9 us (36%)
  Pallas kernels  47.7 us (29%)
  starting transfers between devices  31.1 us (19%)
  waiting for transfers between devices  25.2 us (15%)
    pallas_call x5, Pallas kernels, attend_call(): pl.pallas_call(functools.partial(attend_kernel, 512, unroll, len(biases),...  32.8 us
    all_to_all x1, blocking collectives, on_device(): x2 = lax.all_to_all(x2, 'seq', 0, 0, tiled=True)  24.4 us
    all_to_all x1, blocking collectives, on_device(): a2 = lax.all_to_all(a2, 'seq', 0, 0, tiled=True)  19 us
    all_to_all x1, blocking collectives, to_heads(): lax.all_to_all(x, 'res', 0, 0, axis_index_groups=same_core, tiled=True)  17.5 us
    ppermute x4, waiting for transfers between devices, ring(): lax.ppermute(right, 'seq', to_right)  15.1 us
    ppermute x4, starting transfers between devices, ring(): lax.ppermute(left, 'seq', to_left)  14.4 us
    all_to_all x1, starting transfers between devices, on_device(): lax.all_to_all(bias, ('seq', 'res'), 0, 0, axis_index_groups=wide_groups,...  7.48 us
    all_to_all x1, waiting for transfers between devices, on_device(): lax.all_to_all(bias, ('seq', 'res'), 0, 0, axis_index_groups=wide_groups,...  6.8 us
  transfers between devices with their start and end apart: 11, of which 4 were waited for; matrix products, arithmetic and copies ran while one was open for 0% of the time, Pallas kernels for 18%

profile of v4, /device:TPU:2, one launch (start us, length us, event | category | flops | bytes accessed | tf_op | source)
XLA Modules:
  0.0 166.7 jit_solution(6718590295441839400)
XLA Ops:
  0.0 0.0 copy-start.3
  0.0 0.0 copy-start.4
  0.0 0.0 copy-start.5
  0.0 0.0 copy-start.6
  0.0 5.1 %pair_bias.1 = bf16[16,128,128]{2,1,0:T(8,128)(2,1)} custom-call(bf16[128,128,128]{2,1,0:T(8,128)(2,1)} %z_ref.1, bf16[8,128]{1,0:T(8,128)(2,1)} %bitcast.8), custom_call_target="tpu_custom_call" | custom-call | flops 5400000000 | bytes 1024 | tf_op jit(solution)/shard_map/pair_bias/pallas_call | solution.py:125
  5.1 7.5 %all-to-all-start = ((bf16[16,128,128]{2,1,0:T(8,128)(2,1)}), bf16[16,128,128]{2,1,0:T(8,128)(2,1)S(1)}, u32[]{:S(2)}, u32[]{:S(2)}) async-start(bf16[16,128,128]{2,1,0:T(8,128)(2,1)} %pair_bias.1), calls=%async_computation | async-start | bytes 1048576 | tf_op jit(solution)/shard_map/all_to_all | solution.py:445
  12.6 0.0 copy-done.15
  12.6 0.0 copy-done.16
  12.6 0.0 copy-done
  12.6 0.0 copy-done.3
  12.6 0.0 copy-done.4
  12.6 0.0 copy-done.5
  12.7 0.0 copy-done.6
  12.7 2.3 %tokens.1 = (bf16[8,784,128]{2,1,0:T(8,128)(2,1)}, f32[256,1024]{1,0:T(8,128)S(1)}) custom-call(bf16[8,128,256]{2,1,0:T(8,128)(2,1)S(1)} %copy-done, f32[8,128]{1,0:T(8,128)S(1)} %get-tuple-element.78.ok_ref, bf16[256,256]{1,0:T(8,128)(2,1)S(1)} %copy-done.3, bf16[256,256]{1,0:T(8,128)(2,1)S(1)} %copy-done.4, bf16[256,256]{1,0:T(8,128)(2,1)S(1)} %copy-done.5, ...), custom_call_target="tpu_custom_call" | custom-call | flops 4499999744 | bytes 1024 | tf_op jit(solution)/shard_map/tokens/pallas_call | solution.py:85
  15.0 1.0 copy-done.13
  16.0 6.8 %all-to-all-done = bf16[16,128,128]{2,1,0:T(8,128)(2,1)S(1)} async-done(((bf16[16,128,128]{2,1,0:T(8,128)(2,1)}), bf16[16,128,128]{2,1,0:T(8,128)(2,1)S(1)}, u32[]{:S(2)}, u32[]{:S(2)}) %all-to-all-start) | async-done | bytes 524320 | tf_op jit(solution)/shard_map/all_to_all | solution.py:445
  22.8 4.9 %all-to-all-start.1 = ((bf16[8,784,128]{2,1,0:T(8,128)(2,1)}), bf16[8,784,128]{2,1,0:T(8,128)(2,1)S(1)}, u32[]{:S(2)}, u32[]{:S(2)}) async-start(bf16[8,784,128]{2,1,0:T(8,128)(2,1)} %get-tuple-element.42), calls=%async_computation.1 | async-start | bytes 3211264 | tf_op jit(solution)/shard_map/all_to_all | solution.py:437
  27.7 1.9 %collective-permute-start = (bf16[2,8,128,128]{3,2,1,0:T(8,128)(2,1)S(1)}, bf16[2,8,128,128]{3,2,1,0:T(8,128)(2,1)S(1)}, u32[]{:S(2)}, u32[]{:S(2)}) collective-permute-start(bf16[2,8,128,128]{3,2,1,0:T(8,128)(2,1)S(1)} %bitcast.4), channel_id=1, source_target_pairs={{0,32},{16,48},{32,64},{48,80},{64,96},{80,112},{96,128},{112,144}... | collective-permute-start | bytes 1572872 | tf_op jit(solution)/shard_map/ppermute | solution.py:459
  29.6 3.9 %collective-permute-start.1 = (bf16[2,8,128,128]{3,2,1,0:T(8,128)(2,1)S(1)}, bf16[2,8,128,128]{3,2,1,0:T(8,128)(2,1)}, u32[]{:S(2)}, u32[]{:S(2)}) collective-permute-start(bf16[2,8,128,128]{3,2,1,0:T(8,128)(2,1)S(1)} %bitcast.5), channel_id=1, source_target_pairs={{0,224},{16,240},{32,0},{48,16},{64,32},{80,48},{96,64},{112,80},{... | collective-permute-start | bytes 1572872 | tf_op jit(solution)/shard_map/ppermute | solution.py:459
  33.6 10.3 %collective-permute-done.refs_3_.refs_4_ = bf16[2,8,128,128]{3,2,1,0:T(8,128)(2,1)S(1)} collective-permute-done((bf16[2,8,128,128]{3,2,1,0:T(8,128)(2,1)S(1)}, bf16[2,8,128,128]{3,2,1,0:T(8,128)(2,1)S(1)}, u32[]{:S(2)}, u32[]{:S(2)}) %collective-permute-start) | collective-permute-done | bytes 524320 | tf_op jit(solution)/shard_map/ppermute | solution.py:459
  43.9 0.0 collective-permute-done.1.refs_4_.refs_5_
  43.9 3.3 %all-to-all-done.1.refs_1_ = bf16[8,784,128]{2,1,0:T(8,128)(2,1)S(1)} async-done(((bf16[8,784,128]{2,1,0:T(8,128)(2,1)}), bf16[8,784,128]{2,1,0:T(8,128)(2,1)S(1)}, u32[]{:S(2)}, u32[]{:S(2)}) %all-to-all-start.1) | async-done | bytes 1605664 | tf_op jit(solution)/shard_map/all_to_all | solution.py:437
  47.2 0.0 collective-permute-start.2
  47.2 0.1 pad_add_fusion.refs_0_
  47.3 1.9 %collective-permute-start.3 = (bf16[2,8,128,128]{3,2,1,0:T(8,128)(2,1)S(1)}, bf16[2,8,128,128]{3,2,1,0:T(8,128)(2,1)S(1)}, u32[]{:S(2)}, u32[]{:S(2)}) collective-permute-start(bf16[2,8,128,128]{3,2,1,0:T(8,128)(2,1)S(1)} %collective-permute-done.refs_3_.refs_4_), channel_id=1, source_target_pairs={{0,32},{16,48},{32,64},{48,80},{64,96},{80,112},{96,128},{112,144}... | collective-permute-start | bytes 1572872 | tf_op jit(solution)/shard_map/ppermute | solution.py:459
  49.2 4.0 %collective-permute-start.4 = (bf16[2,8,128,128]{3,2,1,0:T(8,128)(2,1)}, bf16[2,8,128,128]{3,2,1,0:T(8,128)(2,1)S(1)}, u32[]{:S(2)}, u32[]{:S(2)}) collective-permute-start(bf16[2,8,128,128]{3,2,1,0:T(8,128)(2,1)} %collective-permute-done.1.refs_4_.refs_5_), channel_id=1, source_target_pairs={{0,224},{16,240},{32,0},{48,16},{64,32},{80,48},{96,64},{112,80},{... | collective-permute-start | bytes 1572872 | tf_op jit(solution)/shard_map/ppermute | solution.py:459
  53.3 6.2 %attend.5 = (f32[8,1,1024]{2,1,0:T(1,128)S(1)}, f32[8,1,1024]{2,1,0:T(1,128)S(1)}, f32[8,32,1024]{2,1,0:T(8,128)S(1)}) custom-call(s32[2]{0:T(128)S(1)} %pad_add_fusion.refs_0_, bf16[8,784,128]{2,1,0:T(8,128)(2,1)S(1)} %all-to-all-done.1.refs_1_, bf16[2,8,128,128]{3,2,1,0:T(8,128)(2,1)S(1)} %bitcast.6, ...), custom_call_target="tpu_custom_call" | custom-call | flops 5400000000 | bytes 1024 | tf_op jit(solution)/shard_map/attend/pallas_call | solution.py:259
  59.5 0.0 collective-permute-done.2.refs_2_
  59.5 7.7 %attend.6 = (f32[8,1,1024]{2,1,0:T(1,128)S(1)}, f32[8,1,1024]{2,1,0:T(1,128)S(1)}, f32[8,32,1024]{2,1,0:T(8,128)S(1)}, bf16[8,528,128]{2,1,0:T(8,128)(2,1)S(1)}) custom-call(s32[2]{0:T(128)S(1)} %pad_add_fusion.refs_0_, bf16[8,784,128]{2,1,0:T(8,128)(2,1)S(1)} %all-to-all-done.1.refs_1_, bf16[8,784,128]{2,1,0:T(8,128)(2,1)} %collective-permute-done.2.refs_2_, ...), custom_call_target="tpu_custom_call" | custom-call | flops 5400000000 | bytes 1024 | tf_op jit(solution)/shard_map/attend/pallas_call | solution.py:259
  67.2 0.0 collective-permute-done.3.refs_3_
  67.2 0.0 collective-permute-done.4.refs_4_
  67.2 0.3 collective-permute-start.5
  67.5 3.2 %collective-permute-start.6 = (bf16[2,8,128,128]{3,2,1,0:T(8,128)(2,1)S(1)}, bf16[2,8,128,128]{3,2,1,0:T(8,128)(2,1)S(1)}, u32[]{:S(2)}, u32[]{:S(2)}) collective-permute-start(bf16[2,8,128,128]{3,2,1,0:T(8,128)(2,1)S(1)} %collective-permute-done.4.refs_4_), channel_id=1, source_target_pairs={{0,224},{16,240},{32,0},{48,16},{64,32},{80,48},{96,64},{112,80},{... | collective-permute-start | bytes 1572872 | tf_op jit(solution)/shard_map/ppermute | solution.py:459
  70.7 7.2 %attend.7 = (f32[8,1,1024]{2,1,0:T(1,128)S(1)}, f32[8,1,1024]{2,1,0:T(1,128)S(1)}, f32[8,32,1024]{2,1,0:T(8,128)S(1)}) custom-call(s32[2]{0:T(128)S(1)} %pad_add_fusion.refs_0_, bf16[8,784,128]{2,1,0:T(8,128)(2,1)S(1)} %all-to-all-done.1.refs_1_, bf16[8,528,128]{2,1,0:T(8,128)(2,1)S(1)} %get-tuple-element.54.refs_2_, ...), custom_call_target="tpu_custom_call" | custom-call | flops 6300000256 | bytes 1024 | tf_op jit(solution)/shard_map/attend/pallas_call | solution.py:259
  78.0 4.8 %collective-permute-done.5.refs_3_ = bf16[2,8,128,128]{3,2,1,0:T(8,128)(2,1)S(1)} collective-permute-done((bf16[2,8,128,128]{3,2,1,0:T(8,128)(2,1)S(1)}, bf16[2,8,128,128]{3,2,1,0:T(8,128)(2,1)S(1)}, u32[]{:S(2)}, u32[]{:S(2)}) %collective-permute-start.5) | collective-permute-done | bytes 524320 | tf_op jit(solution)/shard_map/ppermute | solution.py:459
  82.8 0.0 collective-permute-done.6.refs_4_
  82.8 0.2 collective-permute-start.7
  83.0 3.2 %collective-permute-start.8 = (bf16[2,4,128,128]{3,2,1,0:T(8,128)(2,1)S(1)}, bf16[2,4,128,128]{3,2,1,0:T(8,128)(2,1)S(1)}, u32[]{:S(2)}, u32[]{:S(2)}) collective-permute-start(bf16[2,4,128,128]{3,2,1,0:T(8,128)(2,1)S(1)} %slice.7), channel_id=1, source_target_pairs={{0,224},{16,240},{32,0},{48,16},{64,32},{80,48},{96,64},{112,80},{... | collective-permute-start | bytes 786440 | tf_op jit(solution)/shard_map/ppermute | solution.py:459
  86.2 7.2 %attend.8 = (f32[8,1,1024]{2,1,0:T(1,128)S(1)}, f32[8,1,1024]{2,1,0:T(1,128)S(1)}, f32[8,32,1024]{2,1,0:T(8,128)S(1)}) custom-call(s32[2]{0:T(128)S(1)} %pad_add_fusion.refs_0_, bf16[8,784,128]{2,1,0:T(8,128)(2,1)S(1)} %all-to-all-done.1.refs_1_, bf16[8,528,128]{2,1,0:T(8,128)(2,1)S(1)} %get-tuple-element.54.refs_2_, ...), custom_call_target="tpu_custom_call" | custom-call | flops 6300000256 | bytes 1024 | tf_op jit(solution)/shard_map/attend/pallas_call | solution.py:259
  93.4 0.0 collective-permute-done.7.refs_3_
  93.4 0.0 collective-permute-done.8.refs_4_
  93.5 4.4 %attend.9 = f32[8,256,128]{2,1,0:T(8,128)S(1)} custom-call(s32[2]{0:T(128)S(1)} %pad_add_fusion.refs_0_, bf16[8,784,128]{2,1,0:T(8,128)(2,1)S(1)} %all-to-all-done.1.refs_1_, bf16[8,528,128]{2,1,0:T(8,128)(2,1)S(1)} %get-tuple-element.54.refs_2_, bf16[2,4,128,128]{3,2,1,0:T(8,128)(2,1)S(1)} %collective-permute-done.7.refs_3_, ...), custom_call_target="tpu_custom_call" | custom-call | flops 3600000000 | bytes 1024 | tf_op jit(solution)/shard_map/attend/pallas_call | solution.py:259
  97.9 0.0 copy-start.7
  97.9 0.0 copy-start.14
  97.9 17.5 %all_to_all.25.o_ref = f32[8,256,128]{2,1,0:T(8,128)S(1)} all-to-all(f32[8,256,128]{2,1,0:T(8,128)S(1)} %attend.9), channel_id=1, replica_groups={{0,2,4,6,8,10,12,14},{1,3,5,7,9,11,13,15},{16,18,20,22,24,26,28,30},{17..., dimensions={0} | all-to-all | bytes 2097152 | tf_op jit(solution)/shard_map/all_to_all | solution.py:437
  115.4 0.0 copy-done.7
  115.4 0.0 copy-done.14
  115.4 0.0 copy-start.10
  115.4 0.0 copy-start.11
  115.5 1.1 row_mix.1
  116.5 24.4 %all_to_all.26.x_ref = bf16[16,72,256]{2,1,0:T(8,128)(2,1)S(1)} all-to-all(bf16[16,72,256]{2,1,0:T(8,128)(2,1)S(1)} %get-tuple-element.75), channel_id=1, replica_groups=mesh['seq'=16,'res'=16] {'seq'}, dimensions={0} | all-to-all | bytes 1179648 | tf_op jit(solution)/shard_map/all_to_all | solution.py:486
  140.9 0.0 copy-done.8
  140.9 0.0 copy-done.9
  140.9 0.0 copy-done.10
  140.9 0.0 copy-done.11
  140.9 0.0 copy-start.1
  141.0 0.0 copy-start.2
  141.0 0.0 copy-start.12
  141.0 4.0 %column.1 = bf16[16,64,256]{2,1,0:T(8,128)(2,1)S(1)} custom-call(bf16[16,72,256]{2,1,0:T(8,128)(2,1)S(1)} %all_to_all.26.x_ref, bf16[256,256]{1,0:T(8,128)(2,1)S(1)} %copy-done.8, bf16[256,256]{1,0:T(8,128)(2,1)S(1)} %copy-done.9, bf16[256,256]{1,0:T(8,128)(2,1)S(1)} %copy-done.10, bf16[256,256]{1,0:T(8,128)(2,1)S(1)} %copy-done.11), custom_call_target="tpu_custom_call" | custom-call | flops 8999999488 | bytes 1024 | tf_op jit(solution)/shard_map/column/pallas_call | solution.py:353
  145.0 19.0 %all_to_all.27.a_ref = bf16[16,64,256]{2,1,0:T(8,128)(2,1)S(1)} all-to-all(bf16[16,64,256]{2,1,0:T(8,128)(2,1)S(1)} %column.1), channel_id=1, replica_groups=mesh['seq'=16,'res'=16] {'seq'}, dimensions={0} | all-to-all | bytes 1048576 | tf_op jit(solution)/shard_map/all_to_all | solution.py:490
  164.0 0.0 copy-done.1
  164.0 0.0 copy-done.2
  164.0 0.0 copy-done.12
  164.0 2.5 %transition.1 = bf16[8,128,256]{2,1,0:T(8,128)(2,1)} custom-call(bf16[16,64,256]{2,1,0:T(8,128)(2,1)S(1)} %all_to_all.27.a_ref, f32[8,128,256]{2,1,0:T(8,128)S(1)} %get-tuple-element.76.m1_ref, bf16[256,256]{1,0:T(8,128)(2,1)S(1)} %copy-done.12, bf16[256,1024]{1,0:T(8,128)(2,1)S(1)} %copy-done.1, bf16[1024,256]{1,0:T(8,128)(2,1)S(1)} %copy-done.2), custom_call_target="tpu_custom_call" | custom-call | flops 3600000000 | bytes 1024 | tf_op jit(solution)/shard_map/transition/pallas_call | solution.py:394
  (9 shorter events, 0.1 us)
Async XLA Ops:
  0.0 12.6 %copy-start.15 = (s32[8,128]{1,0:T(8,128)S(1)}, s32[8,128]{1,0:T(8,128)}, u32[]{:S(2)}) copy-start(s32[8,128]{1,0:T(8,128)} %param.19) | copy-start | bytes 12292
  0.0 12.6 %copy-start.16 = (s32[128]{0:T(128)S(1)}, s32[128]{0:T(128)}, u32[]{:S(2)}) copy-start(s32[128]{0:T(128)} %param.20) | copy-start | bytes 1540
  0.0 12.6 %copy-start = (bf16[8,128,256]{2,1,0:T(8,128)(2,1)S(1)}, bf16[8,128,256]{2,1,0:T(8,128)(2,1)}, u32[]{:S(2)}) copy-start(bf16[8,128,256]{2,1,0:T(8,128)(2,1)} %hp_ref.3) | copy-start | bytes 1572868
  0.0 12.6 %copy-start.3 = (bf16[256,256]{1,0:T(8,128)(2,1)S(1)}, bf16[256,256]{1,0:T(8,128)(2,1)}, u32[]{:S(2)}) copy-start(bf16[256,256]{1,0:T(8,128)(2,1)} %wq_ref.2) | copy-start | bytes 393220
  0.0 12.6 %copy-start.4 = (bf16[256,256]{1,0:T(8,128)(2,1)S(1)}, bf16[256,256]{1,0:T(8,128)(2,1)}, u32[]{:S(2)}) copy-start(bf16[256,256]{1,0:T(8,128)(2,1)} %wk_ref.2) | copy-start | bytes 393220
  0.0 12.6 %copy-start.5 = (bf16[256,256]{1,0:T(8,128)(2,1)S(1)}, bf16[256,256]{1,0:T(8,128)(2,1)}, u32[]{:S(2)}) copy-start(bf16[256,256]{1,0:T(8,128)(2,1)} %wv_ref.2) | copy-start | bytes 393220
  0.0 12.6 %copy-start.6 = (bf16[256,256]{1,0:T(8,128)(2,1)S(1)}, bf16[256,256]{1,0:T(8,128)(2,1)}, u32[]{:S(2)}) copy-start(bf16[256,256]{1,0:T(8,128)(2,1)} %wg_ref.2) | copy-start | bytes 393220
  5.1 17.6 %all-to-all-start = ((bf16[16,128,128]{2,1,0:T(8,128)(2,1)}), bf16[16,128,128]{2,1,0:T(8,128)(2,1)S(1)}, u32[]{:S(2)}, u32[]{:S(2)}) async-start(bf16[16,128,128]{2,1,0:T(8,128)(2,1)} %pair_bias.1), calls=%async_computation | async-start | bytes 1048576 | tf_op jit(solution)/shard_map/all_to_all | solution.py:445
  15.0 1.0 copy-start.13
  22.8 24.5 %all-to-all-start.1 = ((bf16[8,784,128]{2,1,0:T(8,128)(2,1)}), bf16[8,784,128]{2,1,0:T(8,128)(2,1)S(1)}, u32[]{:S(2)}, u32[]{:S(2)}) async-start(bf16[8,784,128]{2,1,0:T(8,128)(2,1)} %get-tuple-element.42), calls=%async_computation.1 | async-start | bytes 3211264 | tf_op jit(solution)/shard_map/all_to_all | solution.py:437
  27.7 16.2 %collective-permute-start = (bf16[2,8,128,128]{3,2,1,0:T(8,128)(2,1)S(1)}, bf16[2,8,128,128]{3,2,1,0:T(8,128)(2,1)S(1)}, u32[]{:S(2)}, u32[]{:S(2)}) collective-permute-start(bf16[2,8,128,128]{3,2,1,0:T(8,128)(2,1)S(1)} %bitcast.4), channel_id=1, source_target_pairs={{0,32},{16,48},{32,64},{48,80},{64,96},{80,112},{96,128},{112,144}... | collective-permute-start | bytes 1572872 | tf_op jit(solution)/shard_map/ppermute | solution.py:459
  29.6 14.3 %collective-permute-start.1 = (bf16[2,8,128,128]{3,2,1,0:T(8,128)(2,1)S(1)}, bf16[2,8,128,128]{3,2,1,0:T(8,128)(2,1)}, u32[]{:S(2)}, u32[]{:S(2)}) collective-permute-start(bf16[2,8,128,128]{3,2,1,0:T(8,128)(2,1)S(1)} %bitcast.5), channel_id=1, source_target_pairs={{0,224},{16,240},{32,0},{48,16},{64,32},{80,48},{96,64},{112,80},{... | collective-permute-start | bytes 1572872 | tf_op jit(solution)/shard_map/ppermute | solution.py:459
  47.2 12.3 %collective-permute-start.2 = (bf16[8,784,128]{2,1,0:T(8,128)(2,1)S(1)}, bf16[8,784,128]{2,1,0:T(8,128)(2,1)}, u32[]{:S(2)}, u32[]{:S(2)}) collective-permute-start(bf16[8,784,128]{2,1,0:T(8,128)(2,1)S(1)} %all-to-all-done.1.refs_1_), channel_id=1, source_target_pairs={{0,1},{1,0},{2,3},{3,2},{4,5},{5,4},{6,7},{7,6},{8,9},{9,8},{10,11... | collective-permute-start | bytes 4816904 | tf_op jit(solution)/shard_map/ppermute | solution.py:471
  47.3 19.9 %collective-permute-start.3 = (bf16[2,8,128,128]{3,2,1,0:T(8,128)(2,1)S(1)}, bf16[2,8,128,128]{3,2,1,0:T(8,128)(2,1)S(1)}, u32[]{:S(2)}, u32[]{:S(2)}) collective-permute-start(bf16[2,8,128,128]{3,2,1,0:T(8,128)(2,1)S(1)} %collective-permute-done.refs_3_.refs_4_), channel_id=1, source_target_pairs={{0,32},{16,48},{32,64},{48,80},{64,96},{80,112},{96,128},{112,144}... | collective-permute-start | bytes 1572872 | tf_op jit(solution)/shard_map/ppermute | solution.py:459
  49.2 18.0 %collective-permute-start.4 = (bf16[2,8,128,128]{3,2,1,0:T(8,128)(2,1)}, bf16[2,8,128,128]{3,2,1,0:T(8,128)(2,1)S(1)}, u32[]{:S(2)}, u32[]{:S(2)}) collective-permute-start(bf16[2,8,128,128]{3,2,1,0:T(8,128)(2,1)} %collective-permute-done.1.refs_4_.refs_5_), channel_id=1, source_target_pairs={{0,224},{16,240},{32,0},{48,16},{64,32},{80,48},{96,64},{112,80},{... | collective-permute-start | bytes 1572872 | tf_op jit(solution)/shard_map/ppermute | solution.py:459
  67.2 15.5 %collective-permute-start.5 = (bf16[2,8,128,128]{3,2,1,0:T(8,128)(2,1)S(1)}, bf16[2,8,128,128]{3,2,1,0:T(8,128)(2,1)S(1)}, u32[]{:S(2)}, u32[]{:S(2)}) collective-permute-start(bf16[2,8,128,128]{3,2,1,0:T(8,128)(2,1)S(1)} %collective-permute-done.3.refs_3_), channel_id=1, source_target_pairs={{0,32},{16,48},{32,64},{48,80},{64,96},{80,112},{96,128},{112,144}... | collective-permute-start | bytes 1572872 | tf_op jit(solution)/shard_map/ppermute | solution.py:459
  67.5 15.3 %collective-permute-start.6 = (bf16[2,8,128,128]{3,2,1,0:T(8,128)(2,1)S(1)}, bf16[2,8,128,128]{3,2,1,0:T(8,128)(2,1)S(1)}, u32[]{:S(2)}, u32[]{:S(2)}) collective-permute-start(bf16[2,8,128,128]{3,2,1,0:T(8,128)(2,1)S(1)} %collective-permute-done.4.refs_4_), channel_id=1, source_target_pairs={{0,224},{16,240},{32,0},{48,16},{64,32},{80,48},{96,64},{112,80},{... | collective-permute-start | bytes 1572872 | tf_op jit(solution)/shard_map/ppermute | solution.py:459
  82.8 10.6 %collective-permute-start.7 = (bf16[2,4,128,128]{3,2,1,0:T(8,128)(2,1)S(1)}, bf16[2,4,128,128]{3,2,1,0:T(8,128)(2,1)S(1)}, u32[]{:S(2)}, u32[]{:S(2)}) collective-permute-start(bf16[2,4,128,128]{3,2,1,0:T(8,128)(2,1)S(1)} %slice.6), channel_id=1, source_target_pairs={{0,32},{16,48},{32,64},{48,80},{64,96},{80,112},{96,128},{112,144}... | collective-permute-start | bytes 786440 | tf_op jit(solution)/shard_map/ppermute | solution.py:459
  83.0 10.5 %collective-permute-start.8 = (bf16[2,4,128,128]{3,2,1,0:T(8,128)(2,1)S(1)}, bf16[2,4,128,128]{3,2,1,0:T(8,128)(2,1)S(1)}, u32[]{:S(2)}, u32[]{:S(2)}) collective-permute-start(bf16[2,4,128,128]{3,2,1,0:T(8,128)(2,1)S(1)} %slice.7), channel_id=1, source_target_pairs={{0,224},{16,240},{32,0},{48,16},{64,32},{80,48},{96,64},{112,80},{... | collective-permute-start | bytes 786440 | tf_op jit(solution)/shard_map/ppermute | solution.py:459
  97.9 17.5 %copy-start.7 = (bf16[256,256]{1,0:T(8,128)(2,1)S(1)}, bf16[256,256]{1,0:T(8,128)(2,1)}, u32[]{:S(2)}) copy-start(bf16[256,256]{1,0:T(8,128)(2,1)} %wf_ref.2) | copy-start | bytes 393220
  97.9 17.5 %copy-start.14 = (f32[256,1024]{1,0:T(8,128)S(1)}, f32[256,1024]{1,0:T(8,128)}, u32[]{:S(2)}) copy-start(f32[256,1024]{1,0:T(8,128)} %copy-done.13) | copy-start | bytes 3145732
  115.4 25.5 %copy-start.8 = (bf16[256,256]{1,0:T(8,128)(2,1)S(1)}, bf16[256,256]{1,0:T(8,128)(2,1)}, u32[]{:S(2)}) copy-start(bf16[256,256]{1,0:T(8,128)(2,1)} %wq_ref.3) | copy-start | bytes 393220
  115.4 25.5 %copy-start.9 = (bf16[256,256]{1,0:T(8,128)(2,1)S(1)}, bf16[256,256]{1,0:T(8,128)(2,1)}, u32[]{:S(2)}) copy-start(bf16[256,256]{1,0:T(8,128)(2,1)} %wk_ref.3) | copy-start | bytes 393220
  115.4 25.5 %copy-start.10 = (bf16[256,256]{1,0:T(8,128)(2,1)S(1)}, bf16[256,256]{1,0:T(8,128)(2,1)}, u32[]{:S(2)}) copy-start(bf16[256,256]{1,0:T(8,128)(2,1)} %wv_ref.3) | copy-start | bytes 393220
  115.4 25.5 %copy-start.11 = (bf16[256,256]{1,0:T(8,128)(2,1)S(1)}, bf16[256,256]{1,0:T(8,128)(2,1)}, u32[]{:S(2)}) copy-start(bf16[256,256]{1,0:T(8,128)(2,1)} %wg_ref.3) | copy-start | bytes 393220
  140.9 23.0 %copy-start.1 = (bf16[256,1024]{1,0:T(8,128)(2,1)S(1)}, bf16[256,1024]{1,0:T(8,128)(2,1)}, u32[]{:S(2)}) copy-start(bf16[256,1024]{1,0:T(8,128)(2,1)} %ww_ref.1) | copy-start | bytes 1572868
  141.0 23.0 %copy-start.2 = (bf16[1024,256]{1,0:T(8,128)(2,1)S(1)}, bf16[1024,256]{1,0:T(8,128)(2,1)}, u32[]{:S(2)}) copy-start(bf16[1024,256]{1,0:T(8,128)(2,1)} %wn_ref.1) | copy-start | bytes 1572868
  141.0 23.0 %copy-start.12 = (bf16[256,256]{1,0:T(8,128)(2,1)S(1)}, bf16[256,256]{1,0:T(8,128)(2,1)}, u32[]{:S(2)}) copy-start(bf16[256,256]{1,0:T(8,128)(2,1)} %wf_ref.3) | copy-start | bytes 393220
